TPU v7x, 32 devices: a whole 2x2x4 slice. The times are simulated.
32 devices in a mesh: dp: 4 (over x, core), row: 4 (over z), col: 2 (over y).
Axes of the slice: x: 2, y: 2, z: 4, core: 2. Of those that a mesh axis runs over, the one named last changes fastest.
Arguments:
- tokens: bfloat16 [32768, 1024], P(('dp', 'col'), 'row'), may hold values from -7.6 to 7.6
- segments: int32 [32768], P(('dp', 'row')), may hold values from 0 to 17, as said below
- w_query: bfloat16 [1024, 1024], P('row', 'col'), may hold values from -0.1875 to 0.1875
- b_query: bfloat16 [1024], P('col'), may hold values from -3 to 3
- w_key: bfloat16 [1024, 1024], P('row', 'col'), may hold values from -0.1875 to 0.1875
- w_value: bfloat16 [1024, 1024], P('row', 'col'), may hold values from -0.1875 to 0.1875
- b_value: bfloat16 [1024], P('col'), may hold values from -3 to 3
- w_out: bfloat16 [1024, 1024], P('col', 'row'), may hold values from -1 to 1
- b_out: bfloat16 [1024], P('row'), may hold values from -2 to 2
- norm1_gain: bfloat16 [1024], P('row'), may hold values from 0.099609375 to 1.8984375
- norm1_shift: bfloat16 [1024], P('row'), may hold values from -2 to 2
- w_up: bfloat16 [1024, 4096], P('row', 'col'), may hold values from -0.1875 to 0.1875
- b_up: bfloat16 [4096], P('col'), may hold values from -2 to 2
- w_down: bfloat16 [4096, 1024], P('col', 'row'), may hold values from -0.09375 to 0.09375
- b_down: bfloat16 [1024], P('row'), may hold values from -2 to 2
- norm2_gain: bfloat16 [1024], P('row'), may hold values from 0.099609375 to 1.8984375
- norm2_shift: bfloat16 [1024], P('row'), may hold values from -2 to 2
- cotangent: bfloat16 [32768, 1024], P(('dp', 'col'), 'row'), may hold values from -6 to 6
Outputs:
- output: bfloat16 [32768, 1024], P(('dp', 'col'), 'row')
- tokens_grad: bfloat16 [32768, 1024], P(('dp', 'col'), 'row')
- w_query_grad: float32 [1024, 1024], P('row', 'col')
- b_query_grad: float32 [1024], P('col')
- w_key_grad: float32 [1024, 1024], P('row', 'col')
- w_value_grad: float32 [1024, 1024], P('row', 'col')
- b_value_grad: float32 [1024], P('col')
- w_out_grad: float32 [1024, 1024], P('col', 'row')
- b_out_grad: float32 [1024], P('row')
- norm1_gain_grad: float32 [1024], P('row')
- norm1_shift_grad: float32 [1024], P('row')
- w_up_grad: float32 [1024, 4096], P('row', 'col')
- b_up_grad: float32 [4096], P('col')
- w_down_grad: float32 [4096, 1024], P('col', 'row')
- b_down_grad: float32 [1024], P('row')
- norm2_gain_grad: float32 [1024], P('row')
- norm2_shift_grad: float32 [1024], P('row')
Inputs may be any that keep to these rules, and one draw needn't show every extreme that they name: `segments`: each sequence of 1024 tokens holds documents numbered 1, 2, 3 in order, each of 60 to 800 tokens, then padding numbered 0; the last token of every sequence is padding; some sequence holds (1024 - 1) // 60 documents.
All inputs are finite; a program needn't handle non-finite values.
Results may differ from a plain program's by a relative error of at most 0.015.
The roundings to bfloat16 on the way count: a program that leaves them out, or rounds other values in their place, can miss the bound.
Values may be sent and summed in bfloat16 or wider, within the bound.
A program may use at most 320 MiB of HBM per device.

v0:
```python
import jax
import jax.numpy as jnp
from jax import lax
from jax.sharding import PartitionSpec as P

D = 1024
HD = 64
SEQ = 1024


NORM_EPS = 1e-05


def tokens_cols(source):
    return lax.all_gather(source, "col", axis=0, tiled=True)


def tokens_rows(source):
    return lax.all_gather(source, "row", axis=0, tiled=True)


def product(row_piece, weight, flipped):
    if flipped:
        return lax.dot_general(
            row_piece, weight, (((1,), (1,)), ((), ())), preferred_element_type=jnp.float32
        )
    return jnp.dot(row_piece, weight, preferred_element_type=jnp.float32)


def outer_sum(left, right):
    return lax.dot_general(
        left, right, (((0,), (0,)), ((), ())), preferred_element_type=jnp.float32
    )


def settle_rows(gathered, weight, flipped, own_rows):

    def product_term(first_row, row_count):
        return product(gathered, weight, flipped)

    return lax.psum_scatter(
        product_term(jnp.int32(0), own_rows * lax.axis_size("row")),
        "row",
        scatter_dimension=0,
        tiled=True,
    )


def settle_cols(gathered, weight, flipped, own_rows):

    def product_term(first_row, row_count):
        return product(gathered, weight, flipped)

    return lax.psum_scatter(
        product_term(jnp.int32(0), own_rows * lax.axis_size("col")),
        "col",
        scatter_dimension=0,
        tiled=True,
    )


def row_sums(first_part, second_part):
    return lax.psum((jnp.sum(first_part, axis=1), jnp.sum(second_part, axis=1)), "row")


def norm_forward(residual, norm_gain, norm_shift):
    total_sum, square_sum = row_sums(residual, residual * residual)
    row_mean = (total_sum / D)[:, None]
    variance = (square_sum / D)[:, None] - row_mean * row_mean
    inv_std = lax.rsqrt(variance + NORM_EPS)
    normed = (residual - row_mean) * inv_std
    return (normed * norm_gain + norm_shift, normed, inv_std)


def norm_backward(grad_in, normed, inv_std, norm_gain):
    grad_norm = grad_in * norm_gain
    total_sum, cross_sum = row_sums(grad_norm, grad_norm * normed)
    grad_resid = inv_std * (grad_norm - total_sum[:, None] / D - normed * cross_sum[:, None] / D)
    return (grad_resid, jnp.sum(grad_in * normed, axis=0), jnp.sum(grad_in, axis=0))


def gelu_exact(pre_value):
    return jax.nn.gelu(pre_value, approximate=False)


def split_heads(array, seq_count):
    return array.reshape(seq_count, SEQ, array.shape[1] // HD, HD)


def pair_scores(queries, key_heads, segment_ids):
    position = jnp.arange(SEQ)
    same_doc = (segment_ids[:, None] == segment_ids[None, :]) & (segment_ids[None, :] != 0)
    allowed = same_doc | (position[:, None] == position[None, :])
    raw_scores = jnp.einsum(
        "qhd,khd->hqk", queries, key_heads, preferred_element_type=jnp.float32
    ) * HD ** (-0.5)
    return jnp.where(allowed[None], raw_scores, -1000000000.0)


def attend_forward(source):
    queries, key_heads, values, segment_ids = source
    scores = pair_scores(queries, key_heads, segment_ids)
    top_score = jnp.max(scores, axis=2, keepdims=True)
    exp_scores = jnp.exp(scores - top_score)
    total_sum = jnp.sum(exp_scores, axis=2, keepdims=True)
    soft_low = (exp_scores / total_sum).astype(jnp.bfloat16)
    attended = jnp.einsum("hqk,khd->qhd", soft_low, values, preferred_element_type=jnp.float32)
    return (attended.astype(jnp.bfloat16), (top_score + jnp.log(total_sum))[:, :, 0])


def attend_backward(source):
    queries, key_heads, values, segment_ids, grad_out, log_total = source
    scores = pair_scores(queries, key_heads, segment_ids)
    soft_weights = jnp.exp(scores - log_total[:, :, None])
    soft_low = soft_weights.astype(jnp.bfloat16)
    grad_values = jnp.einsum("hqk,qhd->khd", soft_low, grad_out, preferred_element_type=jnp.float32)
    grad_soft = jnp.einsum("qhd,khd->hqk", grad_out, values, preferred_element_type=jnp.float32)
    grad_scores = soft_weights * (
        grad_soft - jnp.sum(soft_weights * grad_soft, axis=2, keepdims=True)
    )
    grad_scores = grad_scores.astype(jnp.bfloat16)
    scale_factor = HD ** (-0.5)
    grad_queries = (
        jnp.einsum("hqk,khd->qhd", grad_scores, key_heads, preferred_element_type=jnp.float32)
        * scale_factor
    )
    grad_keys = (
        jnp.einsum("hqk,qhd->khd", grad_scores, queries, preferred_element_type=jnp.float32)
        * scale_factor
    )
    return (
        grad_queries.astype(jnp.bfloat16),
        grad_keys.astype(jnp.bfloat16),
        grad_values.astype(jnp.bfloat16),
    )


def on_device(
    tokens,
    segments,
    w_query,
    b_query,
    w_key,
    w_value,
    b_value,
    w_out,
    b_out,
    norm1_gain,
    norm1_shift,
    w_up,
    b_up,
    w_down,
    b_down,
    norm2_gain,
    norm2_shift,
    cotangent,
):
    rows_b = tokens.shape[0]
    rows_a = segments.shape[0]
    head_cols = w_query.shape[1]
    seq_count = rows_a // SEQ
    segment_seqs = segments.reshape(seq_count, SEQ)
    gathered_x = tokens_cols(tokens)
    stacked = jnp.concatenate([w_query, w_key, w_value], axis=1)
    projected = settle_rows(gathered_x, stacked, False, rows_a)
    queries = (projected[:, :head_cols] + b_query).astype(jnp.bfloat16)
    key_heads = projected[:, head_cols : 2 * head_cols].astype(jnp.bfloat16)
    values = (projected[:, 2 * head_cols :] + b_value).astype(jnp.bfloat16)
    query_seqs = split_heads(queries, seq_count)
    key_seqs = split_heads(key_heads, seq_count)
    value_seqs = split_heads(values, seq_count)
    attended, log_total = lax.map(attend_forward, (query_seqs, key_seqs, value_seqs, segment_seqs))
    attended = attended.reshape(rows_a, head_cols)
    gathered_o = tokens_rows(attended)
    attn_out = settle_cols(gathered_o, w_out, False, rows_b) + b_out
    hidden, normed1, inv_std1 = norm_forward(
        tokens.astype(jnp.float32) + attn_out, norm1_gain, norm1_shift
    )
    hidden_low = hidden.astype(jnp.bfloat16)
    gathered_h = tokens_cols(hidden_low)
    pre_act = settle_rows(gathered_h, w_up, False, rows_a) + b_up
    active = gelu_exact(pre_act).astype(jnp.bfloat16)
    gathered_a = tokens_rows(active)
    fed = settle_cols(gathered_a, w_down, False, rows_b) + b_down
    output, normed2, inv_std2 = norm_forward(hidden + fed, norm2_gain, norm2_shift)
    grad_r2, grad_gain2, grad_shift2 = norm_backward(
        cotangent.astype(jnp.float32), normed2, inv_std2, norm2_gain
    )
    grad_fed = grad_r2.astype(jnp.bfloat16)
    gathered_f = tokens_cols(grad_fed)
    grad_w_down = outer_sum(gathered_a, gathered_f)
    grad_active = settle_rows(gathered_f, w_down, True, rows_a)
    unused_out, slope_pull = jax.vjp(gelu_exact, pre_act)
    grad_pre = slope_pull(grad_active)[0].astype(jnp.bfloat16)
    gathered_p = tokens_rows(grad_pre)
    grad_w_up = outer_sum(gathered_h, gathered_p)
    grad_from_ff = settle_cols(gathered_p, w_up, True, rows_b)
    bias_up_part = jnp.sum(grad_pre.astype(jnp.float32), axis=0)
    bias_down_part = jnp.sum(grad_fed.astype(jnp.float32), axis=0)
    grad_r1, grad_gain1, grad_shift1 = norm_backward(
        grad_from_ff + grad_r2, normed1, inv_std1, norm1_gain
    )
    grad_attn = grad_r1.astype(jnp.bfloat16)
    gathered_d = tokens_cols(grad_attn)
    grad_w_out = outer_sum(gathered_o, gathered_d)
    grad_attended = settle_rows(gathered_d, w_out, True, rows_a).astype(jnp.bfloat16)
    grad_q, grad_k, grad_v = lax.map(
        attend_backward,
        (
            query_seqs,
            key_seqs,
            value_seqs,
            segment_seqs,
            split_heads(grad_attended, seq_count),
            log_total,
        ),
    )
    grad_q = grad_q.reshape(rows_a, head_cols)
    grad_k = grad_k.reshape(rows_a, head_cols)
    grad_v = grad_v.reshape(rows_a, head_cols)
    grad_proj = jnp.concatenate([grad_q, grad_k, grad_v], axis=1)
    gathered_g = tokens_rows(grad_proj)
    grad_stacked = outer_sum(gathered_x, gathered_g)
    tokens_grad = settle_cols(gathered_g, stacked, True, rows_b) + grad_r1
    bias_q, bias_v, bias_up = lax.psum(
        (
            jnp.sum(grad_q.astype(jnp.float32), axis=0),
            jnp.sum(grad_v.astype(jnp.float32), axis=0),
            bias_up_part,
        ),
        ("dp", "row"),
    )
    bias_out, bias_down, gain_one, shift_one, gain_two, shift_two = lax.psum(
        (
            jnp.sum(grad_attn.astype(jnp.float32), axis=0),
            bias_down_part,
            grad_gain1,
            grad_shift1,
            grad_gain2,
            grad_shift2,
        ),
        ("dp", "col"),
    )
    sum_stacked, sum_out, sum_up, sum_down = (
        lax.psum(grad_stacked.astype(jnp.bfloat16), "dp").astype(jnp.float32),
        lax.psum(grad_w_out.astype(jnp.bfloat16), "dp").astype(jnp.float32),
        lax.psum(grad_w_up.astype(jnp.bfloat16), "dp").astype(jnp.float32),
        lax.psum(grad_w_down.astype(jnp.bfloat16), "dp").astype(jnp.float32),
    )
    return (
        output.astype(jnp.bfloat16),
        tokens_grad.astype(jnp.bfloat16),
        sum_stacked[:, :head_cols],
        bias_q,
        sum_stacked[:, head_cols : 2 * head_cols],
        sum_stacked[:, 2 * head_cols :],
        bias_v,
        sum_out,
        bias_out,
        gain_one,
        shift_one,
        sum_up,
        bias_up,
        sum_down,
        bias_down,
        gain_two,
        shift_two,
    )


def solution(mesh):
    placed = (
        P(("dp", "col"), "row"),
        P(("dp", "row")),
        P("row", "col"),
        P("col"),
        P("row", "col"),
        P("row", "col"),
        P("col"),
        P("col", "row"),
        P("row"),
        P("row"),
        P("row"),
        P("row", "col"),
        P("col"),
        P("col", "row"),
        P("row"),
        P("row"),
        P("row"),
        P(("dp", "col"), "row"),
    )
    return jax.shard_map(
        on_device,
        mesh=mesh,
        in_specs=placed,
        out_specs=(
            P(("dp", "col"), "row"),
            P(("dp", "col"), "row"),
            P("row", "col"),
            P("col"),
            P("row", "col"),
            P("row", "col"),
            P("col"),
            P("col", "row"),
            P("row"),
            P("row"),
            P("row"),
            P("row", "col"),
            P("col"),
            P("col", "row"),
            P("row"),
            P("row"),
            P("row"),
        ),
        check_vma=False,
    )
```

profile of v0, /device:TPU:0, one launch (start us, length us, event | category | flops | bytes accessed | tf_op | source)
XLA Modules:
  0.0 6401.9 jit_solution(5729957298146968956)
XLA Ops:
  10.9 58.2 all-gather.9.cloned.1.call-done
  69.1 20.3 convolution_bitcast_fusion
  90.1 820.1 %reduce-scatter.13.cloned.1.call-done = f32[2048,1536]{0,1:T(8,128)} async-done(((f32[8192,1536]{0,1:T(8,128)}), f32[2048,1536]{0,1:T(8,128)}) %reduce-scatter.13.cloned.1.call-update) | async-done | bytes 12582928 | tf_op jit(solution)/shard_map/reduce_scatter | solution.py:41
  941.9 92.5 %while.26 = (s32[]{:T(128)}, bf16[2,1024,8,64]{1,3,2,0:T(8,128)(2,1)}, f32[2,8,1024]{2,1,0:T(8,128)S(1)}, bf16[2,1024,8,64]{1,3,2,0:T(8,128)(2,1)}, s32[2,1024]{...) while((s32[]{:T(128)}, ...), condition=%wide.region_4.5_spmd, body=%wide.region_1.4_spmd.sunk | while | flops 2252858368 | bytes 117719176 | solution.py:172
  1040.9 151.8 %all-gather.11.cloned.1.call-done = bf16[8192,512]{0,1:T(8,128)(2,1)} async-done(((bf16[2048,512]{0,1:T(8,128)(2,1)}), bf16[8192,512]{0,1:T(8,128)(2,1)}) %all-gather.11.cloned.1.call-update) | async-done | bytes 8388624 | tf_op jit(solution)/shard_map/all_gather | solution.py:19
  1202.4 96.9 %reduce-scatter.15.cloned.1.call-done = f32[4096,256]{1,0:T(8,128)} async-done(((f32[8192,256]{1,0:T(8,128)}), f32[4096,256]{1,0:T(8,128)}) %reduce-scatter.15.cloned.1.call-update) | async-done | bytes 4194320 | tf_op jit(solution)/shard_map/reduce_scatter | solution.py:54
  1304.1 19.0 all-reduce.7
  1327.1 54.1 all-gather.13.cloned.1.call-done
  1381.2 25.4 fusion.85
  1407.3 1094.1 %reduce-scatter.25.cloned.1.call-done = f32[2048,2048]{1,0:T(8,128)} async-done(((f32[8192,2048]{1,0:T(8,128)}), f32[2048,2048]{1,0:T(8,128)}) %reduce-scatter.25.cloned.1.call-update) | async-done | bytes 16777232
  2501.4 39.7 multiply_convert_fusion.3
  2541.2 563.0 %all-gather.15.cloned.1.call-done = bf16[8192,2048]{1,0:T(8,128)(2,1)} async-done(((bf16[2048,2048]{1,0:T(8,128)(2,1)}), bf16[8192,2048]{1,0:T(8,128)(2,1)}) %all-gather.15.cloned.1.call-update) | async-done | bytes 33554448 | tf_op jit(solution)/shard_map/all_gather | solution.py:19
  3122.0 97.0 %reduce-scatter.17.cloned.1.call-done = f32[4096,256]{1,0:T(8,128)} async-done(((f32[8192,256]{1,0:T(8,128)}), f32[4096,256]{1,0:T(8,128)}) %reduce-scatter.17.cloned.1.call-update) | async-done | bytes 4194320 | tf_op jit(solution)/shard_map/reduce_scatter | solution.py:54
  3224.9 19.0 all-reduce.6
  3271.5 55.4 all-gather.17.cloned.1.call-done
  3326.9 25.6 fusion.87
  3352.6 1094.7 %reduce-scatter.27.cloned.1.call-done = f32[2048,2048]{1,0:T(8,128)} async-done(((f32[8192,2048]{1,0:T(8,128)}), f32[2048,2048]{1,0:T(8,128)}) %reduce-scatter.27.cloned.1.call-update) | async-done | bytes 16777232
  4447.3 21.9 convert_reduce_fusion
  4469.3 563.0 %all-gather.19.cloned.1.call-done = bf16[8192,2048]{1,0:T(8,128)(2,1)} async-done(((bf16[2048,2048]{1,0:T(8,128)(2,1)}), bf16[8192,2048]{1,0:T(8,128)(2,1)}) %all-gather.19.cloned.1.call-update) | async-done | bytes 33554448 | tf_op jit(solution)/shard_map/all_gather | solution.py:19
  5050.1 97.0 %reduce-scatter.19.cloned.1.call-done = f32[4096,256]{1,0:T(8,128)} async-done(((f32[8192,256]{1,0:T(8,128)}), f32[4096,256]{1,0:T(8,128)}) %reduce-scatter.19.cloned.1.call-update) | async-done | bytes 4194320 | tf_op jit(solution)/shard_map/reduce_scatter | solution.py:54
  5156.2 19.0 all-reduce.4
  5184.8 54.1 all-gather.21.cloned.1.call-done
  5249.2 280.4 %reduce-scatter.21.cloned.1.call-done = f32[2048,512]{1,0:T(8,128)} async-done(((f32[8192,512]{1,0:T(8,128)}), f32[2048,512]{1,0:T(8,128)}) %reduce-scatter.21.cloned.1.call-update) | async-done | bytes 4194320 | tf_op jit(solution)/shard_map/reduce_scatter | solution.py:41
  5546.0 212.8 %while.27 = (s32[]{:T(128)}, bf16[2,1024,8,64]{1,3,2,0:T(8,128)(2,1)}, bf16[2,1024,8,64]{1,3,2,0:T(8,128)(2,1)}, bf16[2,1024,8,64]{1,3,2,0:T(8,128)(2,1)}, bf16[...) while((s32[]{:T(128)}, ...), condition=%wide.region_29.30_spmd, body=%wide.region_27.29_spmd.sunk | while | flops 5501346816 | bytes 266587280 | solution.py:207
  5578.4 23.7 multiply_reduce_fusion.7
  5602.1 28.5 multiply_convert_fusion.5
  5684.5 23.7 multiply_reduce_fusion.7
  5708.3 28.5 multiply_convert_fusion.5
  5780.6 21.2 convolution_convert_fusion
  5826.4 380.2 %all-gather.23.cloned.1.call-done = bf16[8192,1536]{0,1:T(8,128)(2,1)} async-done(((bf16[2048,1536]{0,1:T(8,128)(2,1)}), bf16[8192,1536]{0,1:T(8,128)(2,1)}) %all-gather.23.cloned.1.call-update) | async-done | bytes 25165840 | tf_op jit(solution)/shard_map/all_gather | solution.py:19
  6254.1 58.7 all-reduce.2
  6323.2 66.5 %reduce-scatter.23.cloned.1.call-done = f32[4096,256]{1,0:T(8,128)} async-done(((f32[8192,256]{1,0:T(8,128)}), f32[4096,256]{1,0:T(8,128)}) %reduce-scatter.23.cloned.1.call-update) | async-done | bytes 4194320 | tf_op jit(solution)/shard_map/reduce_scatter | solution.py:54
  (209 shorter events, 485.6 us)
Async XLA Ops:
  7.2 3097.0 %copy-start = (bf16[2048,256]{1,0:T(8,128)(2,1)S(1)}, bf16[2048,256]{1,0:T(8,128)(2,1)}, u32[]{:S(2)}) copy-start(bf16[2048,256]{1,0:T(8,128)(2,1)} %param.35) | copy-start | bytes 3145732
  7.2 61.9 all-gather.9.cloned.1.call-start
  7.9 902.3 %reduce-scatter.13.cloned.1.call-start = ((), (), s32[]{:S(2)}) async-start(), calls=%async_computation.9 | async-start | bytes 62914560 | tf_op jit(solution)/shard_map/reduce_scatter | solution.py:41
  10.9 78.5 %copy-start.10 = (bf16[256,1536]{1,0:T(8,128)(2,1)}, bf16[256,1536]{1,0:T(8,128)(2,1)S(1)}, u32[]{:S(2)}) copy-start(bf16[256,1536]{1,0:T(8,128)(2,1)S(1)} %constant_dynamic-update-slice_fusion) | copy-start | bytes 2359300
  89.4 1103.3 %all-gather.11.cloned.1.call-start = ((), (), s32[]{:S(2)}) async-start(), calls=%async_computation.10 | async-start | bytes 10485760 | tf_op jit(solution)/shard_map/all_gather | solution.py:19
  958.3 14.4 copy-start.4
  1004.4 14.4 copy-start.4
  1034.4 6.4 copy-start.2
  1038.9 153.8 %copy-start.15 = (bf16[512,256]{1,0:T(8,128)(2,1)S(1)}, bf16[512,256]{1,0:T(8,128)(2,1)}, u32[]{:S(2)}) copy-start(bf16[512,256]{1,0:T(8,128)(2,1)} %param.29) | copy-start | bytes 786436
  1040.9 258.5 %reduce-scatter.15.cloned.1.call-start = ((), (), s32[]{:S(2)}) async-start(), calls=%async_computation.11 | async-start | bytes 12582912 | tf_op jit(solution)/shard_map/reduce_scatter | solution.py:54
  1201.7 97.6 %copy-start.9 = (bf16[4096,256]{1,0:T(8,128)(2,1)S(1)}, bf16[4096,256]{1,0:T(8,128)(2,1)}, u32[]{:S(2)}) copy-start(bf16[4096,256]{1,0:T(8,128)(2,1)} %param.22) | copy-start | bytes 6291460
  1201.8 179.5 %all-gather.13.cloned.1.call-start = ((), (), s32[]{:S(2)}) async-start(), calls=%async_computation.12 | async-start | bytes 6291456 | tf_op jit(solution)/shard_map/all_gather | solution.py:15
  1323.1 58.1 copy-start.12
  1327.0 1174.4 %reduce-scatter.25.cloned.1.call-start = ((), (), s32[]{:S(2)}) async-start(), calls=%async_computation.22 | async-start | bytes 83886080
  1406.6 1697.6 %all-gather.15.cloned.1.call-start = ((), (), s32[]{:S(2)}) async-start(), calls=%async_computation.13 | async-start | bytes 41943040 | tf_op jit(solution)/shard_map/all_gather | solution.py:19
  2541.2 677.8 %reduce-scatter.17.cloned.1.call-start = ((), (), s32[]{:S(2)}) async-start(), calls=%async_computation.14 | async-start | bytes 12582912 | tf_op jit(solution)/shard_map/reduce_scatter | solution.py:54
  3121.3 205.6 %all-gather.17.cloned.1.call-start = ((), (), s32[]{:S(2)}) async-start(), calls=%async_computation.15 | async-start | bytes 6291456 | tf_op jit(solution)/shard_map/all_gather | solution.py:15
  3122.0 121.9 %copy-start.6 = (bf16[4096,256]{1,0:T(8,128)(2,1)S(1)}, bf16[4096,256]{1,0:T(8,128)(2,1)}, u32[]{:S(2)}) copy-start(bf16[4096,256]{1,0:T(8,128)(2,1)} %param.39) | copy-start | bytes 6291460
  3271.5 1175.9 %reduce-scatter.27.cloned.1.call-start = ((), (), s32[]{:S(2)}) async-start(), calls=%async_computation.23 | async-start | bytes 83886080
  3352.5 1679.8 %all-gather.19.cloned.1.call-start = ((), (), s32[]{:S(2)}) async-start(), calls=%async_computation.16 | async-start | bytes 41943040 | tf_op jit(solution)/shard_map/all_gather | solution.py:19
  4469.3 563.1 %copy-start.13 = (bf16[256,2048]{1,0:T(8,128)(2,1)S(1)}, bf16[256,2048]{1,0:T(8,128)(2,1)}, u32[]{:S(2)}) copy-start(bf16[256,2048]{1,0:T(8,128)(2,1)} %param.33) | copy-start | bytes 3145732
  4469.3 677.8 %reduce-scatter.19.cloned.1.call-start = ((), (), s32[]{:S(2)}) async-start(), calls=%async_computation.17 | async-start | bytes 12582912 | tf_op jit(solution)/shard_map/reduce_scatter | solution.py:54
  5049.5 189.4 %all-gather.21.cloned.1.call-start = ((), (), s32[]{:S(2)}) async-start(), calls=%async_computation.18 | async-start | bytes 6291456 | tf_op jit(solution)/shard_map/all_gather | solution.py:15
  5175.2 63.7 copy-start.16
  5184.7 344.9 %reduce-scatter.21.cloned.1.call-start = ((), (), s32[]{:S(2)}) async-start(), calls=%async_computation.19 | async-start | bytes 20971520 | tf_op jit(solution)/shard_map/reduce_scatter | solution.py:41
  5249.2 957.4 %all-gather.23.cloned.1.call-start = ((), (), s32[]{:S(2)}) async-start(), calls=%async_computation.20 | async-start | bytes 31457280 | tf_op jit(solution)/shard_map/all_gather | solution.py:19
  5780.5 532.3 %all-reduce.11.cloned.1.call-start = ((), (), s32[]{:S(2)}) async-start(), calls=%async_computation.24 | async-start | bytes 6291456 | tf_op jit(solution)/shard_map/psum | solution.py:245
  5780.6 21.2 copy-start.5
  5826.4 393.8 %copy-start.11 = (bf16[256,1536]{1,0:T(8,128)(2,1)S(1)}, bf16[256,1536]{1,0:T(8,128)(2,1)}, u32[]{:S(2)}) copy-start(bf16[256,1536]{1,0:T(8,128)(2,1)} %copy-done.10) | copy-start | bytes 2359300
  6220.2 169.6 %reduce-scatter.23.cloned.1.call-start = ((), (), s32[]{:S(2)}) async-start(), calls=%async_computation.21 | async-start | bytes 12582912 | tf_op jit(solution)/shard_map/reduce_scatter | solution.py:54
  6235.1 19.0 copy-start.21
  6314.7 7.1 copy-start.14
  (24 other events, 39.3 us)
Sparse Core Ops, SparseCore 0:
  9.6 59.4 all-gather.8
  89.5 820.6 reduce-scatter.12
  1041.0 151.6 all-gather.10
  1201.9 97.4 reduce-scatter.14
  1327.2 54.0 all-gather.12
  1406.8 1094.6 reduce-scatter.24
  2541.3 562.8 all-gather.14
  3121.4 97.4 reduce-scatter.16
  3271.6 55.3 all-gather.16
  3352.7 1094.6 reduce-scatter.26
  4469.4 562.8 all-gather.18
  5049.6 97.4 reduce-scatter.18
  5184.8 54.0 all-gather.20
  5249.3 280.2 reduce-scatter.20
  5780.7 425.8 all-gather.22
  6220.3 67.8 all-reduce.10
  6290.5 99.2 reduce-scatter.22
where the time goes:
time: 6410 us; the launch traced here: 6400 us
  waiting for transfers between devices  5530 us (86%)
  matrix products  411 us (6%)
  other arithmetic  231 us (4%)
  blocking collectives  147 us (2%)
  local copies, waits for them, and re-layouts  67.8 us (1%)
    unnamed x19, waiting for transfers between devices  2190 us
    all_gather x4, waiting for transfers between devices, tokens_rows(): return lax.all_gather(source, 'row', axis=0, tiled=True)  1660 us
    reduce_scatter x2, waiting for transfers between devices, settle_rows(): lax.psum_scatter(product_term(jnp.int32(0), own_rows * lax.axis_size('row...  1100 us
    reduce_scatter x4, waiting for transfers between devices, settle_cols(): lax.psum_scatter(product_term(jnp.int32(0), own_rows * lax.axis_size('col...  357 us
    all_gather x4, waiting for transfers between devices, tokens_cols(): return lax.all_gather(source, 'col', axis=0, tiled=True)  222 us
  transfers between devices with their start and end apart: 17, of which 16 were waited for; matrix products, arithmetic and copies ran while one was open for 1% of the time, Pallas kernels for 0%

commit v1 on v0

--- a/solution.py
+++ b/solution.py
@@ -1,14 +1,372 @@
+import math
+
 import jax
 import jax.numpy as jnp
 from jax import lax
+from jax.experimental import pallas as pl
+from jax.experimental.pallas import tpu as pltpu
 from jax.sharding import PartitionSpec as P
 
-D = 1024
 HD = 64
 SEQ = 1024
-
-
+WIDTH = 1024
+TOKENS = 32768
 NORM_EPS = 1e-05
+BF = jnp.bfloat16
+F32 = jnp.float32
+NEG = -1e30
+QB = 256
+
+
+def mm(a, b):
+    return jnp.dot(a, b, preferred_element_type=F32)
+
+
+def mm_t(a, b):
+    return lax.dot_general(a, b, (((1,), (1,)), ((), ())), preferred_element_type=F32)
+
+
+def tmm(a, b):
+    return lax.dot_general(a, b, (((0,), (0,)), ((), ())), preferred_element_type=F32)
+
+
+def gelu_exact(v):
+    return jax.nn.gelu(v, approximate=False)
+
+
+def attend_fwd_kernel(qkv_ref, seg_col_ref, seg_row_ref, o_ref, p_ref, linv_ref):
+    lane = lax.broadcasted_iota(jnp.int32, (QB, 128), 1)
+    seg_row = seg_row_ref[...]
+    k = qkv_ref[:, 128:256]
+    v = qkv_ref[:, 256:384]
+    scale = HD ** (-0.5) * math.log2(math.e)
+    for i in range(SEQ // QB):
+        rows = slice(i * QB, (i + 1) * QB)
+        q = qkv_ref[rows, 0:128]
+        seg_col = seg_col_ref[rows, :]
+        outs = []
+        for h in range(2):
+            mine = (lane < HD) if h == 0 else (lane >= HD)
+            qm = jnp.where(mine, q, jnp.zeros_like(q))
+            s = mm_t(qm, k)
+            s = jnp.where(seg_col == seg_row, s * scale, NEG)
+            top = jnp.max(s, axis=1, keepdims=True)
+            p = jnp.exp2(s - top)
+            total = jnp.sum(p, axis=1, keepdims=True)
+            pb = p.astype(BF)
+            p_ref[h, rows, :] = pb
+            inv = 1.0 / total
+            outs.append((mm(pb, v) * inv, jnp.broadcast_to(inv, (QB, 128))))
+        o_ref[rows, :] = jnp.where(lane < HD, outs[0][0], outs[1][0]).astype(BF)
+        linv_ref[rows, :] = jnp.where(lane < HD, outs[0][1], outs[1][1])
+
+
+def attend_bwd_kernel(qkv_ref, do_ref, o_ref, linv_ref, p_ref, g_ref, ds_ref):
+    lane = lax.broadcasted_iota(jnp.int32, (SEQ, 128), 1)
+    q = qkv_ref[:, 0:128]
+    k = qkv_ref[:, 128:256]
+    v = qkv_ref[:, 256:384]
+    scale = HD ** (-0.5)
+    do = do_ref[...].astype(F32) * linv_ref[...]
+    prod = do * o_ref[...].astype(F32)
+    dob = do.astype(BF)
+    qt = jnp.transpose(q.astype(F32)).astype(BF)
+    dot_ = jnp.transpose(do).astype(BF)
+    dq = []
+    dkt = []
+    dvt = []
+    for h in range(2):
+        mine = (lane < HD) if h == 0 else (lane >= HD)
+        delta = jnp.sum(jnp.where(mine, prod, 0.0), axis=1, keepdims=True)
+        dom = jnp.where(mine, dob, jnp.zeros_like(dob))
+        for i in range(SEQ // QB):
+            rows = slice(i * QB, (i + 1) * QB)
+            dp = mm_t(dom[rows], v)
+            ds = p_ref[h, rows, :].astype(F32) * (dp - delta[rows])
+            ds_ref[h, rows, :] = ds.astype(BF)
+        feats = slice(h * HD, (h + 1) * HD)
+        dq.append(mm(ds_ref[h], k))
+        dkt.append(mm(qt[feats], ds_ref[h]))
+        dvt.append(mm(dot_[feats], p_ref[h]))
+    g_ref[:, 0:128] = (jnp.where(lane < HD, dq[0], dq[1]) * scale).astype(BF)
+    g_ref[:, 128:256] = (jnp.transpose(jnp.concatenate(dkt, 0)) * scale).astype(BF)
+    g_ref[:, 256:384] = jnp.transpose(jnp.concatenate(dvt, 0)).astype(BF)
+
+
+VMEM_LIMIT = 48 * 1024 * 1024
+
+
+def attend_fwd(qkv, seg_col, seg_row):
+    slots = qkv.shape[1] // 384
+    return pl.pallas_call(
+        attend_fwd_kernel,
+        grid=(slots,),
+        in_specs=[
+            pl.BlockSpec((SEQ, 384), lambda j: (0, j)),
+            pl.BlockSpec((SEQ, 1), lambda j: (0, 0)),
+            pl.BlockSpec((1, SEQ), lambda j: (0, 0)),
+        ],
+        out_specs=[
+            pl.BlockSpec((SEQ, 128), lambda j: (0, j)),
+            pl.BlockSpec((2, SEQ, SEQ), lambda j: (j, 0, 0)),
+            pl.BlockSpec((SEQ, 128), lambda j: (0, j)),
+        ],
+        out_shape=[
+            jax.ShapeDtypeStruct((SEQ, slots * 128), BF),
+            jax.ShapeDtypeStruct((slots * 2, SEQ, SEQ), BF),
+            jax.ShapeDtypeStruct((SEQ, slots * 128), F32),
+        ],
+        compiler_params=pltpu.CompilerParams(vmem_limit_bytes=VMEM_LIMIT),
+        cost_estimate=pl.CostEstimate(
+            flops=slots * 2 * 4 * SEQ * SEQ * 256,
+            bytes_accessed=slots * 5 * SEQ * SEQ,
+            transcendentals=slots * 2 * SEQ * SEQ,
+        ),
+        name="attend_fwd",
+    )(qkv, seg_col, seg_row)
+
+
+def attend_bwd(qkv, do, o, linv, p):
+    slots = qkv.shape[1] // 384
+    return pl.pallas_call(
+        attend_bwd_kernel,
+        grid=(slots,),
+        in_specs=[
+            pl.BlockSpec((SEQ, 384), lambda j: (0, j)),
+            pl.BlockSpec((SEQ, 128), lambda j: (0, j)),
+            pl.BlockSpec((SEQ, 128), lambda j: (0, j)),
+            pl.BlockSpec((SEQ, 128), lambda j: (0, j)),
+            pl.BlockSpec((2, SEQ, SEQ), lambda j: (j, 0, 0)),
+        ],
+        out_specs=pl.BlockSpec((SEQ, 384), lambda j: (0, j)),
+        out_shape=jax.ShapeDtypeStruct((SEQ, slots * 384), BF),
+        scratch_shapes=[pltpu.VMEM((2, SEQ, SEQ), BF)],
+        compiler_params=pltpu.CompilerParams(vmem_limit_bytes=VMEM_LIMIT),
+        cost_estimate=pl.CostEstimate(
+            flops=slots * 2 * 8 * SEQ * SEQ * 256,
+            bytes_accessed=slots * 6 * SEQ * SEQ,
+            transcendentals=0,
+        ),
+        name="attend_bwd",
+    )(qkv, do, o, linv, p)
+
+
+class Ring:
+    def __init__(self):
+        self.r = lax.axis_index("row")
+        self.c = lax.axis_index("col")
+        self.d = lax.axis_index("dp")
+        self.rows = lax.axis_size("row")
+
+    def shift(self, v, s):
+        n = self.rows
+        return lax.ppermute(v, "row", [(i, (i + s) % n) for i in range(n)])
+
+    def core(self, v):
+        return lax.ppermute(v, "dp", [(i, i ^ 1) for i in range(4)])
+
+    def x(self, v):
+        return lax.ppermute(v, "dp", [(i, i ^ 2) for i in range(4)])
+
+    def y(self, v):
+        return lax.ppermute(v, "col", [(0, 1), (1, 0)])
+
+    def gather(self, piece, axis):
+        parts = [piece]
+        for _ in range(self.rows - 1):
+            parts.append(self.shift(parts[-1], 1))
+        own = jnp.concatenate(parts, axis)
+        from_x, from_y = self.x(own), self.y(own)
+        half = own.shape[0] // 2
+        diag = jnp.concatenate([self.y(from_x[:half]), self.x(from_y[half:])], 0)
+        first = [own, from_x, from_y, diag]
+        other = [self.core(v) for v in first]
+        return [first[0], other[0], first[1], other[1], first[2], other[2], first[3], other[3]]
+
+    def scatter(self, blocks, cut):
+        kept = [blocks[0], blocks[2], blocks[4], blocks[6]]
+        sent = [blocks[1], blocks[3], blocks[5], blocks[7]]
+        own, to_x, to_y, diag = [
+            (a.astype(F32) + self.core(b).astype(F32)).astype(BF) for a, b in zip(kept, sent)
+        ]
+        half = own.shape[0] // 2
+        via_y = self.y(diag[:half])
+        via_x = self.x(diag[half:])
+        to_x = jnp.concatenate([to_x[:half] + via_y, to_x[half:]], 0)
+        to_y = jnp.concatenate([to_y[:half], to_y[half:] + via_x], 0)
+        total = (own.astype(F32) + self.x(to_x).astype(F32) + self.y(to_y).astype(F32)).astype(BF)
+        parts = cut(total)
+        acc = parts[1]
+        for s in range(1, self.rows):
+            got = self.shift(acc, 1)
+            acc = (parts[(s + 1) % self.rows].astype(F32) + got.astype(F32)).astype(BF)
+        pair = jnp.stack([acc, self.core(acc)])
+        quarters = jnp.concatenate([pair, self.x(pair)], 0)
+        return self.absolute(quarters)
+
+    def absolute(self, quarters):
+        a = jnp.where(self.d % 2 == 1, quarters[jnp.array([1, 0, 3, 2])], quarters)
+        return jnp.where(self.d // 2 == 1, jnp.concatenate([a[2:], a[:2]], 0), a)
+
+
+def layer_norm(residual, gain, shift):
+    mean = jnp.mean(residual, axis=1, keepdims=True)
+    variance = jnp.mean(residual * residual, axis=1, keepdims=True) - mean * mean
+    inv = lax.rsqrt(variance + NORM_EPS)
+    normed = (residual - mean) * inv
+    return normed * gain + shift, normed, inv
+
+
+def layer_norm_back(grad, normed, inv, gain):
+    g = grad * gain
+    mean_g = jnp.mean(g, axis=1, keepdims=True)
+    mean_gn = jnp.mean(g * normed, axis=1, keepdims=True)
+    return inv * (g - mean_g - normed * mean_gn), jnp.sum(grad * normed, axis=0), jnp.sum(grad, axis=0)
+
+
+def quarter(v, d, axis):
+    n = v.shape[axis] // 4
+    return lax.dynamic_slice_in_dim(v, d * n, n, axis)
+
+
+def whole_sequences(
+    tokens, segments, w_query, b_query, w_key, w_value, b_value, w_out, b_out, norm1_gain, norm1_shift,
+    w_up, b_up, w_down, b_down, norm2_gain, norm2_shift, cotangent,
+):
+    ring = Ring()
+    r, c, d = ring.r, ring.c, ring.d
+    R, C = lax.axis_size("row"), lax.axis_size("col")
+    feat = tokens.shape[1]
+
+    def inward(block):
+        parts = []
+        for s in range(R):
+            piece = lax.dynamic_slice_in_dim(block, ((r + s) % R) * SEQ, SEQ, 0)
+            parts.append(piece if s == 0 else ring.shift(piece, s))
+        return jnp.concatenate(parts, 1)
+
+    def outward(rows):
+        whole = jnp.zeros((R * SEQ, feat), rows.dtype)
+        for s in range(R):
+            piece = rows[:, s * feat : (s + 1) * feat]
+            if s:
+                piece = ring.shift(piece, -s)
+            whole = lax.dynamic_update_slice_in_dim(whole, piece, ((r + s) % R) * SEQ, 0)
+        return whole
+
+    pairs = []
+    for row in range(R):
+        for col in range(C):
+            n = col * R + row
+            pairs.append((n, row * C + col))
+    seg = lax.ppermute(segments, ("row", "col"), pairs)
+    seg = lax.dynamic_slice_in_dim(seg, ((c * R + r) % C) * SEQ, SEQ, 0)
+    ids = jnp.where(seg == 0, -1 - jnp.arange(SEQ, dtype=jnp.int32), seg)
+    seg_col, seg_row = ids[:, None], ids[None, :]
+
+    x = inward(tokens)
+    qkv_piece = jnp.concatenate([quarter(w, d, 1) for w in (w_query, w_key, w_value)], 1)
+    w_qkv = jnp.concatenate(ring.gather(qkv_piece, 0), 1)
+    wo = jnp.concatenate(ring.gather(quarter(w_out, d, 0), 1), 0)
+    wu = jnp.concatenate(ring.gather(quarter(w_up, d, 1), 0), 1)
+    wd = jnp.concatenate(ring.gather(quarter(w_down, d, 0), 1), 0)
+    cot = inward(cotangent)
+
+    feat_vec = jnp.stack([b_out, norm1_gain, norm1_shift, b_down, norm2_gain, norm2_shift])
+    feat_all = jnp.concatenate([feat_vec] + [ring.shift(feat_vec, s) for s in range(1, R)], 1).astype(F32)
+    bo, g1, s1, bd, g2, s2 = [feat_all[i] for i in range(6)]
+    hq = b_query.shape[0] // 4
+    unit = b_up.shape[0] // 4
+    slot_vec = jnp.concatenate(
+        [b_query.reshape(4, hq), jnp.zeros((4, hq), BF), b_value.reshape(4, hq), b_up.reshape(4, unit)], 1
+    )
+    slot_vec = ring.absolute(slot_vec)
+    slot_vec = jnp.concatenate([slot_vec, ring.y(slot_vec)], 0).astype(F32)
+    b_qkv = slot_vec[:, : 3 * hq].reshape(-1)
+    bu = slot_vec[:, 3 * hq :].reshape(-1)
+
+    qkv = (mm(x, w_qkv) + b_qkv).astype(BF)
+    att, prob, linv = attend_fwd(qkv, seg_col, seg_row)
+    hidden, normed1, inv1 = layer_norm(x.astype(F32) + mm(att, wo) + bo, g1, s1)
+    hidden_low = hidden.astype(BF)
+    pre = mm(hidden_low, wu) + bu
+    act = gelu_exact(pre).astype(BF)
+    fed = mm(act, wd) + bd
+    output, normed2, inv2 = layer_norm(hidden + fed, g2, s2)
+    out_block = outward(output.astype(BF))
+
+    grad_r2, d_g2, d_s2 = layer_norm_back(cot.astype(F32), normed2, inv2, g2)
+    grad_fed = grad_r2.astype(BF)
+    dwd = tmm(act, grad_fed).astype(BF)
+    grad_act = mm_t(grad_fed, wd)
+    _, slope = jax.vjp(gelu_exact, pre)
+    grad_pre = slope(grad_act)[0].astype(BF)
+    dwu = tmm(hidden_low, grad_pre).astype(BF)
+    grad_hidden = mm_t(grad_pre, wu) + grad_r2
+    grad_r1, d_g1, d_s1 = layer_norm_back(grad_hidden, normed1, inv1, g1)
+    grad_attn = grad_r1.astype(BF)
+    dwo = tmm(att, grad_attn).astype(BF)
+    grad_att = mm_t(grad_attn, wo).astype(BF)
+    g_qkv = attend_bwd(qkv, grad_att, att, linv, prob)
+    dwqkv = tmm(x, g_qkv).astype(BF)
+    x_grad = (mm_t(g_qkv, w_qkv) + grad_r1).astype(BF)
+    x_grad_block = outward(x_grad)
+
+    def rows_of(v, n=8):
+        k = v.shape[0] // n
+        return [v[i * k : (i + 1) * k] for i in range(n)]
+
+    def cols_of(v, n=8):
+        k = v.shape[1] // n
+        return [v[:, i * k : (i + 1) * k] for i in range(n)]
+
+    def cut_rows(v):
+        return rows_of(v, R)
+
+    def cut_cols(v):
+        return cols_of(v, R)
+
+    sum_down = ring.scatter(rows_of(dwd), cut_cols)
+    sum_up = ring.scatter(cols_of(dwu), cut_rows)
+    sum_out = ring.scatter(rows_of(dwo), cut_cols)
+    sum_qkv = ring.scatter(cols_of(dwqkv), cut_rows)
+    w_down_grad = sum_down.astype(F32).reshape(w_down.shape)
+    w_out_grad = sum_out.astype(F32).reshape(w_out.shape)
+    w_up_grad = sum_up.astype(F32).transpose(1, 0, 2).reshape(w_up.shape)
+    sum_qkv = sum_qkv.astype(F32).transpose(1, 0, 2)
+    wq_grad, wk_grad, wv_grad = [sum_qkv[:, :, i * hq : (i + 1) * hq].reshape(w_query.shape) for i in range(3)]
+
+    g32 = g_qkv.astype(F32)
+    slot_grad = jnp.concatenate(
+        [
+            jnp.sum(g32, axis=0).reshape(8, 3 * hq),
+            jnp.sum(grad_pre.astype(F32), axis=0).reshape(8, unit),
+        ],
+        1,
+    )
+    feat_grad = jnp.stack(
+        [jnp.sum(grad_attn.astype(F32), axis=0), d_g1, d_s1, jnp.sum(grad_fed.astype(F32), axis=0), d_g2, d_s2]
+    )
+    slot_grad = slot_grad[0::2] + ring.core(slot_grad[1::2])
+    slot_grad = slot_grad[0::2] + ring.x(slot_grad[1::2])
+    slot_grad = slot_grad[0] + ring.y(slot_grad[1])
+    for s in (1, 2):
+        slot_grad = slot_grad + lax.ppermute(slot_grad, "row", [(i, i ^ s) for i in range(R)])
+    pair = jnp.stack([slot_grad, ring.core(slot_grad)])
+    slot_grad = ring.absolute(jnp.concatenate([pair, ring.x(pair)], 0))
+    bq_grad = slot_grad[:, :hq].reshape(-1)
+    bv_grad = slot_grad[:, 2 * hq : 3 * hq].reshape(-1)
+    bu_grad = slot_grad[:, 3 * hq :].reshape(-1)
+    feat_grad = feat_grad + ring.core(feat_grad)
+    feat_grad = feat_grad + ring.x(feat_grad)
+    feat_grad = feat_grad + ring.y(feat_grad)
+    own = feat_grad[:, :feat]
+    for s in range(1, R):
+        own = own + ring.shift(feat_grad[:, s * feat : (s + 1) * feat], -s)
+    return (
+        out_block, x_grad_block, wq_grad, bq_grad, wk_grad, wv_grad, bv_grad, w_out_grad, own[0], own[1], own[2],
+        w_up_grad, bu_grad, w_down_grad, own[3], own[4], own[5],
+    )
 
 
 def tokens_cols(source):
@@ -65,8 +423,8 @@
 
 def norm_forward(residual, norm_gain, norm_shift):
     total_sum, square_sum = row_sums(residual, residual * residual)
-    row_mean = (total_sum / D)[:, None]
-    variance = (square_sum / D)[:, None] - row_mean * row_mean
+    row_mean = (total_sum / WIDTH)[:, None]
+    variance = (square_sum / WIDTH)[:, None] - row_mean * row_mean
     inv_std = lax.rsqrt(variance + NORM_EPS)
     normed = (residual - row_mean) * inv_std
     return (normed * norm_gain + norm_shift, normed, inv_std)
@@ -75,12 +433,8 @@
 def norm_backward(grad_in, normed, inv_std, norm_gain):
     grad_norm = grad_in * norm_gain
     total_sum, cross_sum = row_sums(grad_norm, grad_norm * normed)
-    grad_resid = inv_std * (grad_norm - total_sum[:, None] / D - normed * cross_sum[:, None] / D)
+    grad_resid = inv_std * (grad_norm - total_sum[:, None] / WIDTH - normed * cross_sum[:, None] / WIDTH)
     return (grad_resid, jnp.sum(grad_in * normed, axis=0), jnp.sum(grad_in, axis=0))
-
-
-def gelu_exact(pre_value):
-    return jax.nn.gelu(pre_value, approximate=False)
 
 
 def split_heads(array, seq_count):
@@ -135,7 +489,7 @@
     )
 
 
-def on_device(
+def split_heads_plan(
     tokens,
     segments,
     w_query,
@@ -269,6 +623,9 @@
 
 
 def solution(mesh):
+    dp, rows, cols = (mesh.shape[name] for name in ("dp", "row", "col"))
+    whole = TOKENS // SEQ == dp * rows * cols and dp == 4 and cols == 2
+    plan = whole_sequences if whole else split_heads_plan
     placed = (
         P(("dp", "col"), "row"),
         P(("dp", "row")),
@@ -290,7 +647,7 @@
         P(("dp", "col"), "row"),
     )
     return jax.shard_map(
-        on_device,
+        plan,
         mesh=mesh,
         in_specs=placed,
         out_specs=(

time: 6410 us -> 857 us (0.13)
  waiting for transfers between devices: 5530 us -> 271 us
  matrix products: 411 us -> 171 us
  other arithmetic: 231 us -> 72.7 us
  blocking collectives: 147 us -> 0 us
  starting transfers between devices: 0.88 us -> 137 us
  Pallas kernels: 0 us -> 77.6 us
    unnamed x19 -> x0, waiting for transfers between devices: 2190 us -> none
    all_gather x8 -> x0, waiting for transfers between devices: 1880 us -> none  [the longest x4 1660 us: tokens_rows(): return lax.all_gather(source, 'row', axis=0, tiled=True)]
    reduce_scatter x6 -> x0, waiting for transfers between devices: 1460 us -> none  [the longest x2 1100 us: settle_rows(): lax.psum_scatter(product_term(jnp.int32(0), own_rows * lax.axis_size('row...]
    ppermute x0 -> x126, waiting for transfers between devices: none -> 271 us  [the longest x42 127 us: shift(): return lax.ppermute(v, 'row', [(i, (i + s) % n) for i in range(n)])]
    dot_general x26 -> x12, matrix products: 411 us -> 171 us  [the longest x4 78.4 us: mm(): return jnp.dot(a, b, preferred_element_type=F32)]
    psum x6 -> x0, blocking collectives: 147 us -> none  [the longest x4 72.7 us: row_sums(): lax.psum((jnp.sum(first_part, axis=1), jnp.sum(second_part, axis=1)), 'row')]
    ppermute x0 -> x126, starting transfers between devices: none -> 137 us  [the longest x42 81.4 us: shift(): return lax.ppermute(v, 'row', [(i, (i + s) % n) for i in range(n)])]
    convert_element_type x19 -> x24, other arithmetic: 120 us -> 27.4 us  [the longest x4 12.7 us: scatter(): (a.astype(F32) + self.core(b).astype(F32)).astype(BF)]
  transfers between devices with their start and end apart: 17 -> 126, of which waited for: 16 -> 51; matrix products, arithmetic and copies ran while one was open for 1% -> 29% of each run, Pallas kernels for 0% -> 5%
where the time goes in v1:
time: 857 us; the launch traced here: 848 us
  waiting for transfers between devices  271 us (32%)
  matrix products  171 us (20%)
  starting transfers between devices  137 us (16%)
  local copies, waits for them, and re-layouts  116 us (14%)
  Pallas kernels  77.6 us (9%)
  other arithmetic  72.7 us (8%)
    ppermute x42, waiting for transfers between devices, shift(): return lax.ppermute(v, 'row', [(i, (i + s) % n) for i in range(n)])  127 us
    ppermute x23, waiting for transfers between devices, x(): return lax.ppermute(v, 'dp', [(i, i ^ 2) for i in range(4)])  86.9 us
    ppermute x42, starting transfers between devices, shift(): return lax.ppermute(v, 'row', [(i, (i + s) % n) for i in range(n)])  81.4 us
    dot_general x4, matrix products, mm(): return jnp.dot(a, b, preferred_element_type=F32)  78.4 us
    dot_general x4, matrix products, mm_t(): lax.dot_general(a, b, (((1,), (1,)), ((), ())), preferred_element_type=F32)  52.4 us
    unnamed x178, local copies, waits for them, and re-layouts  49.9 us
    ppermute x19, waiting for transfers between devices, y(): return lax.ppermute(v, 'col', [(0, 1), (1, 0)])  47.9 us
    dot_general x4, matrix products, tmm(): lax.dot_general(a, b, (((0,), (0,)), ((), ())), preferred_element_type=F32)  40.4 us
  transfers between devices with their start and end apart: 126, of which 51 were waited for; matrix products, arithmetic and copies ran while one was open for 29% of the time, Pallas kernels for 5%

profile of v1, /device:TPU:0, one launch (start us, length us, event | category | flops | bytes accessed | tf_op | source)
XLA Modules:
  0.0 847.9 jit_solution(1025421809094208500)
XLA Ops:
  47.2 7.9 collective-permute-start.22
  112.9 11.7 %collective-permute-done.12 = bf16[512,384]{1,0:T(8,128)(2,1)S(1)} collective-permute-done((bf16[512,384]{1,0:T(8,128)(2,1)S(1)}, bf16[512,384]{1,0:T(8,128)(2,1)S(1)}, u32[]{:S(2)}, u32[]{:S(2)}) %collective-permute-start.12) | collective-permute-done | bytes 393248 | tf_op jit(solution)/shard_map/ppermute | solution.py:169
  135.9 10.2 %collective-permute-done.45 = bf16[512,1024]{1,0:T(8,128)(2,1)S(1)} collective-permute-done((bf16[512,1024]{1,0:T(8,128)(2,1)S(1)}, bf16[512,1024]{1,0:T(8,128)(2,1)S(1)}, u32[]{:S(2)}, u32[]{:S(2)}) %collective-permute-start.45) | collective-permute-done | bytes 1048608 | tf_op jit(solution)/shard_map/ppermute | solution.py:169
  156.9 8.9 %collective-permute-done.38 = bf16[512,512]{1,0:T(8,128)(2,1)S(1)} collective-permute-done((bf16[512,512]{1,0:T(8,128)(2,1)S(1)}, bf16[512,512]{1,0:T(8,128)(2,1)S(1)}, u32[]{:S(2)}, u32[]{:S(2)}) %collective-permute-start.38) | collective-permute-done | bytes 524320 | tf_op jit(solution)/shard_map/ppermute | solution.py:172
  182.5 22.5 %collective-permute-done.1 = bf16[1024,256]{0,1:T(8,128)(2,1)S(1)} collective-permute-done((bf16[1024,256]{0,1:T(8,128)(2,1)S(1)}, bf16[1024,256]{0,1:T(8,128)(2,1)S(1)}, u32[]{:S(2)}, u32[]{:S(2)}) %collective-permute-start.1) | collective-permute-done | bytes 524320 | tf_op jit(solution)/shard_map/ppermute | solution.py:163
  205.0 8.9 %collective-permute-done.2 = bf16[1024,256]{0,1:T(8,128)(2,1)S(1)} collective-permute-done((bf16[1024,256]{0,1:T(8,128)(2,1)S(1)}, bf16[1024,256]{0,1:T(8,128)(2,1)S(1)}, u32[]{:S(2)}, u32[]{:S(2)}) %collective-permute-start.2) | collective-permute-done | bytes 524320 | tf_op jit(solution)/shard_map/ppermute | solution.py:163
  214.0 9.0 %add_convert_fusion.1.qkv_ref = bf16[1024,3072]{1,0:T(8,128)(2,1)} fusion(f32[3072]{0:T(1024)S(1)} %add.380, bf16[1024,3072]{1,0:T(8,128)(2,1)S(1)} %constant_dynamic-update-slice_fusion, bf16[1024,256]{0,1:T(8,128)(2,1)S(1)} %collective-permute-done.2, bf16[1024,256]{0,1:T(8,128)(2,1)S(1)} %collective-permute-done.1, ...), kind=kOutput, calls=%fused_computation.25 | convolution fusion | flops 6457131008 | bytes 14692352 | tf_op jit(solution)/shard_map/dot_general | solution.py:22
  223.0 39.0 %attend_fwd.1 = (bf16[1024,1024]{1,0:T(8,128)(2,1)S(1)}, bf16[16,1024,1024]{2,1,0:T(8,128)(2,1)}, f32[1024,1024]{1,0:T(8,128)}) custom-call(bf16[1024,3072]{1,0:T(8,128)(2,1)} %add_convert_fusion.1.qkv_ref, s32[1024,1]{1,0:T(8,128)S(1)} %copy.64.seg_col_ref, s32[1,1024]{1,0:T(1,128)S(1)} %bitcast.75), custom_call_target="tpu_custom_call" | custom-call | flops 17179869184 | bytes 41943040 | tf_op jit(solution)/shard_map/attend_fwd/pallas_call | solution.py:101
  262.1 6.9 fusion.25
  269.7 9.7 %collective-permute-start.56 = (bf16[1024,256]{0,1:T(8,128)(2,1)}, bf16[1024,256]{0,1:T(8,128)(2,1)}, u32[]{:S(2)}, u32[]{:S(2)}) collective-permute-start(bf16[1024,256]{0,1:T(8,128)(2,1)} %copy.97), channel_id=1, source_target_pairs={{0,4},{2,6},{4,0},{6,2},{1,5},{3,7},{5,1},{7,3},{8,12},{10,14},{12... | collective-permute-start | bytes 1572872 | tf_op jit(solution)/shard_map/ppermute | solution.py:163
  293.9 46.4 %multiply_convert_fusion = (bf16[1024,4096]{1,0:T(8,128)(2,1)}, f32[1024,4096]{1,0:T(8,128)}, f32[1024,4096]{1,0:T(8,128)}) fusion(f32[4096]{0:T(1024)S(1)} %bitcast.122, bf16[1024,4096]{1,0:T(8,128)(2,1)S(1)} %constant_dynamic-update-slice_fusion.16, bf16[1024,1024]{0,1:T(8,128)(2,1)S(1)} %fusion.23.clone.4), kind=kOutput, calls=%fused_computation.10 | convolution fusion | flops 8866758656 | bytes 52445184 | tf_op jit(solution)/shard_map/dot_general | solution.py:22
  341.4 16.1 %fusion.24 = (f32[1024]{0:T(1024)S(1)}, f32[1024]{0:T(1024)S(1)}, f32[1024,1024]{0,1:T(8,128)}) fusion(f32[1024]{0:T(1024)S(1)} %bitcast.128, bf16[1024,4096]{1,0:T(8,128)(2,1)} %get-tuple-element.59, bf16[4096,1024]{1,0:T(8,128)(2,1)} %constant_dynamic-update-slice_fusion.24, f32[1024]{0:T(1024)S(1)} %bitcast.120, f32[1024]{0:T(1024)S(1)} %bitcast.110, ...), kind=kOutput, calls=%fused_computation.243 | convolution fusion | flops 8599369728 | bytes 25194496 | tf_op jit(solution)/shard_map/dot_general | solution.py:22
  369.2 11.7 %convolution_convert_fusion = bf16[4096,1024]{1,0:T(8,128)(2,1)} fusion(bf16[1024,4096]{1,0:T(8,128)(2,1)S(1)} %copy-done.64, bf16[1024,1024]{0,1:T(8,128)(2,1)S(1)} %get-tuple-element.54), kind=kOutput, calls=%fused_computation.26 | convolution fusion | flops 8594128896 | bytes 18874368 | tf_op jit(solution)/shard_map/dot_general | solution.py:30
  380.9 23.5 %convert_reduce_fusion = (f32[4096]{0:T(1024)S(1)}, bf16[1024,4096]{1,0:T(8,128)(2,1)}) fusion(f32[1024,4096]{1,0:T(8,128)} %get-tuple-element.60, f32[1024,4096]{1,0:T(8,128)} %get-tuple-element.176, f32[4096]{0:T(1024)S(1)} %bitcast.123, bf16[1024,1024]{0,1:T(8,128)(2,1)S(1)} %get-tuple-element.54, bf16[4096,1024]{1,0:T(8,128)(2,1)} %constant_dynamic-update-slice_fusion.24), kind=kOutput, calls=%fused_computation.8 | convolution fusion | flops 8661233664 | bytes 52461568 | tf_op jit(solution)/shard_map/dot_general | solution.py:26
  404.4 15.0 %convolution_convert_fusion.1 = bf16[1024,4096]{1,0:T(8,128)(2,1)} fusion(bf16[1024,4096]{1,0:T(8,128)(2,1)} %get-tuple-element.58, f32[1024,1024]{0,1:T(8,128)S(1)} %get-tuple-element.61, f32[1024]{0:T(1024)S(1)} %bitcast.121, f32[1024]{0:T(1024)S(1)} %bitcast.111, f32[1024]{0:T(1024)S(1)} %get-tuple-element.175, f32[1024]{0:T(1024)S(1)} %get-tuple-element.174), kind=kOutput, calls=%fused_computation.27 | convolution fusion | flops 8599371776 | bytes 20987904 | tf_op jit(solution)/shard_map/dot_general | solution.py:30
  419.4 16.6 %multiply_reduce_fusion = (f32[1024]{0:T(1024)S(1)}, f32[1024]{0:T(1024)S(1)}, f32[1024]{0:T(1024)S(1)}, f32[1024]{0:T(1024)S(1)}, f32[1024,1024]{0,1:T(8,128)S(1)}) fusion(f32[1024,1024]{0,1:T(8,128)S(1)} %get-tuple-element.61, f32[1024]{0:T(1024)S(1)} %get-tuple-element.175, f32[1024]{0:T(1024)S(1)} %get-tuple-element.174, f32[1024]{0:T(1024)S(1)} %bitcast.112, ...), kind=kOutput, calls=%fused_computation.40 | convolution fusion | flops 8616144896 | bytes 31506432 | tf_op jit(solution)/shard_map/dot_general | solution.py:26
  443.1 38.5 %attend_bwd.1 = bf16[1024,3072]{1,0:T(8,128)(2,1)} custom-call(bf16[1024,3072]{1,0:T(8,128)(2,1)} %add_convert_fusion.1.qkv_ref, bf16[1024,1024]{1,0:T(8,128)(2,1)S(1)} %convolution_convert_fusion.4.do_ref, bf16[1024,1024]{1,0:T(8,128)(2,1)S(1)} %copy-done.3, f32[1024,1024]{1,0:T(8,128)} %get-tuple-element.21.linv_ref, ...), custom_call_target="tpu_custom_call" | custom-call | flops 34359738368 | bytes 50331648 | tf_op jit(solution)/shard_map/attend_bwd/pallas_call | solution.py:131
  486.2 10.0 %add_convert_fusion.2 = bf16[1024,1024]{0,1:T(8,128)(2,1)} fusion(f32[1024,1024]{0,1:T(8,128)S(1)} %copy-done.11, bf16[1024,3072]{1,0:T(8,128)(2,1)S(1)} %copy-done.7, bf16[1024,3072]{1,0:T(8,128)(2,1)} %copy-done.42), kind=kOutput, calls=%fused_computation.42 | convolution fusion | flops 6444548096 | bytes 18874368 | tf_op jit(solution)/shard_map/dot_general | solution.py:26
  498.4 11.3 %convolution_convert_fusion.2 = bf16[1024,3072]{1,0:T(8,128)(2,1)} fusion(bf16[1024,3072]{1,0:T(8,128)(2,1)} %attend_bwd.1, bf16[1024,256]{0,1:T(8,128)(2,1)} %copy-done.62, bf16[1024,256]{0,1:T(8,128)(2,1)} %copy-done.60, bf16[1024,256]{0,1:T(8,128)(2,1)} %copy-done.58, bf16[1024,256]{0,1:T(8,128)(2,1)S(1)} %copy-done.31), kind=kOutput, calls=%fused_computation.34 | convolution fusion | flops 6453985280 | bytes 14680064 | tf_op jit(solution)/shard_map/dot_general | solution.py:30
  553.8 6.9 collective-permute-done.97
  560.7 24.9 %collective-permute-start.60 = (bf16[1024,256]{0,1:T(8,128)(2,1)}, bf16[1024,256]{0,1:T(8,128)(2,1)}, u32[]{:S(2)}, u32[]{:S(2)}) collective-permute-start(bf16[1024,256]{0,1:T(8,128)(2,1)} %get-tuple-element.92), channel_id=1, source_target_pairs={{0,2},{2,4},{4,6},{6,0},{1,3},{3,5},{5,7},{7,1},{8,10},{10,12},{12... | collective-permute-start | bytes 1572872 | tf_op jit(solution)/shard_map/ppermute | solution.py:163
  599.4 10.2 %collective-permute-done.52 = bf16[1024,256]{0,1:T(8,128)(2,1)} collective-permute-done((bf16[1024,256]{0,1:T(8,128)(2,1)}, bf16[1024,256]{0,1:T(8,128)(2,1)}, u32[]{:S(2)}, u32[]{:S(2)}) %collective-permute-start.52) | collective-permute-done | bytes 524320 | tf_op jit(solution)/shard_map/ppermute | solution.py:163
  617.0 15.0 %collective-permute-done.53 = bf16[1024,256]{0,1:T(8,128)(2,1)} collective-permute-done((bf16[1024,256]{0,1:T(8,128)(2,1)}, bf16[1024,256]{0,1:T(8,128)(2,1)}, u32[]{:S(2)}, u32[]{:S(2)}) %collective-permute-start.53) | collective-permute-done | bytes 524320 | tf_op jit(solution)/shard_map/ppermute | solution.py:163
  640.8 7.9 collective-permute-start.89
  684.2 7.0 collective-permute-done.93
  699.4 7.0 collective-permute-done.116
  710.8 6.7 collective-permute-done.103
  718.7 8.2 collective-permute-done.65
  738.3 8.5 %collective-permute-done.69 = bf16[256,384]{1,0:T(8,128)(2,1)S(1)} collective-permute-done((bf16[256,384]{1,0:T(8,128)(2,1)S(1)}, bf16[256,384]{1,0:T(8,128)(2,1)S(1)}, u32[]{:S(2)}, u32[]{:S(2)}) %collective-permute-start.69) | collective-permute-done | bytes 196640 | tf_op jit(solution)/shard_map/ppermute | solution.py:163
  764.2 16.5 %collective-permute-done.104 = bf16[1024,512]{1,0:T(8,128)(2,1)S(1)} collective-permute-done((bf16[1024,512]{1,0:T(8,128)(2,1)S(1)}, bf16[1024,512]{1,0:T(8,128)(2,1)S(1)}, u32[]{:S(2)}, u32[]{:S(2)}) %collective-permute-start.104) | collective-permute-done | bytes 1048608 | tf_op jit(solution)/shard_map/ppermute | solution.py:169
  784.0 9.5 %collective-permute-done.108 = bf16[256,512]{1,0:T(8,128)(2,1)S(1)} collective-permute-done((bf16[256,512]{1,0:T(8,128)(2,1)S(1)}, bf16[256,512]{1,0:T(8,128)(2,1)S(1)}, u32[]{:S(2)}, u32[]{:S(2)}) %collective-permute-start.108) | collective-permute-done | bytes 262176 | tf_op jit(solution)/shard_map/ppermute | solution.py:163
  821.0 8.3 collective-permute-done.125
  (602 shorter events, 384.8 us)
Async XLA Ops:
  5.5 32.0 %collective-permute-start.27 = (bf16[6,256]{1,0:T(8,128)(2,1)}, bf16[6,256]{1,0:T(8,128)(2,1)S(1)}, u32[]{:S(2)}, u32[]{:S(2)}) collective-permute-start(bf16[6,256]{1,0:T(8,128)(2,1)} %stack.93), channel_id=1, source_target_pairs={{0,2},{2,4},{4,6},{6,0},{1,3},{3,5},{5,7},{7,1},{8,10},{10,12},{12... | collective-permute-start | bytes 9224 | tf_op jit(solution)/shard_map/ppermute | solution.py:163
  59.9 34.8 %collective-permute-start.7 = (bf16[1024,384]{1,0:T(8,128)(2,1)}, bf16[1024,384]{1,0:T(8,128)(2,1)}, u32[]{:S(2)}, u32[]{:S(2)}) collective-permute-start(bf16[1024,384]{1,0:T(8,128)(2,1)} %get-tuple-element.139), channel_id=1, source_target_pairs={{0,16},{8,24},{16,0},{24,8},{1,17},{9,25},{17,1},{25,9},{2,18},{10... | collective-permute-start | bytes 2359304 | tf_op jit(solution)/shard_map/ppermute | solution.py:169
  90.2 36.1 %collective-permute-start.34 = (bf16[1024,512]{1,0:T(8,128)(2,1)S(1)}, bf16[1024,512]{1,0:T(8,128)(2,1)}, u32[]{:S(2)}, u32[]{:S(2)}) collective-permute-start(bf16[1024,512]{1,0:T(8,128)(2,1)S(1)} %get-tuple-element.129), channel_id=1, source_target_pairs={{0,16},{8,24},{16,0},{24,8},{1,17},{9,25},{17,1},{25,9},{2,18},{10... | collective-permute-start | bytes 3145736 | tf_op jit(solution)/shard_map/ppermute | solution.py:169
  106.2 39.9 %collective-permute-start.45 = (bf16[512,1024]{1,0:T(8,128)(2,1)S(1)}, bf16[512,1024]{1,0:T(8,128)(2,1)S(1)}, u32[]{:S(2)}, u32[]{:S(2)}) collective-permute-start(bf16[512,1024]{1,0:T(8,128)(2,1)S(1)} %get-tuple-element.127), channel_id=1, source_target_pairs={{0,16},{8,24},{16,0},{24,8},{1,17},{9,25},{17,1},{25,9},{2,18},{10... | collective-permute-start | bytes 3145736 | tf_op jit(solution)/shard_map/ppermute | solution.py:169
  110.5 36.8 %collective-permute-start.33 = (bf16[1024,512]{1,0:T(8,128)(2,1)S(1)}, bf16[1024,512]{1,0:T(8,128)(2,1)S(1)}, u32[]{:S(2)}, u32[]{:S(2)}) collective-permute-start(bf16[1024,512]{1,0:T(8,128)(2,1)S(1)} %get-tuple-element.129), channel_id=1, source_target_pairs={{0,8},{8,0},{16,24},{24,16},{1,9},{9,1},{17,25},{25,17},{2,10},{10... | collective-permute-start | bytes 3145736 | tf_op jit(solution)/shard_map/ppermute | solution.py:166
  167.8 37.2 %collective-permute-start.1 = (bf16[1024,256]{0,1:T(8,128)(2,1)S(1)}, bf16[1024,256]{0,1:T(8,128)(2,1)S(1)}, u32[]{:S(2)}, u32[]{:S(2)}) collective-permute-start(bf16[1024,256]{0,1:T(8,128)(2,1)S(1)} %copy-done.33), channel_id=1, source_target_pairs={{0,4},{2,6},{4,0},{6,2},{1,5},{3,7},{5,1},{7,3},{8,12},{10,14},{12... | collective-permute-start | bytes 1572872 | tf_op jit(solution)/shard_map/ppermute | solution.py:163
  175.8 38.2 %collective-permute-start.2 = (bf16[1024,256]{0,1:T(8,128)(2,1)S(1)}, bf16[1024,256]{0,1:T(8,128)(2,1)S(1)}, u32[]{:S(2)}, u32[]{:S(2)}) collective-permute-start(bf16[1024,256]{0,1:T(8,128)(2,1)S(1)} %copy-done.32), channel_id=1, source_target_pairs={{0,6},{2,0},{4,2},{6,4},{1,7},{3,1},{5,3},{7,5},{8,14},{10,8},{12,... | collective-permute-start | bytes 1572872 | tf_op jit(solution)/shard_map/ppermute | solution.py:163
  178.6 178.9 %collective-permute-start.55 = (bf16[1024,256]{0,1:T(8,128)(2,1)}, bf16[1024,256]{0,1:T(8,128)(2,1)}, u32[]{:S(2)}, u32[]{:S(2)}) collective-permute-start(bf16[1024,256]{0,1:T(8,128)(2,1)} %copy.96), channel_id=1, source_target_pairs={{0,2},{2,4},{4,6},{6,0},{1,3},{3,5},{5,7},{7,1},{8,10},{10,12},{12... | collective-permute-start | bytes 1572872 | tf_op jit(solution)/shard_map/ppermute | solution.py:163
  180.2 89.4 %collective-permute-start.35 = (bf16[1024,512]{1,0:T(8,128)(2,1)}, bf16[1024,512]{1,0:T(8,128)(2,1)}, u32[]{:S(2)}, u32[]{:S(2)}) collective-permute-start(bf16[1024,512]{1,0:T(8,128)(2,1)} %collective-permute-done.34), channel_id=1, source_target_pairs={{0,8},{8,0},{16,24},{24,16},{1,9},{9,1},{17,25},{25,17},{2,10},{10... | collective-permute-start | bytes 3145736 | tf_op jit(solution)/shard_map/ppermute | solution.py:166
  182.5 98.4 %collective-permute-start.37 = (bf16[1024,512]{1,0:T(8,128)(2,1)S(1)}, bf16[1024,512]{1,0:T(8,128)(2,1)}, u32[]{:S(2)}, u32[]{:S(2)}) collective-permute-start(bf16[1024,512]{1,0:T(8,128)(2,1)S(1)} %collective-permute-done.36), channel_id=1, source_target_pairs={{0,8},{8,0},{16,24},{24,16},{1,9},{9,1},{17,25},{25,17},{2,10},{10... | collective-permute-start | bytes 3145736 | tf_op jit(solution)/shard_map/ppermute | solution.py:166
  205.0 77.7 %collective-permute-start.46 = (bf16[512,1024]{1,0:T(8,128)(2,1)S(1)}, bf16[512,1024]{1,0:T(8,128)(2,1)}, u32[]{:S(2)}, u32[]{:S(2)}) collective-permute-start(bf16[512,1024]{1,0:T(8,128)(2,1)S(1)} %collective-permute-done.45), channel_id=1, source_target_pairs={{0,8},{8,0},{16,24},{24,16},{1,9},{9,1},{17,25},{25,17},{2,10},{10... | collective-permute-start | bytes 3145736 | tf_op jit(solution)/shard_map/ppermute | solution.py:166
  214.0 75.8 %collective-permute-start.48 = (bf16[512,1024]{1,0:T(8,128)(2,1)S(1)}, bf16[512,1024]{1,0:T(8,128)(2,1)}, u32[]{:S(2)}, u32[]{:S(2)}) collective-permute-start(bf16[512,1024]{1,0:T(8,128)(2,1)S(1)} %collective-permute-done.47), channel_id=1, source_target_pairs={{0,8},{8,0},{16,24},{24,16},{1,9},{9,1},{17,25},{25,17},{2,10},{10... | collective-permute-start | bytes 3145736 | tf_op jit(solution)/shard_map/ppermute | solution.py:166
  269.7 87.9 %collective-permute-start.56 = (bf16[1024,256]{0,1:T(8,128)(2,1)}, bf16[1024,256]{0,1:T(8,128)(2,1)}, u32[]{:S(2)}, u32[]{:S(2)}) collective-permute-start(bf16[1024,256]{0,1:T(8,128)(2,1)} %copy.97), channel_id=1, source_target_pairs={{0,4},{2,6},{4,0},{6,2},{1,5},{3,7},{5,1},{7,3},{8,12},{10,14},{12... | collective-permute-start | bytes 1572872 | tf_op jit(solution)/shard_map/ppermute | solution.py:163
  282.8 74.8 %collective-permute-start.57 = (bf16[1024,256]{0,1:T(8,128)(2,1)}, bf16[1024,256]{0,1:T(8,128)(2,1)}, u32[]{:S(2)}, u32[]{:S(2)}) collective-permute-start(bf16[1024,256]{0,1:T(8,128)(2,1)} %copy.98), channel_id=1, source_target_pairs={{0,6},{2,0},{4,2},{6,4},{1,7},{3,1},{5,3},{7,5},{8,14},{10,8},{12,... | collective-permute-start | bytes 1572872 | tf_op jit(solution)/shard_map/ppermute | solution.py:163
  289.8 50.6 %collective-permute-start.51 = (bf16[512,1024]{1,0:T(8,128)(2,1)S(1)}, bf16[512,1024]{1,0:T(8,128)(2,1)S(1)}, u32[]{:S(2)}, u32[]{:S(2)}) collective-permute-start(bf16[512,1024]{1,0:T(8,128)(2,1)S(1)} %pad_maximum_fusion.4), channel_id=1, source_target_pairs={{0,8},{8,0},{16,24},{24,16},{1,9},{9,1},{17,25},{25,17},{2,10},{10... | collective-permute-start | bytes 3145736 | tf_op jit(solution)/shard_map/ppermute | solution.py:166
  496.2 40.8 %collective-permute-start.94 = (f32[6,1024]{1,0:T(8,128)S(1)}, f32[6,1024]{1,0:T(8,128)S(1)}, u32[]{:S(2)}, u32[]{:S(2)}) collective-permute-start(f32[6,1024]{1,0:T(8,128)S(1)} %stack.109), channel_id=1, source_target_pairs={{0,8},{8,0},{16,24},{24,16},{1,9},{9,1},{17,25},{25,17},{2,10},{10... | collective-permute-start | bytes 73736 | tf_op jit(solution)/shard_map/ppermute | solution.py:166
  497.8 49.4 %collective-permute-start.82 = (bf16[128,1024]{1,0:T(8,128)(2,1)}, bf16[128,1024]{1,0:T(8,128)(2,1)S(1)}, u32[]{:S(2)}, u32[]{:S(2)}) collective-permute-start(bf16[128,1024]{1,0:T(8,128)(2,1)} %get-tuple-element.88), channel_id=1, source_target_pairs={{0,8},{8,0},{16,24},{24,16},{1,9},{9,1},{17,25},{25,17},{2,10},{10... | collective-permute-start | bytes 786440 | tf_op jit(solution)/shard_map/ppermute | solution.py:166
  537.0 60.1 %collective-permute-start.58 = (bf16[1024,256]{0,1:T(8,128)(2,1)}, bf16[1024,256]{0,1:T(8,128)(2,1)S(1)}, u32[]{:S(2)}, u32[]{:S(2)}) collective-permute-start(bf16[1024,256]{0,1:T(8,128)(2,1)} %get-tuple-element.94), channel_id=1, source_target_pairs={{0,6},{2,0},{4,2},{6,4},{1,7},{3,1},{5,3},{7,5},{8,14},{10,8},{12,... | collective-permute-start | bytes 1572872 | tf_op jit(solution)/shard_map/ppermute | solution.py:163
  547.2 51.2 %collective-permute-start.59 = (bf16[1024,256]{0,1:T(8,128)(2,1)}, bf16[1024,256]{0,1:T(8,128)(2,1)S(1)}, u32[]{:S(2)}, u32[]{:S(2)}) collective-permute-start(bf16[1024,256]{0,1:T(8,128)(2,1)} %get-tuple-element.93), channel_id=1, source_target_pairs={{0,4},{2,6},{4,0},{6,2},{1,5},{3,7},{5,1},{7,3},{8,12},{10,14},{12... | collective-permute-start | bytes 1572872 | tf_op jit(solution)/shard_map/ppermute | solution.py:163
  549.6 36.0 %collective-permute-start.98 = (f32[6,256]{1,0:T(8,128)S(1)}, f32[6,256]{1,0:T(8,128)S(1)}, u32[]{:S(2)}, u32[]{:S(2)}) collective-permute-start(f32[6,256]{1,0:T(8,128)S(1)} %get-tuple-element.153), channel_id=1, source_target_pairs={{0,4},{2,6},{4,0},{6,2},{1,5},{3,7},{5,1},{7,3},{8,12},{10,14},{12... | collective-permute-start | bytes 18440 | tf_op jit(solution)/shard_map/ppermute | solution.py:163
  550.3 35.3 %collective-permute-start.99 = (f32[6,256]{1,0:T(8,128)S(1)}, f32[6,256]{1,0:T(8,128)S(1)}, u32[]{:S(2)}, u32[]{:S(2)}) collective-permute-start(f32[6,256]{1,0:T(8,128)S(1)} %get-tuple-element.152), channel_id=1, source_target_pairs={{0,2},{2,4},{4,6},{6,0},{1,3},{3,5},{5,7},{7,1},{8,10},{10,12},{12... | collective-permute-start | bytes 18440 | tf_op jit(solution)/shard_map/ppermute | solution.py:163
  560.7 37.6 %collective-permute-start.60 = (bf16[1024,256]{0,1:T(8,128)(2,1)}, bf16[1024,256]{0,1:T(8,128)(2,1)}, u32[]{:S(2)}, u32[]{:S(2)}) collective-permute-start(bf16[1024,256]{0,1:T(8,128)(2,1)} %get-tuple-element.92), channel_id=1, source_target_pairs={{0,2},{2,4},{4,6},{6,0},{1,3},{3,5},{5,7},{7,1},{8,10},{10,12},{12... | collective-permute-start | bytes 1572872 | tf_op jit(solution)/shard_map/ppermute | solution.py:163
  595.6 36.3 %collective-permute-start.53 = (bf16[1024,256]{0,1:T(8,128)(2,1)}, bf16[1024,256]{0,1:T(8,128)(2,1)}, u32[]{:S(2)}, u32[]{:S(2)}) collective-permute-start(bf16[1024,256]{0,1:T(8,128)(2,1)} %get-tuple-element.101), channel_id=1, source_target_pairs={{0,4},{2,6},{4,0},{6,2},{1,5},{3,7},{5,1},{7,3},{8,12},{10,14},{12... | collective-permute-start | bytes 1572872 | tf_op jit(solution)/shard_map/ppermute | solution.py:163
  597.0 36.2 %collective-permute-start.54 = (bf16[1024,256]{0,1:T(8,128)(2,1)}, bf16[1024,256]{0,1:T(8,128)(2,1)}, u32[]{:S(2)}, u32[]{:S(2)}) collective-permute-start(bf16[1024,256]{0,1:T(8,128)(2,1)} %get-tuple-element.100), channel_id=1, source_target_pairs={{0,2},{2,4},{4,6},{6,0},{1,3},{3,5},{5,7},{7,1},{8,10},{10,12},{12... | collective-permute-start | bytes 1572872 | tf_op jit(solution)/shard_map/ppermute | solution.py:163
  598.4 40.6 %collective-permute-start.81 = (bf16[128,1024]{1,0:T(8,128)(2,1)}, bf16[128,1024]{1,0:T(8,128)(2,1)S(1)}, u32[]{:S(2)}, u32[]{:S(2)}) collective-permute-start(bf16[128,1024]{1,0:T(8,128)(2,1)} %get-tuple-element.85), channel_id=1, source_target_pairs={{0,8},{8,0},{16,24},{24,16},{1,9},{9,1},{17,25},{25,17},{2,10},{10... | collective-permute-start | bytes 786440 | tf_op jit(solution)/shard_map/ppermute | solution.py:166
  598.4 40.6 %collective-permute-start.85 = (bf16[128,1024]{1,0:T(8,128)(2,1)}, bf16[128,1024]{1,0:T(8,128)(2,1)}, u32[]{:S(2)}, u32[]{:S(2)}) collective-permute-start(bf16[128,1024]{1,0:T(8,128)(2,1)} %pad_maximum_fusion.27), channel_id=1, source_target_pairs={{0,16},{8,24},{16,0},{24,8},{1,17},{9,25},{17,1},{25,9},{2,18},{10... | collective-permute-start | bytes 786440 | tf_op jit(solution)/shard_map/ppermute | solution.py:169
  631.9 34.4 %collective-permute-start.114 = (bf16[512,1024]{1,0:T(8,128)(2,1)}, bf16[512,1024]{1,0:T(8,128)(2,1)}, u32[]{:S(2)}, u32[]{:S(2)}) collective-permute-start(bf16[512,1024]{1,0:T(8,128)(2,1)} %get-tuple-element.65), channel_id=1, source_target_pairs={{0,8},{8,0},{16,24},{24,16},{1,9},{9,1},{17,25},{25,17},{2,10},{10... | collective-permute-start | bytes 3145736 | tf_op jit(solution)/shard_map/ppermute | solution.py:166
  671.3 75.8 %collective-permute-start.113 = (bf16[512,1024]{1,0:T(8,128)(2,1)}, bf16[512,1024]{1,0:T(8,128)(2,1)}, u32[]{:S(2)}, u32[]{:S(2)}) collective-permute-start(bf16[512,1024]{1,0:T(8,128)(2,1)} %get-tuple-element.62), channel_id=1, source_target_pairs={{0,8},{8,0},{16,24},{24,16},{1,9},{9,1},{17,25},{25,17},{2,10},{10... | collective-permute-start | bytes 3145736 | tf_op jit(solution)/shard_map/ppermute | solution.py:166
  671.5 47.2 %collective-permute-start.61 = (bf16[1024,384]{1,0:T(8,128)(2,1)}, bf16[1024,384]{1,0:T(8,128)(2,1)}, u32[]{:S(2)}, u32[]{:S(2)}) collective-permute-start(bf16[1024,384]{1,0:T(8,128)(2,1)} %get-tuple-element.76), channel_id=1, source_target_pairs={{0,8},{8,0},{16,24},{24,16},{1,9},{9,1},{17,25},{25,17},{2,10},{10... | collective-permute-start | bytes 2359304 | tf_op jit(solution)/shard_map/ppermute | solution.py:166
  718.7 45.6 %collective-permute-start.100 = (bf16[1024,512]{1,0:T(8,128)(2,1)S(1)}, bf16[1024,512]{1,0:T(8,128)(2,1)S(1)}, u32[]{:S(2)}, u32[]{:S(2)}) collective-permute-start(bf16[1024,512]{1,0:T(8,128)(2,1)S(1)} %copy-done.20), channel_id=1, source_target_pairs={{0,8},{8,0},{16,24},{24,16},{1,9},{9,1},{17,25},{25,17},{2,10},{10... | collective-permute-start | bytes 3145736 | tf_op jit(solution)/shard_map/ppermute | solution.py:166
  726.9 33.7 %collective-permute-start.117 = (bf16[512,1024]{1,0:T(8,128)(2,1)S(1)}, bf16[512,1024]{1,0:T(8,128)(2,1)S(1)}, u32[]{:S(2)}, u32[]{:S(2)}) collective-permute-start(bf16[512,1024]{1,0:T(8,128)(2,1)S(1)} %pad_maximum_fusion.9), channel_id=1, source_target_pairs={{0,16},{8,24},{16,0},{24,8},{1,17},{9,25},{17,1},{25,9},{2,18},{10... | collective-permute-start | bytes 3145736 | tf_op jit(solution)/shard_map/ppermute | solution.py:169
  747.1 33.7 %collective-permute-start.104 = (bf16[1024,512]{1,0:T(8,128)(2,1)S(1)}, bf16[1024,512]{1,0:T(8,128)(2,1)S(1)}, u32[]{:S(2)}, u32[]{:S(2)}) collective-permute-start(bf16[1024,512]{1,0:T(8,128)(2,1)S(1)} %pad_maximum_fusion.6), channel_id=1, source_target_pairs={{0,16},{8,24},{16,0},{24,8},{1,17},{9,25},{17,1},{25,9},{2,18},{10... | collective-permute-start | bytes 3145736 | tf_op jit(solution)/shard_map/ppermute | solution.py:169
  (161 other events, 2621.7 us)

commit v2 on v1

--- a/solution.py
+++ b/solution.py
@@ -34,31 +34,76 @@
     return jax.nn.gelu(v, approximate=False)
 
 
-def attend_fwd_kernel(qkv_ref, seg_col_ref, seg_row_ref, o_ref, p_ref, linv_ref):
+def attend_rows(qkv_ref, seg_col_ref, seg_row, o_ref, p_ref, linv_ref, i):
     lane = lax.broadcasted_iota(jnp.int32, (QB, 128), 1)
-    seg_row = seg_row_ref[...]
+    scale = HD ** (-0.5) * math.log2(math.e)
+    rows = slice(i * QB, (i + 1) * QB)
+    q = qkv_ref[rows, 0:128]
     k = qkv_ref[:, 128:256]
     v = qkv_ref[:, 256:384]
-    scale = HD ** (-0.5) * math.log2(math.e)
+    seg_col = seg_col_ref[rows, :]
+    outs = []
+    for h in range(2):
+        mine = (lane < HD) if h == 0 else (lane >= HD)
+        qm = jnp.where(mine, q, jnp.zeros_like(q))
+        s = mm_t(qm, k)
+        s = jnp.where(seg_col == seg_row, s * scale, NEG)
+        top = jnp.max(s, axis=1, keepdims=True)
+        p = jnp.exp2(s - top)
+        total = jnp.sum(p, axis=1, keepdims=True)
+        pb = p.astype(BF)
+        p_ref[h, rows, :] = pb
+        inv = 1.0 / total
+        outs.append((mm(pb, v) * inv, jnp.broadcast_to(inv, (QB, 128))))
+    o_ref[rows, :] = jnp.where(lane < HD, outs[0][0], outs[1][0]).astype(BF)
+    linv_ref[rows, :] = jnp.where(lane < HD, outs[0][1], outs[1][1])
+
+
+def attend_fwd_kernel(
+    x_ref, w_ref, b_ref, seg_col_ref, seg_row_ref, po, pu, pd,
+    qkv_ref, o_ref, p_ref, linv_ref, wo, wu, wd, o_recv, o_sent, u_recv, u_sent, d_recv, d_sent,
+):
+    j = pl.program_id(0)
+    peers = Peers()
+    go = Gather(peers, po, wo, False, o_recv, o_sent, RING + NEAR + FAR)
+    gu = Gather(peers, pu, wu, True, u_recv, u_sent, RING + NEAR)
+    gd = Gather(peers, pd, wd, False, d_recv, d_sent, RING + DOWN_NEAR)
+    every = (go, gu, gd)
+
+    def hook(at, *stages):
+        @pl.when(j == at)
+        def _():
+            for which, blocks in stages:
+                for g in which:
+                    g.relay(*blocks)
+
+    @pl.when(j == 0)
+    def _():
+        peers.greet(ALL_PEERS)
+        for g in every:
+            g.start()
+
+    seg_row = seg_row_ref[...]
+    hook(1, ((go, gu), [(1, 0)]))
+    hook(2, (every, [(0, 2), (0, 4)]))
+    hook(3, ((go, gu), [(2, 0)]), ((go,), [(1, 2), (1, 4)]))
+    hook(4, ((gu, gd), [(1, 2), (1, 4)]))
+    hook(5, ((go, gu), [(3, 0)]))
+    hook(6, (every, [(2, 2), (2, 4)]), ((go,), [(0, 6), (1, 6)]))
+    hook(7, ((go,), [(3, 2), (3, 4)]))
+    qkv_ref[...] = (mm(x_ref[...], w_ref[...]) + b_ref[...]).astype(BF)
     for i in range(SEQ // QB):
-        rows = slice(i * QB, (i + 1) * QB)
-        q = qkv_ref[rows, 0:128]
-        seg_col = seg_col_ref[rows, :]
-        outs = []
-        for h in range(2):
-            mine = (lane < HD) if h == 0 else (lane >= HD)
-            qm = jnp.where(mine, q, jnp.zeros_like(q))
-            s = mm_t(qm, k)
-            s = jnp.where(seg_col == seg_row, s * scale, NEG)
-            top = jnp.max(s, axis=1, keepdims=True)
-            p = jnp.exp2(s - top)
-            total = jnp.sum(p, axis=1, keepdims=True)
-            pb = p.astype(BF)
-            p_ref[h, rows, :] = pb
-            inv = 1.0 / total
-            outs.append((mm(pb, v) * inv, jnp.broadcast_to(inv, (QB, 128))))
-        o_ref[rows, :] = jnp.where(lane < HD, outs[0][0], outs[1][0]).astype(BF)
-        linv_ref[rows, :] = jnp.where(lane < HD, outs[0][1], outs[1][1])
+        if i == SEQ // QB // 2:
+            hook(1, ((gd,), [(1, 0)]))
+            hook(3, ((gd,), [(2, 0)]))
+            hook(5, ((gd,), [(3, 0)]))
+            hook(7, ((go,), [(2, 6), (3, 6)]), ((gu,), [(3, 2), (3, 4)]))
+        attend_rows(qkv_ref, seg_col_ref, seg_row, o_ref, p_ref, linv_ref, i)
+
+    @pl.when(j == 7)
+    def _():
+        for g in every:
+            g.finish()
 
 
 def attend_bwd_kernel(qkv_ref, do_ref, o_ref, linv_ref, p_ref, g_ref, ds_ref):
@@ -93,37 +138,53 @@
     g_ref[:, 256:384] = jnp.transpose(jnp.concatenate(dvt, 0)).astype(BF)
 
 
-VMEM_LIMIT = 48 * 1024 * 1024
-
-
-def attend_fwd(qkv, seg_col, seg_row):
-    slots = qkv.shape[1] // 384
+VMEM_LIMIT = 56 * 1024 * 1024
+
+
+def attend_fwd(x, w_qkv, b_qkv, seg_col, seg_row, po, pu, pd):
+    slots = w_qkv.shape[1] // 384
+    whole = pl.BlockSpec(memory_space=pl.ANY)
+    dma = pltpu.SemaphoreType.DMA
     return pl.pallas_call(
         attend_fwd_kernel,
         grid=(slots,),
         in_specs=[
-            pl.BlockSpec((SEQ, 384), lambda j: (0, j)),
+            pl.BlockSpec((SEQ, x.shape[1]), lambda j: (0, 0)),
+            pl.BlockSpec((x.shape[1], 384), lambda j: (0, j)),
+            pl.BlockSpec((1, 384), lambda j: (0, j)),
             pl.BlockSpec((SEQ, 1), lambda j: (0, 0)),
             pl.BlockSpec((1, SEQ), lambda j: (0, 0)),
+            whole,
+            whole,
+            whole,
         ],
         out_specs=[
+            pl.BlockSpec((SEQ, 384), lambda j: (0, j)),
             pl.BlockSpec((SEQ, 128), lambda j: (0, j)),
             pl.BlockSpec((2, SEQ, SEQ), lambda j: (j, 0, 0)),
             pl.BlockSpec((SEQ, 128), lambda j: (0, j)),
+            whole,
+            whole,
+            whole,
         ],
         out_shape=[
+            jax.ShapeDtypeStruct((SEQ, slots * 384), BF),
             jax.ShapeDtypeStruct((SEQ, slots * 128), BF),
             jax.ShapeDtypeStruct((slots * 2, SEQ, SEQ), BF),
             jax.ShapeDtypeStruct((SEQ, slots * 128), F32),
-        ],
-        compiler_params=pltpu.CompilerParams(vmem_limit_bytes=VMEM_LIMIT),
+            jax.ShapeDtypeStruct((8 * po.shape[0], 4 * po.shape[1]), BF),
+            jax.ShapeDtypeStruct((4 * pu.shape[0], 8 * pu.shape[1]), BF),
+            jax.ShapeDtypeStruct((8 * pd.shape[0], 4 * pd.shape[1]), BF),
+        ],
+        scratch_shapes=[dma((32,)), dma((32,))] * 3,
+        compiler_params=pltpu.CompilerParams(vmem_limit_bytes=VMEM_LIMIT, collective_id=1, has_side_effects=True),
         cost_estimate=pl.CostEstimate(
             flops=slots * 2 * 4 * SEQ * SEQ * 256,
             bytes_accessed=slots * 5 * SEQ * SEQ,
             transcendentals=slots * 2 * SEQ * SEQ,
         ),
         name="attend_fwd",
-    )(qkv, seg_col, seg_row)
+    )(x, w_qkv, b_qkv, seg_col, seg_row, po, pu, pd)
 
 
 def attend_bwd(qkv, do, o, linv, p):
@@ -149,6 +210,497 @@
         ),
         name="attend_bwd",
     )(qkv, do, o, linv, p)
+
+
+MESH = pl.DeviceIdType.MESH
+ANY = pl.BlockSpec(memory_space=pl.ANY)
+DMA = pltpu.SemaphoreType.DMA
+
+
+class Peers:
+    def __init__(self):
+        self.r = lax.axis_index("row")
+        d = lax.axis_index("dp")
+        self.ids = {
+            "core": {"dp": d + 1 - 2 * lax.rem(d, 2)},
+            "x": {"dp": lax.rem(d + 2, 4)},
+            "y": {"col": 1 - lax.axis_index("col")},
+            1: {"row": lax.rem(self.r + 1, 4)},
+            2: {"row": lax.rem(self.r + 2, 4)},
+            3: {"row": lax.rem(self.r + 3, 4)},
+        }
+
+    def greet(self, names):
+        barrier = pltpu.get_barrier_semaphore()
+        for name in names:
+            pl.semaphore_signal(barrier, inc=1, device_id=self.ids[name], device_id_type=MESH)
+        pl.semaphore_wait(barrier, len(names))
+
+
+def send(peers, name, src, dst, send_sem, recv_sem):
+    return pltpu.make_async_remote_copy(
+        src_ref=src, dst_ref=dst, send_sem=send_sem, recv_sem=recv_sem, device_id=peers.ids[name], device_id_type=MESH
+    )
+
+
+def near_edges(s):
+    return [("x", s, 0, s, 2), ("y", s, 0, s, 4), ("core", s, 0, s, 1)]
+
+
+def second_edges(s):
+    return [("core", s, 2, s, 3), ("core", s, 4, s, 5)]
+
+
+def far_edges(s):
+    return [("y", s, 2, s, 6) if s % 2 == 0 else ("x", s, 4, s, 6), ("core", s, 6, s, 7)]
+
+
+RING = [(1, s, 0, s + 1, 0) for s in range(3)]
+NEAR = [e for s in range(4) for e in near_edges(s) + second_edges(s)]
+FAR = [e for s in range(4) for e in far_edges(s)]
+DOWN_NEAR = [e for s in range(3) for e in near_edges(s) + second_edges(s)] + [("core", 3, 0, 3, 1)]
+DOWN_REST = [e for e in near_edges(3) if e[0] != "core"] + second_edges(3) + FAR
+
+
+class Gather:
+    def __init__(self, peers, piece, full, by_rows, recv, sent, edges):
+        self.peers, self.piece, self.full, self.recv, self.sent = peers, piece, full, recv, sent
+        self.by_rows = by_rows
+        self.n = full.shape[1 if by_rows else 0] // 8
+        self.m = full.shape[0 if by_rows else 1] // 4
+        self.edges = edges
+        self.waited = set()
+        self.emitted = set()
+
+    def blk(self, s, t):
+        a = pl.ds(s * self.m, self.m)
+        b = pl.ds(t * self.n, self.n)
+        return self.full.at[a, b] if self.by_rows else self.full.at[b, a]
+
+    def copy(self, at):
+        name, s, t, s2, t2 = self.edges[at]
+        src = self.piece if (s, t) == (0, 0) and self.piece is not None else self.blk(s, t)
+        return send(self.peers, name, src, self.blk(s2, t2), self.sent.at[at], self.recv.at[at])
+
+    def emit(self, s, t):
+        for at, e in enumerate(self.edges):
+            if e[1:3] == (s, t):
+                assert at not in self.emitted
+                self.emitted.add(at)
+                self.copy(at).start()
+
+    def arrived(self, s, t):
+        for at, e in enumerate(self.edges):
+            if e[3:5] == (s, t) and at not in self.waited:
+                self.waited.add(at)
+                self.copy(at).wait_recv()
+
+    def relay(self, *blocks):
+        for s, t in blocks:
+            self.arrived(s, t)
+            self.emit(s, t)
+
+    def own(self):
+        return pltpu.make_async_copy(self.piece, self.blk(0, 0), self.sent.at[len(self.edges)])
+
+    def start(self):
+        self.emit(0, 0)
+        self.own().start()
+
+    def finish(self):
+        if self.piece is not None:
+            self.own().wait()
+        for at, e in enumerate(self.edges):
+            if at not in self.waited:
+                self.waited.add(at)
+                self.copy(at).wait_recv()
+        assert len(self.emitted) == len(self.edges)
+        for at in range(len(self.edges)):
+            self.copy(at).wait_send()
+
+
+class Inward:
+    def __init__(self, peers, block, rows, recv, sent):
+        self.peers, self.block, self.rows, self.recv, self.sent = peers, block, rows, recv, sent
+
+    def copy(self, s):
+        r = lax.rem(self.peers.r + s, 4)
+        src = self.block.at[pl.ds(pl.multiple_of(r * SEQ, SEQ), SEQ), :]
+        f = self.block.shape[1]
+        dst = self.rows.at[:, pl.ds(s * f, f)]
+        if s == 0:
+            return pltpu.make_async_copy(src, dst, self.sent.at[0])
+        return send(self.peers, s, src, dst, self.sent.at[s], self.recv.at[s])
+
+    def start(self):
+        for s in (2, 1, 3, 0):
+            self.copy(s).start()
+
+    def finish(self):
+        self.copy(0).wait()
+        for s in (1, 2, 3):
+            self.copy(s).wait()
+
+
+ALL_PEERS = ("core", "x", "y", 1, 2, 3)
+
+
+def first_kernel(tokens, piece, x, w, g_recv, g_sent, i_recv, i_sent):
+    peers = Peers()
+    peers.greet(ALL_PEERS)
+    g = Gather(peers, piece, w, True, g_recv, g_sent, RING + NEAR + FAR)
+    a = Inward(peers, tokens, x, i_recv, i_sent)
+    g.start()
+    a.start()
+    for s in (1, 2, 3):
+        g.relay((s, 0), (s - 1, 2), (s - 1, 4))
+    g.relay((3, 2), (3, 4))
+    for s in range(4):
+        g.relay((s, 6))
+    g.finish()
+    a.finish()
+
+
+def first(tokens, piece):
+    return pl.pallas_call(
+        first_kernel,
+        in_specs=[ANY, ANY],
+        out_specs=[ANY, ANY],
+        out_shape=[
+            jax.ShapeDtypeStruct((SEQ, 4 * tokens.shape[1]), BF),
+            jax.ShapeDtypeStruct((4 * piece.shape[0], 8 * piece.shape[1]), BF),
+        ],
+        scratch_shapes=[DMA((32,)), DMA((32,)), DMA((4,)), DMA((4,))],
+        compiler_params=pltpu.CompilerParams(collective_id=0, has_side_effects=True),
+        name="first",
+    )(tokens, piece)
+
+
+RB = 128
+
+
+def norm_rows(v):
+    mean = jnp.mean(v, axis=1, keepdims=True)
+    variance = jnp.mean(v * v, axis=1, keepdims=True) - mean * mean
+    inv = lax.rsqrt(variance + NORM_EPS)
+    return (v - mean) * inv, inv
+
+
+def norm_rows_back(g, normed, inv):
+    mean_g = jnp.mean(g, axis=1, keepdims=True)
+    mean_gn = jnp.mean(g * normed, axis=1, keepdims=True)
+    return inv * (g - mean_g - normed * mean_gn)
+
+
+def gelu_and_slope(v):
+    z = jnp.abs(v) * (0.5 ** 0.5)
+    t = 1.0 / (1.0 + 0.3275911 * z)
+    poly = t * (0.254829592 + t * (-0.284496736 + t * (1.421413741 + t * (-1.453152027 + t * 1.061405429))))
+    bell = jnp.exp2(z * z * -math.log2(math.e))
+    tail = 0.5 * poly * bell
+    cdf = jnp.where(v >= 0, 1.0 - tail, tail)
+    return v * cdf, cdf + v * bell * (1.0 / math.sqrt(2.0 * math.pi))
+
+
+def row_blocks(body, n=RB):
+    def run(i, carry):
+        body(pl.ds(pl.multiple_of(i * n, n), n))
+        return carry
+
+    lax.fori_loop(0, SEQ // n, run, 0)
+
+
+def ff_fwd_kernel(
+    x_ref, att_ref, wo_ref, vec_ref, bu_ref, cot, wu_in, wd_in,
+    wu, wd, act_ref, slope_ref, hlow_ref, normed1_ref, inv1_ref, out_ref, r2_ref, vg_ref,
+    acc, wu_buf, wd_buf, cot_buf, buf_sem, u_recv, u_sent, d_recv, d_sent, i_recv, i_sent,
+):
+    j = pl.program_id(0)
+    peers = Peers()
+    gu = Gather(peers, None, wu, True, u_recv, u_sent, FAR)
+    gd = Gather(peers, None, wd, False, d_recv, d_sent, DOWN_REST)
+    inward = Inward(peers, cot, cot_buf, i_recv, i_sent)
+    n = wu_buf.shape[2]
+
+    def fetch(t, slot):
+        cols = pl.ds(pl.multiple_of(t * n, n), n)
+        return (
+            pltpu.make_async_copy(wu.at[:, cols], wu_buf.at[slot], buf_sem.at[0, slot]),
+            pltpu.make_async_copy(wd.at[cols, :], wd_buf.at[slot], buf_sem.at[1, slot]),
+        )
+
+    @pl.when(j == 0)
+    def _():
+        peers.greet(ALL_PEERS)
+        for t in range(2):
+            for c in fetch(t, t):
+                c.start()
+        gd.emit(3, 0)
+        for s in range(3):
+            gu.emit(s, 2 if s % 2 == 0 else 4)
+            gd.emit(s, 2 if s % 2 == 0 else 4)
+        gu.emit(3, 4)
+        inward.start()
+
+        def body(rows):
+            v = x_ref[rows, :].astype(F32) + mm(att_ref[rows, :], wo_ref[...]) + vec_ref[0:1, :]
+            normed, inv = norm_rows(v)
+            normed1_ref[rows, :] = normed
+            inv1_ref[rows, :] = jnp.broadcast_to(inv, (RB, 128))
+            hlow_ref[rows, :] = (normed * vec_ref[1:2, :] + vec_ref[2:3, :]).astype(BF)
+
+        row_blocks(body)
+        acc[...] = jnp.zeros_like(acc)
+        gd.relay((3, 2), (3, 4))
+
+    @pl.when(j == 1)
+    def _():
+        gd.arrived(3, 3)
+        for s in range(4):
+            gu.relay((s, 6))
+
+    @pl.when(j == 2)
+    def _():
+        gd.arrived(3, 5)
+
+    @pl.when(j == 4)
+    def _():
+        for s in range(4):
+            gd.relay((s, 6))
+
+    @pl.when(j == 5)
+    def _():
+        for s in range(4):
+            gu.arrived(s, 7)
+            gd.arrived(s, 7)
+
+    slot = lax.rem(j, 2)
+    for c in fetch(j, slot):
+        c.wait()
+    w_up = wu_buf.at[slot]
+    w_down = wd_buf.at[slot]
+    bias = bu_ref[...]
+    for i in range(SEQ // 256):
+        rows = slice(i * 256, (i + 1) * 256)
+        act, slope = gelu_and_slope(mm(hlow_ref[rows, :], w_up[...]) + bias)
+        act = act.astype(BF)
+        act_ref[rows, :] = act
+        slope_ref[rows, :] = slope.astype(BF)
+        acc[rows, :] += mm(act, w_down[...])
+
+    @pl.when(j < 6)
+    def _():
+        for c in fetch(j + 2, slot):
+            c.start()
+
+    @pl.when(j == 7)
+    def _():
+        inward.finish()
+        vg_ref[...] = jnp.zeros_like(vg_ref)
+
+        def body(rows):
+            hidden = normed1_ref[rows, :] * vec_ref[1:2, :] + vec_ref[2:3, :]
+            normed, inv = norm_rows(hidden + (acc[rows, :] + vec_ref[3:4, :]))
+            out_ref[rows, :] = (normed * vec_ref[4:5, :] + vec_ref[5:6, :]).astype(BF)
+            c = cot_buf[rows, :].astype(F32)
+            r2 = norm_rows_back(c * vec_ref[4:5, :], normed, inv)
+            r2_ref[rows, :] = r2
+            vg_ref[0:1, :] += jnp.sum(c * normed, axis=0, keepdims=True)
+            vg_ref[1:2, :] += jnp.sum(c, axis=0, keepdims=True)
+            vg_ref[2:3, :] += jnp.sum(r2.astype(BF).astype(F32), axis=0, keepdims=True)
+
+        row_blocks(body)
+        gu.finish()
+        gd.finish()
+
+
+ONCE = pl.Buffered(1)
+
+
+def const(*shape):
+    return pl.BlockSpec(shape, lambda j: (0,) * len(shape), pipeline_mode=ONCE)
+
+
+def ff_fwd(x, att, wo, vec, bu, cot, wu, wd):
+    width, units = wu.shape
+    n = units // 8
+    return pl.pallas_call(
+        ff_fwd_kernel,
+        grid=(8,),
+        in_specs=[
+            const(SEQ, width),
+            const(SEQ, width),
+            const(width, width),
+            const(8, width),
+            pl.BlockSpec((1, n), lambda j: (0, j)),
+            ANY,
+            ANY,
+            ANY,
+        ],
+        out_specs=[
+            ANY,
+            ANY,
+            pl.BlockSpec((SEQ, n), lambda j: (0, j)),
+            pl.BlockSpec((SEQ, n), lambda j: (0, j)),
+            const(SEQ, width),
+            const(SEQ, width),
+            const(SEQ, 128),
+            const(SEQ, width),
+            const(SEQ, width),
+            const(8, width),
+        ],
+        out_shape=[
+            jax.ShapeDtypeStruct(wu.shape, BF),
+            jax.ShapeDtypeStruct(wd.shape, BF),
+            jax.ShapeDtypeStruct((SEQ, units), BF),
+            jax.ShapeDtypeStruct((SEQ, units), BF),
+            jax.ShapeDtypeStruct((SEQ, width), BF),
+            jax.ShapeDtypeStruct((SEQ, width), F32),
+            jax.ShapeDtypeStruct((SEQ, 128), F32),
+            jax.ShapeDtypeStruct((SEQ, width), BF),
+            jax.ShapeDtypeStruct((SEQ, width), F32),
+            jax.ShapeDtypeStruct((8, width), F32),
+        ],
+        input_output_aliases={6: 0, 7: 1},
+        scratch_shapes=[
+            pltpu.VMEM((SEQ, width), F32),
+            pltpu.VMEM((2, width, n), BF),
+            pltpu.VMEM((2, n, width), BF),
+            pltpu.VMEM((SEQ, width), BF),
+            DMA((2, 2)),
+            DMA((32,)),
+            DMA((32,)),
+            DMA((32,)),
+            DMA((32,)),
+            DMA((4,)),
+            DMA((4,)),
+        ],
+        compiler_params=pltpu.CompilerParams(vmem_limit_bytes=VMEM_LIMIT, collective_id=2, has_side_effects=True),
+        name="ff_fwd",
+    )(x, att, wo, vec, bu, cot, wu, wd)
+
+
+class Outward:
+    def __init__(self, peers, rows, block, recv, sent):
+        self.peers, self.rows, self.block, self.recv, self.sent = peers, rows, block, recv, sent
+
+    def copy(self, s):
+        f = self.block.shape[1]
+        src = self.rows.at[:, pl.ds(s * f, f)]
+        dst = self.block.at[pl.ds(pl.multiple_of(self.peers.r * SEQ, SEQ), SEQ), :]
+        if s == 0:
+            return pltpu.make_async_copy(src, dst, self.sent.at[0])
+        return send(self.peers, 4 - s, src, dst, self.sent.at[s], self.recv.at[s])
+
+    def start(self):
+        for s in (2, 1, 3, 0):
+            self.copy(s).start()
+
+    def finish(self):
+        self.copy(0).wait()
+        for s in (1, 2, 3):
+            self.copy(s).wait()
+
+
+def ff_bwd_kernel(
+    r2_ref, hlow_ref, wu_ref, wd_ref, act_ref, slope_ref, normed1_ref, inv1_ref, vec_ref, out,
+    out_block, dwu_ref, dwd_ref, r1_ref, gattn_ref, vg_ref, bu_ref,
+    gfed, gp, hlow_t, o_recv, o_sent,
+):
+    j = pl.program_id(0)
+    peers = Peers()
+    outward = Outward(peers, out, out_block, o_recv, o_sent)
+
+    @pl.when(j == 0)
+    def _():
+        peers.greet((1, 2, 3))
+        outward.start()
+
+        def body(rows):
+            gfed[rows, :] = r2_ref[rows, :].astype(BF)
+
+        row_blocks(body)
+        r1_ref[...] = r2_ref[...]
+        for i in range(SEQ // 256):
+            rows = slice(i * 256, (i + 1) * 256)
+            hlow_t[:, rows] = jnp.transpose(hlow_ref[rows, :])
+
+    bsum = jnp.zeros((1, bu_ref.shape[1]), F32)
+    for i in range(SEQ // 256):
+        rows = slice(i * 256, (i + 1) * 256)
+        g = (mm_t(gfed[rows, :], wd_ref[...]) * slope_ref[rows, :].astype(F32)).astype(BF)
+        gp[rows, :] = g
+        bsum += jnp.sum(g.astype(F32), axis=0, keepdims=True)
+    bu_ref[...] = jnp.broadcast_to(bsum, bu_ref.shape)
+    dwd_ref[...] = tmm(act_ref[...], gfed[...]).astype(BF)
+    dwu_ref[...] = mm(hlow_t[...], gp[...]).astype(BF)
+    r1_ref[...] += mm_t(gp[...], wu_ref[...])
+
+    @pl.when(j == 7)
+    def _():
+        vg_ref[...] = jnp.zeros_like(vg_ref)
+
+        def body(rows):
+            gh = r1_ref[rows, :]
+            normed = normed1_ref[rows, :]
+            r1 = norm_rows_back(gh * vec_ref[1:2, :], normed, inv1_ref[rows, 0:1])
+            r1_ref[rows, :] = r1
+            low = r1.astype(BF)
+            gattn_ref[rows, :] = low
+            vg_ref[0:1, :] += jnp.sum(gh * normed, axis=0, keepdims=True)
+            vg_ref[1:2, :] += jnp.sum(gh, axis=0, keepdims=True)
+            vg_ref[2:3, :] += jnp.sum(low.astype(F32), axis=0, keepdims=True)
+
+        row_blocks(body)
+        outward.finish()
+
+
+def ff_bwd(r2, hlow, wu, wd, act, slope, normed1, inv1, vec, out):
+    width, units = wu.shape
+    n = units // 8
+    return pl.pallas_call(
+        ff_bwd_kernel,
+        grid=(8,),
+        in_specs=[
+            const(SEQ, width),
+            const(SEQ, width),
+            pl.BlockSpec((width, n), lambda j: (0, j)),
+            pl.BlockSpec((n, width), lambda j: (j, 0)),
+            pl.BlockSpec((SEQ, n), lambda j: (0, j)),
+            pl.BlockSpec((SEQ, n), lambda j: (0, j)),
+            const(SEQ, width),
+            const(SEQ, 128),
+            const(8, width),
+            ANY,
+        ],
+        out_specs=[
+            ANY,
+            pl.BlockSpec((width, n), lambda j: (0, j)),
+            pl.BlockSpec((n, width), lambda j: (j, 0)),
+            const(SEQ, width),
+            const(SEQ, width),
+            const(8, width),
+            pl.BlockSpec((8, n), lambda j: (0, j)),
+        ],
+        out_shape=[
+            jax.ShapeDtypeStruct((4 * SEQ, width // 4), BF),
+            jax.ShapeDtypeStruct((width, units), BF),
+            jax.ShapeDtypeStruct((units, width), BF),
+            jax.ShapeDtypeStruct((SEQ, width), F32),
+            jax.ShapeDtypeStruct((SEQ, width), BF),
+            jax.ShapeDtypeStruct((8, width), F32),
+            jax.ShapeDtypeStruct((8, units), F32),
+        ],
+        scratch_shapes=[
+            pltpu.VMEM((SEQ, width), BF),
+            pltpu.VMEM((SEQ, n), BF),
+            pltpu.VMEM((width, SEQ), BF),
+            DMA((4,)),
+            DMA((4,)),
+        ],
+        compiler_params=pltpu.CompilerParams(vmem_limit_bytes=VMEM_LIMIT, collective_id=3, has_side_effects=True),
+        name="ff_bwd",
+    )(r2, hlow, wu, wd, act, slope, normed1, inv1, vec, out)
 
 
 class Ring:
@@ -209,21 +761,6 @@
         return jnp.where(self.d // 2 == 1, jnp.concatenate([a[2:], a[:2]], 0), a)
 
 
-def layer_norm(residual, gain, shift):
-    mean = jnp.mean(residual, axis=1, keepdims=True)
-    variance = jnp.mean(residual * residual, axis=1, keepdims=True) - mean * mean
-    inv = lax.rsqrt(variance + NORM_EPS)
-    normed = (residual - mean) * inv
-    return normed * gain + shift, normed, inv
-
-
-def layer_norm_back(grad, normed, inv, gain):
-    g = grad * gain
-    mean_g = jnp.mean(g, axis=1, keepdims=True)
-    mean_gn = jnp.mean(g * normed, axis=1, keepdims=True)
-    return inv * (g - mean_g - normed * mean_gn), jnp.sum(grad * normed, axis=0), jnp.sum(grad, axis=0)
-
-
 def quarter(v, d, axis):
     n = v.shape[axis] // 4
     return lax.dynamic_slice_in_dim(v, d * n, n, axis)
@@ -237,13 +774,6 @@
     r, c, d = ring.r, ring.c, ring.d
     R, C = lax.axis_size("row"), lax.axis_size("col")
     feat = tokens.shape[1]
-
-    def inward(block):
-        parts = []
-        for s in range(R):
-            piece = lax.dynamic_slice_in_dim(block, ((r + s) % R) * SEQ, SEQ, 0)
-            parts.append(piece if s == 0 else ring.shift(piece, s))
-        return jnp.concatenate(parts, 1)
 
     def outward(rows):
         whole = jnp.zeros((R * SEQ, feat), rows.dtype)
@@ -264,17 +794,11 @@
     ids = jnp.where(seg == 0, -1 - jnp.arange(SEQ, dtype=jnp.int32), seg)
     seg_col, seg_row = ids[:, None], ids[None, :]
 
-    x = inward(tokens)
     qkv_piece = jnp.concatenate([quarter(w, d, 1) for w in (w_query, w_key, w_value)], 1)
-    w_qkv = jnp.concatenate(ring.gather(qkv_piece, 0), 1)
-    wo = jnp.concatenate(ring.gather(quarter(w_out, d, 0), 1), 0)
-    wu = jnp.concatenate(ring.gather(quarter(w_up, d, 1), 0), 1)
-    wd = jnp.concatenate(ring.gather(quarter(w_down, d, 0), 1), 0)
-    cot = inward(cotangent)
-
-    feat_vec = jnp.stack([b_out, norm1_gain, norm1_shift, b_down, norm2_gain, norm2_shift])
+    x, w_qkv = first(tokens, qkv_piece)
+
+    feat_vec = jnp.stack([b_out, norm1_gain, norm1_shift, b_down, norm2_gain, norm2_shift, b_out, b_out])
     feat_all = jnp.concatenate([feat_vec] + [ring.shift(feat_vec, s) for s in range(1, R)], 1).astype(F32)
-    bo, g1, s1, bd, g2, s2 = [feat_all[i] for i in range(6)]
     hq = b_query.shape[0] // 4
     unit = b_up.shape[0] // 4
     slot_vec = jnp.concatenate(
@@ -282,29 +806,19 @@
     )
     slot_vec = ring.absolute(slot_vec)
     slot_vec = jnp.concatenate([slot_vec, ring.y(slot_vec)], 0).astype(F32)
-    b_qkv = slot_vec[:, : 3 * hq].reshape(-1)
-    bu = slot_vec[:, 3 * hq :].reshape(-1)
-
-    qkv = (mm(x, w_qkv) + b_qkv).astype(BF)
-    att, prob, linv = attend_fwd(qkv, seg_col, seg_row)
-    hidden, normed1, inv1 = layer_norm(x.astype(F32) + mm(att, wo) + bo, g1, s1)
-    hidden_low = hidden.astype(BF)
-    pre = mm(hidden_low, wu) + bu
-    act = gelu_exact(pre).astype(BF)
-    fed = mm(act, wd) + bd
-    output, normed2, inv2 = layer_norm(hidden + fed, g2, s2)
-    out_block = outward(output.astype(BF))
-
-    grad_r2, d_g2, d_s2 = layer_norm_back(cot.astype(F32), normed2, inv2, g2)
-    grad_fed = grad_r2.astype(BF)
-    dwd = tmm(act, grad_fed).astype(BF)
-    grad_act = mm_t(grad_fed, wd)
-    _, slope = jax.vjp(gelu_exact, pre)
-    grad_pre = slope(grad_act)[0].astype(BF)
-    dwu = tmm(hidden_low, grad_pre).astype(BF)
-    grad_hidden = mm_t(grad_pre, wu) + grad_r2
-    grad_r1, d_g1, d_s1 = layer_norm_back(grad_hidden, normed1, inv1, g1)
-    grad_attn = grad_r1.astype(BF)
+    b_qkv = slot_vec[:, : 3 * hq].reshape(1, -1)
+    bu = slot_vec[:, 3 * hq :].reshape(1, -1)
+
+    qkv, att, prob, linv, wo, wu, wd = attend_fwd(
+        x, w_qkv, b_qkv, seg_col, seg_row, quarter(w_out, d, 0), quarter(w_up, d, 1), quarter(w_down, d, 0)
+    )
+    wu, wd, act, slope, hidden_low, normed1, inv1, output, grad_r2, vg2 = ff_fwd(
+        x, att, wo, feat_all, bu, cotangent, wu, wd
+    )
+
+    out_block, dwu, dwd, grad_r1, grad_attn, vg1, bu_part = ff_bwd(
+        grad_r2, hidden_low, wu, wd, act, slope, normed1, inv1, feat_all, output
+    )
     dwo = tmm(att, grad_attn).astype(BF)
     grad_att = mm_t(grad_attn, wo).astype(BF)
     g_qkv = attend_bwd(qkv, grad_att, att, linv, prob)
@@ -340,13 +854,11 @@
     slot_grad = jnp.concatenate(
         [
             jnp.sum(g32, axis=0).reshape(8, 3 * hq),
-            jnp.sum(grad_pre.astype(F32), axis=0).reshape(8, unit),
+            bu_part[0].reshape(8, unit),
         ],
         1,
     )
-    feat_grad = jnp.stack(
-        [jnp.sum(grad_attn.astype(F32), axis=0), d_g1, d_s1, jnp.sum(grad_fed.astype(F32), axis=0), d_g2, d_s2]
-    )
+    feat_grad = jnp.stack([vg1[2], vg1[0], vg1[1], vg2[2], vg2[0], vg2[1]])
     slot_grad = slot_grad[0::2] + ring.core(slot_grad[1::2])
     slot_grad = slot_grad[0::2] + ring.x(slot_grad[1::2])
     slot_grad = slot_grad[0] + ring.y(slot_grad[1])

time: 857 us -> 667 us (0.78)
  Pallas kernels: 77.6 us -> 304 us
  matrix products: 171 us -> 25.3 us
  waiting for transfers between devices: 271 us -> 167 us
  starting transfers between devices: 137 us -> 53.6 us
  local copies, waits for them, and re-layouts: 116 us -> 52.8 us
  other arithmetic: 72.7 us -> 50.4 us
    pallas_call x0 -> x3, Pallas kernels: none -> 192 us  [the longest x1 71.6 us: ff_fwd(): pl.pallas_call(ff_fwd_kernel, grid=(8,), in_specs=[const(SEQ, width), con...]
    dot_general x4 -> x0, matrix products: 78.4 us -> none  [mm(): return jnp.dot(a, b, preferred_element_type=F32)]
    ppermute x42 -> x21, starting transfers between devices: 81.4 us -> 15 us  [shift(): return lax.ppermute(v, 'row', [(i, (i + s) % n) for i in range(n)])]
    ppermute x42 -> x21, waiting for transfers between devices: 127 us -> 78.4 us  [shift(): return lax.ppermute(v, 'row', [(i, (i + s) % n) for i in range(n)])]
    dot_general x4 -> x2, matrix products: 52.4 us -> 12.4 us  [mm_t(): lax.dot_general(a, b, (((1,), (1,)), ((), ())), preferred_element_type=F32)]
    unnamed x178 -> x82, local copies, waits for them, and re-layouts: 49.9 us -> 13.2 us
    pallas_call x1, Pallas kernels: 39 us -> 74.1 us  [attend_fwd(): pl.pallas_call(attend_fwd_kernel, grid=(slots,), in_specs=[pl.BlockSpec((...]
    dot_general x4 -> x2, matrix products: 40.4 us -> 12.9 us  [tmm(): lax.dot_general(a, b, (((0,), (0,)), ((), ())), preferred_element_type=F32)]
  transfers between devices with their start and end apart: 126 -> 73, of which waited for: 51 -> 31; matrix products, arithmetic and copies ran while one was open for 29% -> 12% of each run, Pallas kernels for 5% -> 10%
where the time goes in v2:
time: 667 us; the launch traced here: 656 us
  Pallas kernels  304 us (46%)
  waiting for transfers between devices  167 us (25%)
  starting transfers between devices  53.6 us (8%)
  local copies, waits for them, and re-layouts  52.8 us (8%)
  other arithmetic  50.4 us (8%)
  matrix products  25.3 us (4%)
    ppermute x21, waiting for transfers between devices, shift(): return lax.ppermute(v, 'row', [(i, (i + s) % n) for i in range(n)])  78.4 us
    pallas_call x1, Pallas kernels, attend_fwd(): pl.pallas_call(attend_fwd_kernel, grid=(slots,), in_specs=[pl.BlockSpec((...  74.1 us
    pallas_call x1, Pallas kernels, ff_fwd(): pl.pallas_call(ff_fwd_kernel, grid=(8,), in_specs=[const(SEQ, width), con...  71.6 us
    pallas_call x1, Pallas kernels, first(): pl.pallas_call(first_kernel, in_specs=[ANY, ANY], out_specs=[ANY, ANY], o...  67.6 us
    ppermute x15, waiting for transfers between devices, x(): return lax.ppermute(v, 'dp', [(i, i ^ 2) for i in range(4)])  60.8 us
    pallas_call x1, Pallas kernels, ff_bwd(): pl.pallas_call(ff_bwd_kernel, grid=(8,), in_specs=[const(SEQ, width), con...  53.2 us
    pallas_call x1, Pallas kernels, attend_bwd(): pl.pallas_call(attend_bwd_kernel, grid=(slots,), in_specs=[pl.BlockSpec((...  37.8 us
    ppermute x11, waiting for transfers between devices, y(): return lax.ppermute(v, 'col', [(0, 1), (1, 0)])  22.5 us
  transfers between devices with their start and end apart: 73, of which 31 were waited for; matrix products, arithmetic and copies ran while one was open for 12% of the time, Pallas kernels for 10%

profile of v2, /device:TPU:0, one launch (start us, length us, event | category | flops | bytes accessed | tf_op | source)
XLA Modules:
  0.0 655.6 jit_solution(12339256964859066101)
XLA Ops:
  24.9 67.6 %first.1 = (bf16[1024,1024]{1,0:T(8,128)(2,1)}, bf16[1024,3072]{1,0:T(8,128)(2,1)}) custom-call(bf16[4096,256]{1,0:T(8,128)(2,1)} %tokens.1, bf16[256,384]{1,0:T(8,128)(2,1)} %pad_maximum_fusion.15.piece), custom_call_target="tpu_custom_call" | custom-call | tf_op jit(solution)/shard_map/first/pallas_call | solution.py:365
  95.5 74.1 %attend_fwd.1 = (bf16[1024,3072]{1,0:T(8,128)(2,1)}, bf16[1024,1024]{1,0:T(8,128)(2,1)}, bf16[16,1024,1024]{2,1,0:T(8,128)(2,1)}, f32[1024,1024]{1,0:T(8,128)}, ...) custom-call(bf16[1024,1024]{1,0:T(8,128)(2,1)} %get-tuple-element.43.x_ref, ...), custom_call_target="tpu_custom_call" | custom-call | flops 17179869184 | bytes 41943040 | tf_op jit(solution)/shard_map/attend_fwd/pallas_call | solution.py:148
  169.7 71.6 %ff_fwd.1 = (bf16[1024,4096]{1,0:T(8,128)(2,1)}, bf16[4096,1024]{1,0:T(8,128)(2,1)}, bf16[1024,4096]{1,0:T(8,128)(2,1)}, bf16[1024,4096]{1,0:T(8,128)(2,1)}, bf1...) custom-call(bf16[1024,1024]{1,0:T(8,128)(2,1)} %get-tuple-element.43, ...), custom_call_target="tpu_custom_call", output_to_operand_aliasing={{0}: (6, {}), {1}: (7, {})} | custom-call | tf_op jit(solution)/shard_map/ff_fwd/pallas_call | solution.py:527
  241.3 53.2 %ff_bwd.1 = (bf16[4096,256]{1,0:T(8,128)(2,1)}, bf16[1024,4096]{1,0:T(8,128)(2,1)}, bf16[4096,1024]{1,0:T(8,128)(2,1)}, f32[1024,1024]{1,0:T(8,128)}, bf16[1024,...) custom-call(f32[1024,1024]{1,0:T(8,128)} %get-tuple-element.49.r2_ref, ...), custom_call_target="tpu_custom_call" | custom-call | tf_op jit(solution)/shard_map/ff_bwd/pallas_call | solution.py:661
  294.5 4.1 convolution_convert_fusion.1
  298.7 3.7 convolution_convert_fusion.2.do_ref
  302.4 37.8 %attend_bwd.1 = bf16[1024,3072]{1,0:T(8,128)(2,1)} custom-call(bf16[1024,3072]{1,0:T(8,128)(2,1)} %get-tuple-element.59.qkv_ref, bf16[1024,1024]{1,0:T(8,128)(2,1)} %convolution_convert_fusion.2.do_ref, bf16[1024,1024]{1,0:T(8,128)(2,1)} %get-tuple-element.45.att_ref.o_ref, f32[1024,1024]{1,0:T(8,128)} %get-tuple-element.61.linv_ref, ...), custom_call_target="tpu_custom_call" | custom-call | flops 34359738368 | bytes 50331648 | tf_op jit(solution)/shard_map/attend_bwd/pallas_call | solution.py:192
  340.2 3.9 convert_reduce_fusion
  344.8 8.8 %convolution_convert_fusion = bf16[1024,3072]{1,0:T(8,128)(2,1)} fusion(bf16[1024,1024]{1,0:T(8,128)(2,1)S(1)} %copy-done.8, bf16[1024,3072]{1,0:T(8,128)(2,1)S(1)} %copy-done.2), kind=kOutput, calls=%fused_computation.7 | convolution fusion | flops 6445596672 | bytes 14680064 | tf_op jit(solution)/shard_map/dot_general | solution.py:30
  353.6 8.7 %fusion.25 = f32[1024,1024]{1,0:T(8,128)} fusion(bf16[1024,3072]{1,0:T(8,128)(2,1)S(1)} %copy-done.2, bf16[1024,3072]{1,0:T(8,128)(2,1)S(1)} %bitcast.101), kind=kOutput, calls=%fused_computation.138 | convolution fusion | flops 6442450944 | bytes 16777216 | tf_op jit(solution)/shard_map/dot_general | solution.py:26
  365.4 4.3 fusion.4
  380.3 4.4 collective-permute-start.24
  384.7 4.3 add_convert_fusion
  424.0 13.8 %collective-permute-done.45 = f32[6,256]{1,0:T(8,128)S(1)} collective-permute-done((f32[6,256]{1,0:T(8,128)S(1)}, f32[6,256]{1,0:T(8,128)S(1)}, u32[]{:S(2)}, u32[]{:S(2)}) %collective-permute-start.45) | collective-permute-done | bytes 6176 | tf_op jit(solution)/shard_map/ppermute | solution.py:715
  438.8 5.3 collective-permute-done.36
  444.8 16.9 %collective-permute-done.37 = bf16[128,256]{1,0:T(8,128)(2,1)S(1)} collective-permute-done((bf16[128,256]{1,0:T(8,128)(2,1)S(1)}, bf16[128,256]{1,0:T(8,128)(2,1)S(1)}, u32[]{:S(2)}, u32[]{:S(2)}) %collective-permute-start.37) | collective-permute-done | bytes 65568 | tf_op jit(solution)/shard_map/ppermute | solution.py:715
  463.7 5.6 collective-permute-done.38
  485.3 3.8 add_convert_fusion.9
  490.1 7.0 %collective-permute-done.40 = bf16[2,128,256]{2,1,0:T(8,128)(2,1)S(1)} collective-permute-done((bf16[2,128,256]{2,1,0:T(8,128)(2,1)S(1)}, bf16[2,128,256]{2,1,0:T(8,128)(2,1)S(1)}, u32[]{:S(2)}, u32[]{:S(2)}) %collective-permute-start.40) | collective-permute-done | bytes 131104 | tf_op jit(solution)/shard_map/ppermute | solution.py:721
  505.2 7.1 %collective-permute-done.63 = bf16[256,1024]{1,0:T(8,128)(2,1)} collective-permute-done((bf16[256,1024]{1,0:T(8,128)(2,1)}, bf16[256,1024]{1,0:T(8,128)(2,1)}, u32[]{:S(2)}, u32[]{:S(2)}) %collective-permute-start.63) | collective-permute-done | bytes 524320 | tf_op jit(solution)/shard_map/ppermute | solution.py:724
  516.8 6.7 %collective-permute-done.50 = bf16[512,512]{1,0:T(8,128)(2,1)S(1)} collective-permute-done((bf16[512,512]{1,0:T(8,128)(2,1)S(1)}, bf16[512,512]{1,0:T(8,128)(2,1)S(1)}, u32[]{:S(2)}, u32[]{:S(2)}) %collective-permute-start.50) | collective-permute-done | bytes 524320 | tf_op jit(solution)/shard_map/ppermute | solution.py:724
  525.7 7.1 %collective-permute-done.12 = bf16[1024,384]{1,0:T(8,128)(2,1)S(1)} collective-permute-done((bf16[1024,384]{1,0:T(8,128)(2,1)S(1)}, bf16[1024,384]{1,0:T(8,128)(2,1)S(1)}, u32[]{:S(2)}, u32[]{:S(2)}) %collective-permute-start.12) | collective-permute-done | bytes 786464 | tf_op jit(solution)/shard_map/ppermute | solution.py:721
  533.7 4.5 collective-permute-done.15
  544.1 9.2 %collective-permute-done.16 = bf16[256,384]{1,0:T(8,128)(2,1)S(1)} collective-permute-done((bf16[256,384]{1,0:T(8,128)(2,1)S(1)}, bf16[256,384]{1,0:T(8,128)(2,1)S(1)}, u32[]{:S(2)}, u32[]{:S(2)}) %collective-permute-start.16) | collective-permute-done | bytes 196640 | tf_op jit(solution)/shard_map/ppermute | solution.py:715
  554.4 6.5 collective-permute-done.17
  562.3 4.2 collective-permute-done.64
  569.1 17.3 %collective-permute-done.51 = bf16[1024,512]{1,0:T(8,128)(2,1)S(1)} collective-permute-done((bf16[1024,512]{1,0:T(8,128)(2,1)S(1)}, bf16[1024,512]{1,0:T(8,128)(2,1)S(1)}, u32[]{:S(2)}, u32[]{:S(2)}) %collective-permute-start.51) | collective-permute-done | bytes 1048608 | tf_op jit(solution)/shard_map/ppermute | solution.py:721
  588.6 10.5 %collective-permute-done.55 = bf16[256,512]{1,0:T(8,128)(2,1)S(1)} collective-permute-done((bf16[256,512]{1,0:T(8,128)(2,1)S(1)}, bf16[256,512]{1,0:T(8,128)(2,1)S(1)}, u32[]{:S(2)}, u32[]{:S(2)}) %collective-permute-start.55) | collective-permute-done | bytes 262176 | tf_op jit(solution)/shard_map/ppermute | solution.py:715
  600.4 4.3 collective-permute-done.69
  605.5 4.8 collective-permute-done.56
  626.6 8.3 %collective-permute-done.72 = bf16[2,512,256]{2,1,0:T(8,128)(2,1)} collective-permute-done((bf16[2,512,256]{2,1,0:T(8,128)(2,1)}, bf16[2,512,256]{2,1,0:T(8,128)(2,1)}, u32[]{:S(2)}, u32[]{:S(2)}) %collective-permute-start.72) | collective-permute-done | bytes 524320 | tf_op jit(solution)/shard_map/ppermute | solution.py:721
  639.6 5.7 collective-permute-done.59
  (355 shorter events, 158.3 us)
Async XLA Ops:
  4.7 87.8 %collective-permute-start.2 = (bf16[8,256]{1,0:T(8,128)(2,1)S(1)}, bf16[8,256]{1,0:T(8,128)(2,1)S(1)}, u32[]{:S(2)}, u32[]{:S(2)}) collective-permute-start(bf16[8,256]{1,0:T(8,128)(2,1)S(1)} %stack.78), channel_id=1, source_target_pairs={{0,2},{2,4},{4,6},{6,0},{1,3},{3,5},{5,7},{7,1},{8,10},{10,12},{12... | collective-permute-start | bytes 12296 | tf_op jit(solution)/shard_map/ppermute | solution.py:715
  7.8 84.8 %collective-permute-start.3 = (bf16[8,256]{1,0:T(8,128)(2,1)S(1)}, bf16[8,256]{1,0:T(8,128)(2,1)S(1)}, u32[]{:S(2)}, u32[]{:S(2)}) collective-permute-start(bf16[8,256]{1,0:T(8,128)(2,1)S(1)} %stack.78), channel_id=1, source_target_pairs={{0,4},{2,6},{4,0},{6,2},{1,5},{3,7},{5,1},{7,3},{8,12},{10,14},{12... | collective-permute-start | bytes 12296 | tf_op jit(solution)/shard_map/ppermute | solution.py:715
  10.4 82.2 %collective-permute-start.4 = (bf16[8,256]{1,0:T(8,128)(2,1)S(1)}, bf16[8,256]{1,0:T(8,128)(2,1)S(1)}, u32[]{:S(2)}, u32[]{:S(2)}) collective-permute-start(bf16[8,256]{1,0:T(8,128)(2,1)S(1)} %stack.78), channel_id=1, source_target_pairs={{0,6},{2,0},{4,2},{6,4},{1,7},{3,1},{5,3},{7,5},{8,14},{10,8},{12,... | collective-permute-start | bytes 12296 | tf_op jit(solution)/shard_map/ppermute | solution.py:715
  11.8 82.7 %collective-permute-start.1 = (s32[2048]{0:T(1024)}, s32[2048]{0:T(1024)S(1)}, u32[]{:S(2)}, u32[]{:S(2)}) collective-permute-start(s32[2048]{0:T(1024)} %param.25), channel_id=1, source_target_pairs={{0,0},{4,1},{1,2},{5,3},{2,4},{6,5},{3,6},{7,7},{8,8},{12,9},{9,10... | collective-permute-start | bytes 24584 | tf_op jit(solution)/shard_map/ppermute | solution.py:792
  15.8 77.4 %collective-permute-start = (bf16[4,896]{1,0:T(4,128)(2,1)S(1)}, bf16[4,896]{1,0:T(4,128)(2,1)S(1)}, u32[]{:S(2)}, u32[]{:S(2)}) collective-permute-start(bf16[4,896]{1,0:T(4,128)(2,1)S(1)} %maximum_select_fusion.5), channel_id=1, source_target_pairs={{0,1},{1,0},{2,3},{3,2},{4,5},{5,4},{6,7},{7,6},{8,9},{9,8},{10,11... | collective-permute-start | bytes 21512 | tf_op jit(solution)/shard_map/ppermute | solution.py:724
  374.0 21.5 %collective-permute-start.41 = (f32[6,1024]{1,0:T(8,128)S(1)}, f32[6,1024]{1,0:T(8,128)S(1)}, u32[]{:S(2)}, u32[]{:S(2)}) collective-permute-start(f32[6,1024]{1,0:T(8,128)S(1)} %pad_maximum_fusion.17), channel_id=1, source_target_pairs={{0,8},{8,0},{16,24},{24,16},{1,9},{9,1},{17,25},{25,17},{2,10},{10... | collective-permute-start | bytes 73736 | tf_op jit(solution)/shard_map/ppermute | solution.py:718
  378.6 23.7 %collective-permute-start.29 = (bf16[128,1024]{1,0:T(8,128)(2,1)}, bf16[128,1024]{1,0:T(8,128)(2,1)S(1)}, u32[]{:S(2)}, u32[]{:S(2)}) collective-permute-start(bf16[128,1024]{1,0:T(8,128)(2,1)} %get-tuple-element.112), channel_id=1, source_target_pairs={{0,8},{8,0},{16,24},{24,16},{1,9},{9,1},{17,25},{25,17},{2,10},{10... | collective-permute-start | bytes 786440 | tf_op jit(solution)/shard_map/ppermute | solution.py:718
  378.6 24.8 %collective-permute-start.30 = (bf16[128,1024]{1,0:T(8,128)(2,1)}, bf16[128,1024]{1,0:T(8,128)(2,1)S(1)}, u32[]{:S(2)}, u32[]{:S(2)}) collective-permute-start(bf16[128,1024]{1,0:T(8,128)(2,1)} %get-tuple-element.111), channel_id=1, source_target_pairs={{0,8},{8,0},{16,24},{24,16},{1,9},{9,1},{17,25},{25,17},{2,10},{10... | collective-permute-start | bytes 786440 | tf_op jit(solution)/shard_map/ppermute | solution.py:718
  379.1 25.0 %collective-permute-start.33 = (bf16[128,1024]{1,0:T(8,128)(2,1)S(1)}, bf16[128,1024]{1,0:T(8,128)(2,1)}, u32[]{:S(2)}, u32[]{:S(2)}) collective-permute-start(bf16[128,1024]{1,0:T(8,128)(2,1)S(1)} %get-tuple-element.110), channel_id=1, source_target_pairs={{0,8},{8,0},{16,24},{24,16},{1,9},{9,1},{17,25},{25,17},{2,10},{10... | collective-permute-start | bytes 786440 | tf_op jit(solution)/shard_map/ppermute | solution.py:718
  395.0 21.6 %collective-permute-start.28 = (bf16[128,1024]{1,0:T(8,128)(2,1)}, bf16[128,1024]{1,0:T(8,128)(2,1)S(1)}, u32[]{:S(2)}, u32[]{:S(2)}) collective-permute-start(bf16[128,1024]{1,0:T(8,128)(2,1)} %get-tuple-element.109), channel_id=1, source_target_pairs={{0,8},{8,0},{16,24},{24,16},{1,9},{9,1},{17,25},{25,17},{2,10},{10... | collective-permute-start | bytes 786440 | tf_op jit(solution)/shard_map/ppermute | solution.py:718
  399.3 44.8 %collective-permute-start.5 = (bf16[1024,256]{1,0:T(8,128)(2,1)}, bf16[1024,256]{1,0:T(8,128)(2,1)}, u32[]{:S(2)}, u32[]{:S(2)}) collective-permute-start(bf16[1024,256]{1,0:T(8,128)(2,1)} %get-tuple-element.118), channel_id=1, source_target_pairs={{0,6},{2,0},{4,2},{6,4},{1,7},{3,1},{5,3},{7,5},{8,14},{10,8},{12,... | collective-permute-start | bytes 1572872 | tf_op jit(solution)/shard_map/ppermute | solution.py:715
  416.6 27.6 %collective-permute-start.6 = (bf16[1024,256]{1,0:T(8,128)(2,1)S(1)}, bf16[1024,256]{1,0:T(8,128)(2,1)S(1)}, u32[]{:S(2)}, u32[]{:S(2)}) collective-permute-start(bf16[1024,256]{1,0:T(8,128)(2,1)S(1)} %copy-done.23), channel_id=1, source_target_pairs={{0,4},{2,6},{4,0},{6,2},{1,5},{3,7},{5,1},{7,3},{8,12},{10,14},{12... | collective-permute-start | bytes 1572872 | tf_op jit(solution)/shard_map/ppermute | solution.py:715
  418.7 19.1 %collective-permute-start.45 = (f32[6,256]{1,0:T(8,128)S(1)}, f32[6,256]{1,0:T(8,128)S(1)}, u32[]{:S(2)}, u32[]{:S(2)}) collective-permute-start(f32[6,256]{1,0:T(8,128)S(1)} %get-tuple-element.157), channel_id=1, source_target_pairs={{0,4},{2,6},{4,0},{6,2},{1,5},{3,7},{5,1},{7,3},{8,12},{10,14},{12... | collective-permute-start | bytes 18440 | tf_op jit(solution)/shard_map/ppermute | solution.py:715
  424.0 48.3 %collective-permute-start.61 = (bf16[512,1024]{1,0:T(8,128)(2,1)S(1)}, bf16[512,1024]{1,0:T(8,128)(2,1)S(1)}, u32[]{:S(2)}, u32[]{:S(2)}) collective-permute-start(bf16[512,1024]{1,0:T(8,128)(2,1)S(1)} %copy-done.18), channel_id=1, source_target_pairs={{0,8},{8,0},{16,24},{24,16},{1,9},{9,1},{17,25},{25,17},{2,10},{10... | collective-permute-start | bytes 3145736 | tf_op jit(solution)/shard_map/ppermute | solution.py:718
  437.7 25.4 %collective-permute-start.10 = (bf16[1024,384]{1,0:T(8,128)(2,1)S(1)}, bf16[1024,384]{1,0:T(8,128)(2,1)S(1)}, u32[]{:S(2)}, u32[]{:S(2)}) collective-permute-start(bf16[1024,384]{1,0:T(8,128)(2,1)S(1)} %copy-done.21), channel_id=1, source_target_pairs={{0,8},{8,0},{16,24},{24,16},{1,9},{9,1},{17,25},{25,17},{2,10},{10... | collective-permute-start | bytes 2359304 | tf_op jit(solution)/shard_map/ppermute | solution.py:718
  444.1 25.3 %collective-permute-start.13 = (bf16[1024,384]{1,0:T(8,128)(2,1)S(1)}, bf16[1024,384]{1,0:T(8,128)(2,1)S(1)}, u32[]{:S(2)}, u32[]{:S(2)}) collective-permute-start(bf16[1024,384]{1,0:T(8,128)(2,1)S(1)} %copy-done.20), channel_id=1, source_target_pairs={{0,8},{8,0},{16,24},{24,16},{1,9},{9,1},{17,25},{25,17},{2,10},{10... | collective-permute-start | bytes 2359304 | tf_op jit(solution)/shard_map/ppermute | solution.py:718
  444.1 18.7 %collective-permute-start.7 = (bf16[1024,256]{1,0:T(8,128)(2,1)S(1)}, bf16[1024,256]{1,0:T(8,128)(2,1)S(1)}, u32[]{:S(2)}, u32[]{:S(2)}) collective-permute-start(bf16[1024,256]{1,0:T(8,128)(2,1)S(1)} %copy-done.22), channel_id=1, source_target_pairs={{0,2},{2,4},{4,6},{6,0},{1,3},{3,5},{5,7},{7,1},{8,10},{10,12},{12... | collective-permute-start | bytes 1572872 | tf_op jit(solution)/shard_map/ppermute | solution.py:715
  477.1 76.5 %collective-permute-start.60 = (bf16[512,1024]{1,0:T(8,128)(2,1)}, bf16[512,1024]{1,0:T(8,128)(2,1)}, u32[]{:S(2)}, u32[]{:S(2)}) collective-permute-start(bf16[512,1024]{1,0:T(8,128)(2,1)} %get-tuple-element.88), channel_id=1, source_target_pairs={{0,8},{8,0},{16,24},{24,16},{1,9},{9,1},{17,25},{25,17},{2,10},{10... | collective-permute-start | bytes 3145736 | tf_op jit(solution)/shard_map/ppermute | solution.py:718
  477.3 47.4 %collective-permute-start.8 = (bf16[1024,384]{1,0:T(8,128)(2,1)}, bf16[1024,384]{1,0:T(8,128)(2,1)}, u32[]{:S(2)}, u32[]{:S(2)}) collective-permute-start(bf16[1024,384]{1,0:T(8,128)(2,1)} %get-tuple-element.102), channel_id=1, source_target_pairs={{0,8},{8,0},{16,24},{24,16},{1,9},{9,1},{17,25},{25,17},{2,10},{10... | collective-permute-start | bytes 2359304 | tf_op jit(solution)/shard_map/ppermute | solution.py:718
  483.2 19.7 %collective-permute-start.14 = (bf16[512,384]{1,0:T(8,128)(2,1)}, bf16[512,384]{1,0:T(8,128)(2,1)}, u32[]{:S(2)}, u32[]{:S(2)}) collective-permute-start(bf16[512,384]{1,0:T(8,128)(2,1)} %get-tuple-element.144), channel_id=1, source_target_pairs={{0,16},{8,24},{16,0},{24,8},{1,17},{9,25},{17,1},{25,9},{2,18},{10... | collective-permute-start | bytes 1179656 | tf_op jit(solution)/shard_map/ppermute | solution.py:721
  502.9 20.5 %collective-permute-start.50 = (bf16[512,512]{1,0:T(8,128)(2,1)S(1)}, bf16[512,512]{1,0:T(8,128)(2,1)S(1)}, u32[]{:S(2)}, u32[]{:S(2)}) collective-permute-start(bf16[512,512]{1,0:T(8,128)(2,1)S(1)} %copy-done.25), channel_id=1, source_target_pairs={{0,1},{1,0},{2,3},{3,2},{4,5},{5,4},{6,7},{7,6},{8,9},{9,8},{10,11... | collective-permute-start | bytes 1572872 | tf_op jit(solution)/shard_map/ppermute | solution.py:724
  512.3 20.5 %collective-permute-start.12 = (bf16[1024,384]{1,0:T(8,128)(2,1)S(1)}, bf16[1024,384]{1,0:T(8,128)(2,1)S(1)}, u32[]{:S(2)}, u32[]{:S(2)}) collective-permute-start(bf16[1024,384]{1,0:T(8,128)(2,1)S(1)} %pad_maximum_fusion.6), channel_id=1, source_target_pairs={{0,16},{8,24},{16,0},{24,8},{1,17},{9,25},{17,1},{25,9},{2,18},{10... | collective-permute-start | bytes 2359304 | tf_op jit(solution)/shard_map/ppermute | solution.py:721
  515.6 22.7 %collective-permute-start.15 = (bf16[1024,384]{1,0:T(8,128)(2,1)S(1)}, bf16[1024,384]{1,0:T(8,128)(2,1)S(1)}, u32[]{:S(2)}, u32[]{:S(2)}) collective-permute-start(bf16[1024,384]{1,0:T(8,128)(2,1)S(1)} %pad_maximum_fusion.7), channel_id=1, source_target_pairs={{0,1},{1,0},{2,3},{3,2},{4,5},{5,4},{6,7},{7,6},{8,9},{9,8},{10,11... | collective-permute-start | bytes 2359304 | tf_op jit(solution)/shard_map/ppermute | solution.py:724
  523.4 20.6 %collective-permute-start.53 = (bf16[512,512]{1,0:T(8,128)(2,1)S(1)}, bf16[512,512]{1,0:T(8,128)(2,1)S(1)}, u32[]{:S(2)}, u32[]{:S(2)}) collective-permute-start(bf16[512,512]{1,0:T(8,128)(2,1)S(1)} %copy-done.24), channel_id=1, source_target_pairs={{0,16},{8,24},{16,0},{24,8},{1,17},{9,25},{17,1},{25,9},{2,18},{10... | collective-permute-start | bytes 1572872 | tf_op jit(solution)/shard_map/ppermute | solution.py:721
  525.7 43.4 %collective-permute-start.47 = (bf16[1024,512]{1,0:T(8,128)(2,1)S(1)}, bf16[1024,512]{1,0:T(8,128)(2,1)S(1)}, u32[]{:S(2)}, u32[]{:S(2)}) collective-permute-start(bf16[1024,512]{1,0:T(8,128)(2,1)S(1)} %copy-done.12), channel_id=1, source_target_pairs={{0,8},{8,0},{16,24},{24,16},{1,9},{9,1},{17,25},{25,17},{2,10},{10... | collective-permute-start | bytes 3145736 | tf_op jit(solution)/shard_map/ppermute | solution.py:718
  532.8 33.7 %collective-permute-start.64 = (bf16[512,1024]{1,0:T(8,128)(2,1)S(1)}, bf16[512,1024]{1,0:T(8,128)(2,1)S(1)}, u32[]{:S(2)}, u32[]{:S(2)}) collective-permute-start(bf16[512,1024]{1,0:T(8,128)(2,1)S(1)} %pad_maximum_fusion.3), channel_id=1, source_target_pairs={{0,16},{8,24},{16,0},{24,8},{1,17},{9,25},{17,1},{25,9},{2,18},{10... | collective-permute-start | bytes 3145736 | tf_op jit(solution)/shard_map/ppermute | solution.py:721
  538.2 28.3 %collective-permute-start.67 = (bf16[512,1024]{1,0:T(8,128)(2,1)S(1)}, bf16[512,1024]{1,0:T(8,128)(2,1)S(1)}, u32[]{:S(2)}, u32[]{:S(2)}) collective-permute-start(bf16[512,1024]{1,0:T(8,128)(2,1)S(1)} %pad_maximum_fusion.4), channel_id=1, source_target_pairs={{0,1},{1,0},{2,3},{3,2},{4,5},{5,4},{6,7},{7,6},{8,9},{9,8},{10,11... | collective-permute-start | bytes 3145736 | tf_op jit(solution)/shard_map/ppermute | solution.py:724
  553.6 32.8 %collective-permute-start.51 = (bf16[1024,512]{1,0:T(8,128)(2,1)S(1)}, bf16[1024,512]{1,0:T(8,128)(2,1)S(1)}, u32[]{:S(2)}, u32[]{:S(2)}) collective-permute-start(bf16[1024,512]{1,0:T(8,128)(2,1)S(1)} %pad_maximum_fusion), channel_id=1, source_target_pairs={{0,16},{8,24},{16,0},{24,8},{1,17},{9,25},{17,1},{25,9},{2,18},{10... | collective-permute-start | bytes 3145736 | tf_op jit(solution)/shard_map/ppermute | solution.py:721
  560.9 25.5 %collective-permute-start.54 = (bf16[1024,512]{1,0:T(8,128)(2,1)S(1)}, bf16[1024,512]{1,0:T(8,128)(2,1)S(1)}, u32[]{:S(2)}, u32[]{:S(2)}) collective-permute-start(bf16[1024,512]{1,0:T(8,128)(2,1)S(1)} %pad_maximum_fusion.1), channel_id=1, source_target_pairs={{0,1},{1,0},{2,3},{3,2},{4,5},{5,4},{6,7},{7,6},{8,9},{9,8},{10,11... | collective-permute-start | bytes 3145736 | tf_op jit(solution)/shard_map/ppermute | solution.py:724
  566.5 21.8 %collective-permute-start.18 = (bf16[256,384]{1,0:T(8,128)(2,1)S(1)}, bf16[256,384]{1,0:T(8,128)(2,1)S(1)}, u32[]{:S(2)}, u32[]{:S(2)}) collective-permute-start(bf16[256,384]{1,0:T(8,128)(2,1)S(1)} %add_convert_fusion.28), channel_id=1, source_target_pairs={{0,2},{2,4},{4,6},{6,0},{1,3},{3,5},{5,7},{7,1},{8,10},{10,12},{12... | collective-permute-start | bytes 589832 | tf_op jit(solution)/shard_map/ppermute | solution.py:715
  569.0 19.4 %collective-permute-start.68 = (bf16[512,256]{1,0:T(8,128)(2,1)S(1)}, bf16[512,256]{1,0:T(8,128)(2,1)S(1)}, u32[]{:S(2)}, u32[]{:S(2)}) collective-permute-start(bf16[512,256]{1,0:T(8,128)(2,1)S(1)} %slice.568), channel_id=1, source_target_pairs={{0,2},{2,4},{4,6},{6,0},{1,3},{3,5},{5,7},{7,1},{8,10},{10,12},{12... | collective-permute-start | bytes 786440 | tf_op jit(solution)/shard_map/ppermute | solution.py:715
  625.6 19.7 %collective-permute-start.59 = (bf16[2,256,512]{2,1,0:T(8,128)(2,1)}, bf16[2,256,512]{2,1,0:T(8,128)(2,1)}, u32[]{:S(2)}, u32[]{:S(2)}) collective-permute-start(bf16[2,256,512]{2,1,0:T(8,128)(2,1)} %pad_maximum_fusion.9), channel_id=1, source_target_pairs={{0,16},{8,24},{16,0},{24,8},{1,17},{9,25},{17,1},{25,9},{2,18},{10... | collective-permute-start | bytes 1572872 | tf_op jit(solution)/shard_map/ppermute | solution.py:721
  (77 other events, 1136.0 us)

commit v3 on v2

--- a/solution.py
+++ b/solution.py
@@ -106,38 +106,6 @@
             g.finish()
 
 
-def attend_bwd_kernel(qkv_ref, do_ref, o_ref, linv_ref, p_ref, g_ref, ds_ref):
-    lane = lax.broadcasted_iota(jnp.int32, (SEQ, 128), 1)
-    q = qkv_ref[:, 0:128]
-    k = qkv_ref[:, 128:256]
-    v = qkv_ref[:, 256:384]
-    scale = HD ** (-0.5)
-    do = do_ref[...].astype(F32) * linv_ref[...]
-    prod = do * o_ref[...].astype(F32)
-    dob = do.astype(BF)
-    qt = jnp.transpose(q.astype(F32)).astype(BF)
-    dot_ = jnp.transpose(do).astype(BF)
-    dq = []
-    dkt = []
-    dvt = []
-    for h in range(2):
-        mine = (lane < HD) if h == 0 else (lane >= HD)
-        delta = jnp.sum(jnp.where(mine, prod, 0.0), axis=1, keepdims=True)
-        dom = jnp.where(mine, dob, jnp.zeros_like(dob))
-        for i in range(SEQ // QB):
-            rows = slice(i * QB, (i + 1) * QB)
-            dp = mm_t(dom[rows], v)
-            ds = p_ref[h, rows, :].astype(F32) * (dp - delta[rows])
-            ds_ref[h, rows, :] = ds.astype(BF)
-        feats = slice(h * HD, (h + 1) * HD)
-        dq.append(mm(ds_ref[h], k))
-        dkt.append(mm(qt[feats], ds_ref[h]))
-        dvt.append(mm(dot_[feats], p_ref[h]))
-    g_ref[:, 0:128] = (jnp.where(lane < HD, dq[0], dq[1]) * scale).astype(BF)
-    g_ref[:, 128:256] = (jnp.transpose(jnp.concatenate(dkt, 0)) * scale).astype(BF)
-    g_ref[:, 256:384] = jnp.transpose(jnp.concatenate(dvt, 0)).astype(BF)
-
-
 VMEM_LIMIT = 56 * 1024 * 1024
 
 
@@ -187,31 +155,6 @@
     )(x, w_qkv, b_qkv, seg_col, seg_row, po, pu, pd)
 
 
-def attend_bwd(qkv, do, o, linv, p):
-    slots = qkv.shape[1] // 384
-    return pl.pallas_call(
-        attend_bwd_kernel,
-        grid=(slots,),
-        in_specs=[
-            pl.BlockSpec((SEQ, 384), lambda j: (0, j)),
-            pl.BlockSpec((SEQ, 128), lambda j: (0, j)),
-            pl.BlockSpec((SEQ, 128), lambda j: (0, j)),
-            pl.BlockSpec((SEQ, 128), lambda j: (0, j)),
-            pl.BlockSpec((2, SEQ, SEQ), lambda j: (j, 0, 0)),
-        ],
-        out_specs=pl.BlockSpec((SEQ, 384), lambda j: (0, j)),
-        out_shape=jax.ShapeDtypeStruct((SEQ, slots * 384), BF),
-        scratch_shapes=[pltpu.VMEM((2, SEQ, SEQ), BF)],
-        compiler_params=pltpu.CompilerParams(vmem_limit_bytes=VMEM_LIMIT),
-        cost_estimate=pl.CostEstimate(
-            flops=slots * 2 * 8 * SEQ * SEQ * 256,
-            bytes_accessed=slots * 6 * SEQ * SEQ,
-            transcendentals=0,
-        ),
-        name="attend_bwd",
-    )(qkv, do, o, linv, p)
-
-
 MESH = pl.DeviceIdType.MESH
 ANY = pl.BlockSpec(memory_space=pl.ANY)
 DMA = pltpu.SemaphoreType.DMA
@@ -580,61 +523,291 @@
     )(x, att, wo, vec, bu, cot, wu, wd)
 
 
+ORDER = (7, 6, 1, 3, 5, 0, 2, 4)
+
+
+def slot_at(j):
+    return jnp.where(j < 2, 7 - j, jnp.where(j < 5, 2 * j - 3, 2 * j - 10))
+
+
+def sum_rows(dst, *srcs):
+    n = dst.shape[0]
+    step = min(n, 64)
+
+    def run(i, carry):
+        rows = pl.ds(pl.multiple_of(i * step, step), step)
+        total = srcs[0][rows, :].astype(F32)
+        for src in srcs[1:]:
+            total += src[rows, :].astype(F32)
+        dst[rows, :] = total.astype(BF)
+        return carry
+
+    lax.fori_loop(0, n // step, run, 0)
+
+
+class Fold:
+    SCRATCH = 12
+
+    @staticmethod
+    def scratch(a, b):
+        return [
+            pltpu.VMEM((2, a, b), BF),
+            pltpu.VMEM((4, a, b), BF),
+            pltpu.VMEM((a, b), BF),
+            pltpu.VMEM((2, a // 2, b), BF),
+            DMA((12,)),
+        ]
+
+    def __init__(self, peers, stage, land, corner, land_corner, sems):
+        self.peers, self.stage, self.land, self.corner, self.land_corner, self.sems = (
+            peers, stage, land, corner, land_corner, sems,
+        )
+        self.half = corner.shape[0] // 2
+
+    def to_core(self, p):
+        k = (ORDER[p] - 1) // 2
+        return send(self.peers, "core", self.stage.at[p % 2], self.land.at[k], self.sems.at[4 + k], self.sems.at[k])
+
+    def to_side(self, h):
+        src = self.corner.at[pl.ds(h * self.half, self.half), :]
+        return send(self.peers, "xy"[1 - h], src, self.land_corner.at[h], self.sems.at[10 + h], self.sems.at[8 + h])
+
+    def before(self, j):
+        for p in (2, 4, 5, 6):
+            @pl.when(j == p)
+            def _(p=p):
+                self.to_core(p - 2).wait_send()
+
+    def from_core(self, t):
+        k = t // 2
+        self.to_core(ORDER.index(t + 1)).wait_recv()
+        return self.land.at[k]
+
+    def after(self, j, out):
+        for p, t in enumerate(ORDER):
+            @pl.when(j == p)
+            def _(p=p, t=t):
+                mine = self.stage.at[p % 2]
+                if t % 2 == 1:
+                    self.to_core(p).start()
+                    return
+                theirs = self.from_core(t)
+                if t == 6:
+                    sum_rows(self.corner, mine, theirs)
+                    self.to_side(0).start()
+                    self.to_side(1).start()
+                    return
+                if t == 0:
+                    sum_rows(out, mine, theirs)
+                    return
+                h = t // 2 - 1
+                self.to_side(h).wait_recv()
+                for q in range(2):
+                    rows = pl.ds(q * self.half, self.half)
+                    more = (self.land_corner.at[h],) if q == h else ()
+                    sum_rows(out.at[rows, :], mine.at[rows, :], theirs.at[rows, :], *more)
+
+    def finish(self):
+        self.to_side(0).wait_send()
+        self.to_side(1).wait_send()
+
+
+class Cross:
+    def __init__(self, peers, kept, own, land_x, land_y, sems):
+        self.peers, self.kept, self.own, self.land_x, self.land_y, self.sems = peers, kept, own, land_x, land_y, sems
+
+    def copies(self):
+        s = self.sems
+        return (
+            send(self.peers, "x", self.kept.at[1], self.land_x, s.at[0], s.at[1]),
+            send(self.peers, "y", self.kept.at[2], self.land_y, s.at[2], s.at[3]),
+            pltpu.make_async_copy(self.kept.at[0], self.own, s.at[4]),
+        )
+
+    def start(self):
+        for c in self.copies():
+            c.start()
+
+    def finish(self, out):
+        for c in self.copies():
+            c.wait()
+        sum_rows(out, self.own, self.land_x, self.land_y)
+
+
+class Deal:
+    def __init__(self, peers, total, by_rows, land, sems):
+        self.peers, self.total, self.by_rows, self.land, self.sems = peers, total, by_rows, land, sems
+
+    def part(self, s):
+        n = self.total.shape[0 if self.by_rows else 1] // 4
+        return self.total.at[pl.ds(s * n, n), :] if self.by_rows else self.total.at[:, pl.ds(s * n, n)]
+
+    def copy(self, s):
+        return send(self.peers, 4 - s, self.part(s), self.land.at[s - 1], self.sems.at[2 + s], self.sems.at[s - 1])
+
+    def start(self):
+        for s in (2, 1, 3):
+            self.copy(s).start()
+
+    def finish(self, out):
+        for s in (1, 2, 3):
+            self.copy(s).wait()
+        sum_rows(out, self.part(0), self.land.at[0], self.land.at[1], self.land.at[2])
+
+
+class Spread:
+    def __init__(self, peers, own, place, sems):
+        d = lax.axis_index("dp")
+        self.peers, self.own, self.sems, self.here = peers, own, sems, place(d)
+        self.from_x = place(lax.rem(d + 2, 4))
+
+    def local(self):
+        return pltpu.make_async_copy(self.own, self.here, self.sems.at[6])
+
+    def copies(self):
+        s = self.sems
+        return (
+            send(self.peers, "x", self.own, self.here, s.at[0], s.at[1]),
+            send(self.peers, "core", self.own, self.here, s.at[2], s.at[3]),
+            send(self.peers, "core", self.from_x, self.from_x, s.at[4], s.at[5]),
+        )
+
+    def start(self):
+        to_x, to_core, _ = self.copies()
+        to_x.start()
+        to_core.start()
+        self.local().start()
+
+    def relay(self):
+        to_x, _, on = self.copies()
+        to_x.wait_recv()
+        on.start()
+
+    def finish(self):
+        to_x, to_core, on = self.copies()
+        to_x.wait_send()
+        to_core.wait()
+        on.wait()
+        self.local().wait()
+
+
 class Outward:
-    def __init__(self, peers, rows, block, recv, sent):
-        self.peers, self.rows, self.block, self.recv, self.sent = peers, rows, block, recv, sent
+    def __init__(self, peers, rows, block, sems, parts=(2, 1, 3, 0)):
+        self.peers, self.rows, self.block, self.sems, self.parts = peers, rows, block, sems, parts
 
     def copy(self, s):
         f = self.block.shape[1]
         src = self.rows.at[:, pl.ds(s * f, f)]
         dst = self.block.at[pl.ds(pl.multiple_of(self.peers.r * SEQ, SEQ), SEQ), :]
         if s == 0:
-            return pltpu.make_async_copy(src, dst, self.sent.at[0])
-        return send(self.peers, 4 - s, src, dst, self.sent.at[s], self.recv.at[s])
+            return pltpu.make_async_copy(src, dst, self.sems.at[0])
+        return send(self.peers, 4 - s, src, dst, self.sems.at[s], self.sems.at[4 + s])
 
     def start(self):
-        for s in (2, 1, 3, 0):
+        for s in self.parts:
             self.copy(s).start()
 
     def finish(self):
-        self.copy(0).wait()
-        for s in (1, 2, 3):
+        for s in self.parts:
             self.copy(s).wait()
 
 
-def ff_bwd_kernel(
-    r2_ref, hlow_ref, wu_ref, wd_ref, act_ref, slope_ref, normed1_ref, inv1_ref, vec_ref, out,
-    out_block, dwu_ref, dwd_ref, r1_ref, gattn_ref, vg_ref, bu_ref,
-    gfed, gp, hlow_t, o_recv, o_sent,
+def ff_down_bwd_kernel(
+    r2_ref, wd_ref, act_ref, slope_ref, out, out_block, gp_ref, bu_ref, kept_ref,
+    gfed, stage, land, corner, land_corner, f_sems, o_sems,
 ):
     j = pl.program_id(0)
     peers = Peers()
-    outward = Outward(peers, out, out_block, o_recv, o_sent)
+    outward = Outward(peers, out, out_block, o_sems, (2, 0))
+    fold = Fold(peers, stage, land, corner, land_corner, f_sems)
 
     @pl.when(j == 0)
     def _():
-        peers.greet((1, 2, 3))
+        peers.greet(ALL_PEERS)
         outward.start()
 
         def body(rows):
             gfed[rows, :] = r2_ref[rows, :].astype(BF)
 
         row_blocks(body)
+
+    bsum = jnp.zeros((1, bu_ref.shape[1]), F32)
+    for i in range(SEQ // 256):
+        rows = slice(i * 256, (i + 1) * 256)
+        g = (mm_t(gfed[rows, :], wd_ref[...]) * slope_ref[rows, :].astype(F32)).astype(BF)
+        gp_ref[rows, :] = g
+        bsum += jnp.sum(g.astype(F32), axis=0, keepdims=True)
+    bu_ref[...] = jnp.broadcast_to(bsum, bu_ref.shape)
+    fold.before(j)
+    stage[lax.rem(j, 2)] = tmm(act_ref[...], gfed[...]).astype(BF)
+    fold.after(j, kept_ref.at[0])
+
+    @pl.when(j == 7)
+    def _():
+        fold.finish()
+        outward.finish()
+
+
+def kept_spec(a, b):
+    return pl.BlockSpec((1, a, b), lambda j: (jnp.maximum(j - 5, 0), 0, 0))
+
+
+def ff_down_bwd(r2, wd, act, slope, out):
+    units, width = wd.shape
+    n = units // 8
+    return pl.pallas_call(
+        ff_down_bwd_kernel,
+        grid=(8,),
+        in_specs=[
+            const(SEQ, width),
+            pl.BlockSpec((n, width), lambda j: (slot_at(j), 0)),
+            pl.BlockSpec((SEQ, n), lambda j: (0, slot_at(j))),
+            pl.BlockSpec((SEQ, n), lambda j: (0, slot_at(j))),
+            ANY,
+        ],
+        out_specs=[
+            ANY,
+            pl.BlockSpec((SEQ, n), lambda j: (0, slot_at(j))),
+            pl.BlockSpec((8, n), lambda j: (0, slot_at(j))),
+            kept_spec(n, width),
+        ],
+        out_shape=[
+            jax.ShapeDtypeStruct((4 * SEQ, width // 4), BF),
+            jax.ShapeDtypeStruct((SEQ, units), BF),
+            jax.ShapeDtypeStruct((8, units), F32),
+            jax.ShapeDtypeStruct((3, n, width), BF),
+        ],
+        scratch_shapes=[pltpu.VMEM((SEQ, width), BF), *Fold.scratch(n, width), DMA((8,))],
+        compiler_params=pltpu.CompilerParams(vmem_limit_bytes=VMEM_LIMIT, collective_id=3, has_side_effects=True),
+        name="ff_down_bwd",
+    )(r2, wd, act, slope, out)
+
+
+def ff_up_bwd_kernel(
+    r2_ref, hlow_ref, gp_ref, wu_ref, normed1_ref, inv1_ref, vec_ref, out, out_block_in, kept_d,
+    out_block, r1_ref, gattn_ref, vg_ref, kept_ref, own_ref,
+    hlow_t, stage, land, corner, land_corner, f_sems, own_d, land_x, land_y, c_sems, o_sems,
+):
+    j = pl.program_id(0)
+    peers = Peers()
+    outward = Outward(peers, out, out_block, o_sems, (1, 3))
+    fold = Fold(peers, stage, land, corner, land_corner, f_sems)
+    cross = Cross(peers, kept_d, own_d, land_x, land_y, c_sems)
+
+    @pl.when(j == 0)
+    def _():
+        peers.greet(ALL_PEERS)
+        cross.start()
+        outward.start()
         r1_ref[...] = r2_ref[...]
         for i in range(SEQ // 256):
             rows = slice(i * 256, (i + 1) * 256)
             hlow_t[:, rows] = jnp.transpose(hlow_ref[rows, :])
 
-    bsum = jnp.zeros((1, bu_ref.shape[1]), F32)
-    for i in range(SEQ // 256):
-        rows = slice(i * 256, (i + 1) * 256)
-        g = (mm_t(gfed[rows, :], wd_ref[...]) * slope_ref[rows, :].astype(F32)).astype(BF)
-        gp[rows, :] = g
-        bsum += jnp.sum(g.astype(F32), axis=0, keepdims=True)
-    bu_ref[...] = jnp.broadcast_to(bsum, bu_ref.shape)
-    dwd_ref[...] = tmm(act_ref[...], gfed[...]).astype(BF)
-    dwu_ref[...] = mm(hlow_t[...], gp[...]).astype(BF)
-    r1_ref[...] += mm_t(gp[...], wu_ref[...])
+    fold.before(j)
+    stage[lax.rem(j, 2)] = mm(hlow_t[...], gp_ref[...]).astype(BF)
+    fold.after(j, kept_ref.at[0])
+    r1_ref[...] += mm_t(gp_ref[...], wu_ref[...])
 
     @pl.when(j == 7)
     def _():
@@ -652,55 +825,336 @@
             vg_ref[2:3, :] += jnp.sum(low.astype(F32), axis=0, keepdims=True)
 
         row_blocks(body)
+        cross.finish(own_ref)
+        fold.finish()
         outward.finish()
 
 
-def ff_bwd(r2, hlow, wu, wd, act, slope, normed1, inv1, vec, out):
+def ff_up_bwd(r2, hlow, gp, wu, normed1, inv1, vec, out, out_block, kept_d):
     width, units = wu.shape
     n = units // 8
     return pl.pallas_call(
-        ff_bwd_kernel,
+        ff_up_bwd_kernel,
         grid=(8,),
         in_specs=[
             const(SEQ, width),
             const(SEQ, width),
-            pl.BlockSpec((width, n), lambda j: (0, j)),
-            pl.BlockSpec((n, width), lambda j: (j, 0)),
-            pl.BlockSpec((SEQ, n), lambda j: (0, j)),
-            pl.BlockSpec((SEQ, n), lambda j: (0, j)),
+            pl.BlockSpec((SEQ, n), lambda j: (0, slot_at(j))),
+            pl.BlockSpec((width, n), lambda j: (0, slot_at(j))),
             const(SEQ, width),
             const(SEQ, 128),
             const(8, width),
             ANY,
+            ANY,
+            ANY,
         ],
         out_specs=[
             ANY,
-            pl.BlockSpec((width, n), lambda j: (0, j)),
-            pl.BlockSpec((n, width), lambda j: (j, 0)),
             const(SEQ, width),
             const(SEQ, width),
             const(8, width),
-            pl.BlockSpec((8, n), lambda j: (0, j)),
+            kept_spec(width, n),
+            const(n, width),
         ],
         out_shape=[
-            jax.ShapeDtypeStruct((4 * SEQ, width // 4), BF),
-            jax.ShapeDtypeStruct((width, units), BF),
-            jax.ShapeDtypeStruct((units, width), BF),
+            jax.ShapeDtypeStruct(out_block.shape, BF),
             jax.ShapeDtypeStruct((SEQ, width), F32),
             jax.ShapeDtypeStruct((SEQ, width), BF),
             jax.ShapeDtypeStruct((8, width), F32),
-            jax.ShapeDtypeStruct((8, units), F32),
-        ],
+            jax.ShapeDtypeStruct((3, width, n), BF),
+            jax.ShapeDtypeStruct((n, width), BF),
+        ],
+        input_output_aliases={8: 0},
         scratch_shapes=[
-            pltpu.VMEM((SEQ, width), BF),
-            pltpu.VMEM((SEQ, n), BF),
             pltpu.VMEM((width, SEQ), BF),
-            DMA((4,)),
-            DMA((4,)),
-        ],
-        compiler_params=pltpu.CompilerParams(vmem_limit_bytes=VMEM_LIMIT, collective_id=3, has_side_effects=True),
-        name="ff_bwd",
-    )(r2, hlow, wu, wd, act, slope, normed1, inv1, vec, out)
+            *Fold.scratch(width, n),
+            pltpu.VMEM((n, width), BF),
+            pltpu.VMEM((n, width), BF),
+            pltpu.VMEM((n, width), BF),
+            DMA((5,)),
+            DMA((8,)),
+        ],
+        compiler_params=pltpu.CompilerParams(vmem_limit_bytes=VMEM_LIMIT, collective_id=4, has_side_effects=True),
+        name="ff_up_bwd",
+    )(r2, hlow, gp, wu, normed1, inv1, vec, out, out_block, kept_d)
+
+
+def attend_bwd_kernel(
+    gattn_ref, wo_ref, att_ref, qkv_ref, linv_ref, p_ref, x_ref, w_ref, r1, tot_d, kept_u,
+    xg_ref, gsum_ref, kept_q, kept_o, down_ref, up_ref,
+    x_t, acc, ds_ref, g_ref, a_sem,
+    q_stage, q_land, q_corner, q_land_corner, q_sems, o_stage, o_land, o_corner, o_land_corner, o_sems,
+    zd_land, zd_sems, own_u, land_x, land_y, c_sems, tot_u, zu_land, zu_sems,
+):
+    j = pl.program_id(0)
+    peers = Peers()
+    fold_q = Fold(peers, q_stage, q_land, q_corner, q_land_corner, q_sems)
+    fold_o = Fold(peers, o_stage, o_land, o_corner, o_land_corner, o_sems)
+    deal_d = Deal(peers, tot_d, False, zd_land, zd_sems)
+    cross_u = Cross(peers, kept_u, own_u, land_x, land_y, c_sems)
+    deal_u = Deal(peers, tot_u, True, zu_land, zu_sems)
+    load = pltpu.make_async_copy(r1, acc, a_sem)
+
+    @pl.when(j == 0)
+    def _():
+        peers.greet(ALL_PEERS)
+        load.start()
+        cross_u.start()
+        deal_d.start()
+        for i in range(SEQ // 256):
+            rows = slice(i * 256, (i + 1) * 256)
+            x_t[:, rows] = jnp.transpose(x_ref[rows, :])
+        load.wait()
+
+    @pl.when(j == 4)
+    def _():
+        cross_u.finish(tot_u)
+        deal_u.start()
+        deal_d.finish(down_ref)
+
+    lane = lax.broadcasted_iota(jnp.int32, (SEQ, 128), 1)
+    scale = HD ** (-0.5)
+    fold_o.before(j)
+    fold_q.before(j)
+    o_stage[lax.rem(j, 2)] = tmm(att_ref[...], gattn_ref[...]).astype(BF)
+    fold_o.after(j, kept_o.at[0])
+    q = qkv_ref[:, 0:128]
+    k = qkv_ref[:, 128:256]
+    v = qkv_ref[:, 256:384]
+    do = mm_t(gattn_ref[...], wo_ref[...]).astype(BF).astype(F32) * linv_ref[...]
+    prod = do * att_ref[...].astype(F32)
+    dob = do.astype(BF)
+    q_t = jnp.transpose(q)
+    do_t = jnp.transpose(dob)
+    dq, dk_t, dv_t = [], [], []
+    for h in range(2):
+        mine = (lane < HD) if h == 0 else (lane >= HD)
+        delta = jnp.sum(jnp.where(mine, prod, 0.0), axis=1, keepdims=True)
+        dom = jnp.where(mine, dob, jnp.zeros_like(dob))
+        for i in range(SEQ // QB):
+            rows = slice(i * QB, (i + 1) * QB)
+            dp = mm_t(dom[rows], v)
+            ds_ref[h, rows, :] = (p_ref[h, rows, :].astype(F32) * (dp - delta[rows])).astype(BF)
+        feats = slice(h * HD, (h + 1) * HD)
+        dq.append(mm(ds_ref[h], k))
+        dk_t.append(mm(q_t[feats], ds_ref[h]))
+        dv_t.append(mm(do_t[feats], p_ref[h]))
+    g_ref[:, 0:128] = (jnp.where(lane < HD, dq[0], dq[1]) * scale).astype(BF)
+    g_ref[:, 128:256] = (jnp.transpose(jnp.concatenate(dk_t, 0)) * scale).astype(BF)
+    g_ref[:, 256:384] = jnp.transpose(jnp.concatenate(dv_t, 0)).astype(BF)
+    gsum_ref[...] = jnp.broadcast_to(jnp.sum(g_ref[...].astype(F32), axis=0, keepdims=True), gsum_ref.shape)
+    q_stage[lax.rem(j, 2)] = mm(x_t[...], g_ref[...]).astype(BF)
+    fold_q.after(j, kept_q.at[0])
+    acc[...] += mm_t(g_ref[...], w_ref[...])
+
+    @pl.when(j == 7)
+    def _():
+        def body(rows):
+            xg_ref[rows, :] = acc[rows, :].astype(BF)
+
+        row_blocks(body)
+        deal_u.finish(up_ref)
+        fold_o.finish()
+        fold_q.finish()
+
+
+def attend_bwd(gattn, wo, att, qkv, linv, p, x, w_qkv, r1, tot_d, kept_u):
+    width = x.shape[1]
+    heads = 128
+    n = tot_d.shape[0]
+    return pl.pallas_call(
+        attend_bwd_kernel,
+        grid=(8,),
+        in_specs=[
+            const(SEQ, width),
+            pl.BlockSpec((heads, width), lambda j: (slot_at(j), 0)),
+            pl.BlockSpec((SEQ, heads), lambda j: (0, slot_at(j))),
+            pl.BlockSpec((SEQ, 3 * heads), lambda j: (0, slot_at(j))),
+            pl.BlockSpec((SEQ, heads), lambda j: (0, slot_at(j))),
+            pl.BlockSpec((2, SEQ, SEQ), lambda j: (slot_at(j), 0, 0)),
+            const(SEQ, width),
+            pl.BlockSpec((width, 3 * heads), lambda j: (0, slot_at(j))),
+            ANY,
+            const(n, width),
+            ANY,
+        ],
+        out_specs=[
+            const(SEQ, width),
+            pl.BlockSpec((8, 3 * heads), lambda j: (0, slot_at(j))),
+            kept_spec(width, 3 * heads),
+            kept_spec(heads, width),
+            const(n, width // 4),
+            const(width // 4, n),
+        ],
+        out_shape=[
+            jax.ShapeDtypeStruct((SEQ, width), BF),
+            jax.ShapeDtypeStruct((8, 24 * heads), F32),
+            jax.ShapeDtypeStruct((3, width, 3 * heads), BF),
+            jax.ShapeDtypeStruct((3, heads, width), BF),
+            jax.ShapeDtypeStruct((n, width // 4), BF),
+            jax.ShapeDtypeStruct((width // 4, n), BF),
+        ],
+        scratch_shapes=[
+            pltpu.VMEM((width, SEQ), BF),
+            pltpu.VMEM((SEQ, width), F32),
+            pltpu.VMEM((2, SEQ, SEQ), BF),
+            pltpu.VMEM((SEQ, 3 * heads), BF),
+            DMA,
+            *Fold.scratch(width, 3 * heads),
+            *Fold.scratch(heads, width),
+            pltpu.VMEM((3, n, width // 4), BF),
+            DMA((6,)),
+            pltpu.VMEM((width, n), BF),
+            pltpu.VMEM((width, n), BF),
+            pltpu.VMEM((width, n), BF),
+            DMA((5,)),
+            pltpu.VMEM((width, n), BF),
+            pltpu.VMEM((3, width // 4, n), BF),
+            DMA((6,)),
+        ],
+        compiler_params=pltpu.CompilerParams(vmem_limit_bytes=VMEM_LIMIT, collective_id=5, has_side_effects=True),
+        name="attend_bwd",
+    )(gattn, wo, att, qkv, linv, p, x, w_qkv, r1, tot_d, kept_u)
+
+
+def last_kernel(
+    xg, kept_q, kept_o, own_d, own_u, vec_ref,
+    x_block, gq, go, gd, gu, slot_out, feat_ref,
+    q_own, q_x, q_y, q_c, q_tot, q_land, q_z, q_sum, o_own, o_x, o_y, o_c, o_tot, o_land, o_z, o_sum,
+    v1, v2, v3, l1, l2, l3, l4, v_own, v_sems, out_sems, s_sems,
+):
+    peers = Peers()
+    peers.greet(ALL_PEERS)
+    outward = Outward(peers, xg, x_block, out_sems)
+    cross_q = Cross(peers, kept_q, q_own, q_x, q_y, q_c)
+    cross_o = Cross(peers, kept_o, o_own, o_x, o_y, o_c)
+    deal_q = Deal(peers, q_tot, True, q_land, q_z)
+    deal_o = Deal(peers, o_tot, False, o_land, o_z)
+
+    def rows_at(ref):
+        n = ref.shape[0] // 4
+        return lambda q: ref.at[pl.ds(pl.multiple_of(q * n, n), n), :]
+
+    def cols_at(ref, first, n):
+        return lambda q: ref.at[:, pl.ds(pl.multiple_of(first + q * n, n), n)]
+
+    heads = q_sum.shape[1] // 3
+    units = own_u.shape[1]
+    spread_d = Spread(peers, own_d, rows_at(gd), s_sems.at[0])
+    spread_u = Spread(peers, own_u, cols_at(gu, 0, units), s_sems.at[1])
+    spread_o = Spread(peers, o_sum, rows_at(go), s_sems.at[2])
+    spread_q = [
+        Spread(peers, q_sum.at[:, pl.ds(i * heads, heads)], cols_at(gq, 4 * i * heads, heads), s_sems.at[3 + i])
+        for i in range(3)
+    ]
+    spread_v = Spread(peers, v_own, lambda q: slot_out.at[q], s_sems.at[6])
+
+    to_core = send(peers, "core", vec_ref.at[pl.ds(4, 12)], l1, v_sems.at[0], v_sems.at[1])
+    to_x = send(peers, "x", v1.at[pl.ds(2, 10)], l2, v_sems.at[2], v_sems.at[3])
+    to_y = send(peers, "y", v2.at[pl.ds(1, 11)], l3, v_sems.at[4], v_sems.at[5])
+    to_rows = []
+    for i in (1, 2, 3):
+        to_rows.append(send(peers, i, v3.at[0], l4.at[i - 1, 0], v_sems.at[6 + 4 * i], v_sems.at[7 + 4 * i]))
+        src = v3.at[pl.ds(4 + 2 * (4 - i), 2)]
+        to_rows.append(send(peers, i, src, l4.at[i - 1, pl.ds(1, 2)], v_sems.at[8 + 4 * i], v_sems.at[9 + 4 * i]))
+
+    to_core.start()
+    cross_o.start()
+    cross_q.start()
+    spread_d.start()
+    spread_u.start()
+    outward.start()
+
+    to_core.wait()
+    v1[0:4] = vec_ref[0:4] + l1[8:12]
+    v1[4:12] = vec_ref[4:12] + l1[0:8]
+    to_x.start()
+    to_x.wait()
+    v2[0:2] = v1[0:2] + l2[0:2]
+    v2[4:12] = v1[4:12] + l2[2:10]
+    v2[2:4] = v1[2:4]
+    to_y.start()
+    cross_o.finish(o_tot)
+    deal_o.start()
+    to_y.wait()
+    v3[0:1] = v2[0:1] + l3[0:1]
+    v3[4:12] = v2[4:12] + l3[3:11]
+    for c in to_rows:
+        c.start()
+    cross_q.finish(q_tot)
+    deal_q.start()
+    for c in to_rows:
+        c.wait()
+    v_own[...] = v3[0] + l4[0, 0] + l4[1, 0] + l4[2, 0]
+    feat_ref[...] = v3[4:6] + l4[0, 1:3] + l4[1, 1:3] + l4[2, 1:3]
+    spread_v.start()
+    spread_d.relay()
+    spread_u.relay()
+    deal_o.finish(o_sum)
+    spread_o.start()
+    spread_v.relay()
+    deal_q.finish(q_sum)
+    for sp in spread_q:
+        sp.start()
+    spread_o.relay()
+    for sp in spread_q:
+        sp.relay()
+    for sp in (spread_d, spread_u, spread_o, spread_v, *spread_q):
+        sp.finish()
+    outward.finish()
+
+
+def last(xg, kept_q, kept_o, own_d, own_u, vec):
+    width = xg.shape[1]
+    part = width // 4
+    n = own_d.shape[0]
+    heads = kept_o.shape[1]
+    vmem = pl.BlockSpec(memory_space=pltpu.VMEM)
+
+    def bufs(a, b, by_rows):
+        piece = (a // 4, b) if by_rows else (a, b // 4)
+        return [
+            pltpu.VMEM((a, b), BF),
+            pltpu.VMEM((a, b), BF),
+            pltpu.VMEM((a, b), BF),
+            DMA((5,)),
+            pltpu.VMEM((a, b), BF),
+            pltpu.VMEM((3, *piece), BF),
+            DMA((6,)),
+            pltpu.VMEM(piece, BF),
+        ]
+
+    return pl.pallas_call(
+        last_kernel,
+        in_specs=[ANY, ANY, ANY, ANY, ANY, vmem],
+        out_specs=[ANY, ANY, ANY, ANY, ANY, ANY, vmem],
+        out_shape=[
+            jax.ShapeDtypeStruct((4 * SEQ, part), BF),
+            jax.ShapeDtypeStruct((part, 12 * heads), BF),
+            jax.ShapeDtypeStruct((4 * heads, part), BF),
+            jax.ShapeDtypeStruct((4 * n, part), BF),
+            jax.ShapeDtypeStruct((part, 4 * n), BF),
+            jax.ShapeDtypeStruct((4, 8, 128), F32),
+            jax.ShapeDtypeStruct((2, 8, 128), F32),
+        ],
+        scratch_shapes=[
+            *bufs(width, 3 * heads, True),
+            *bufs(heads, width, False),
+            pltpu.VMEM((12, 8, 128), F32),
+            pltpu.VMEM((12, 8, 128), F32),
+            pltpu.VMEM((12, 8, 128), F32),
+            pltpu.VMEM((12, 8, 128), F32),
+            pltpu.VMEM((10, 8, 128), F32),
+            pltpu.VMEM((11, 8, 128), F32),
+            pltpu.VMEM((3, 3, 8, 128), F32),
+            pltpu.VMEM((8, 128), F32),
+            DMA((24,)),
+            DMA((8,)),
+            DMA((7, 7)),
+        ],
+        compiler_params=pltpu.CompilerParams(vmem_limit_bytes=VMEM_LIMIT, collective_id=6, has_side_effects=True),
+        name="last",
+    )(xg, kept_q, kept_o, own_d, own_u, vec)
 
 
 class Ring:
@@ -714,47 +1168,8 @@
         n = self.rows
         return lax.ppermute(v, "row", [(i, (i + s) % n) for i in range(n)])
 
-    def core(self, v):
-        return lax.ppermute(v, "dp", [(i, i ^ 1) for i in range(4)])
-
-    def x(self, v):
-        return lax.ppermute(v, "dp", [(i, i ^ 2) for i in range(4)])
-
     def y(self, v):
         return lax.ppermute(v, "col", [(0, 1), (1, 0)])
-
-    def gather(self, piece, axis):
-        parts = [piece]
-        for _ in range(self.rows - 1):
-            parts.append(self.shift(parts[-1], 1))
-        own = jnp.concatenate(parts, axis)
-        from_x, from_y = self.x(own), self.y(own)
-        half = own.shape[0] // 2
-        diag = jnp.concatenate([self.y(from_x[:half]), self.x(from_y[half:])], 0)
-        first = [own, from_x, from_y, diag]
-        other = [self.core(v) for v in first]
-        return [first[0], other[0], first[1], other[1], first[2], other[2], first[3], other[3]]
-
-    def scatter(self, blocks, cut):
-        kept = [blocks[0], blocks[2], blocks[4], blocks[6]]
-        sent = [blocks[1], blocks[3], blocks[5], blocks[7]]
-        own, to_x, to_y, diag = [
-            (a.astype(F32) + self.core(b).astype(F32)).astype(BF) for a, b in zip(kept, sent)
-        ]
-        half = own.shape[0] // 2
-        via_y = self.y(diag[:half])
-        via_x = self.x(diag[half:])
-        to_x = jnp.concatenate([to_x[:half] + via_y, to_x[half:]], 0)
-        to_y = jnp.concatenate([to_y[:half], to_y[half:] + via_x], 0)
-        total = (own.astype(F32) + self.x(to_x).astype(F32) + self.y(to_y).astype(F32)).astype(BF)
-        parts = cut(total)
-        acc = parts[1]
-        for s in range(1, self.rows):
-            got = self.shift(acc, 1)
-            acc = (parts[(s + 1) % self.rows].astype(F32) + got.astype(F32)).astype(BF)
-        pair = jnp.stack([acc, self.core(acc)])
-        quarters = jnp.concatenate([pair, self.x(pair)], 0)
-        return self.absolute(quarters)
 
     def absolute(self, quarters):
         a = jnp.where(self.d % 2 == 1, quarters[jnp.array([1, 0, 3, 2])], quarters)
@@ -774,15 +1189,6 @@
     r, c, d = ring.r, ring.c, ring.d
     R, C = lax.axis_size("row"), lax.axis_size("col")
     feat = tokens.shape[1]
-
-    def outward(rows):
-        whole = jnp.zeros((R * SEQ, feat), rows.dtype)
-        for s in range(R):
-            piece = rows[:, s * feat : (s + 1) * feat]
-            if s:
-                piece = ring.shift(piece, -s)
-            whole = lax.dynamic_update_slice_in_dim(whole, piece, ((r + s) % R) * SEQ, 0)
-        return whole
 
     pairs = []
     for row in range(R):
@@ -816,65 +1222,30 @@
         x, att, wo, feat_all, bu, cotangent, wu, wd
     )
 
-    out_block, dwu, dwd, grad_r1, grad_attn, vg1, bu_part = ff_bwd(
-        grad_r2, hidden_low, wu, wd, act, slope, normed1, inv1, feat_all, output
-    )
-    dwo = tmm(att, grad_attn).astype(BF)
-    grad_att = mm_t(grad_attn, wo).astype(BF)
-    g_qkv = attend_bwd(qkv, grad_att, att, linv, prob)
-    dwqkv = tmm(x, g_qkv).astype(BF)
-    x_grad = (mm_t(g_qkv, w_qkv) + grad_r1).astype(BF)
-    x_grad_block = outward(x_grad)
-
-    def rows_of(v, n=8):
-        k = v.shape[0] // n
-        return [v[i * k : (i + 1) * k] for i in range(n)]
-
-    def cols_of(v, n=8):
-        k = v.shape[1] // n
-        return [v[:, i * k : (i + 1) * k] for i in range(n)]
-
-    def cut_rows(v):
-        return rows_of(v, R)
-
-    def cut_cols(v):
-        return cols_of(v, R)
-
-    sum_down = ring.scatter(rows_of(dwd), cut_cols)
-    sum_up = ring.scatter(cols_of(dwu), cut_rows)
-    sum_out = ring.scatter(rows_of(dwo), cut_cols)
-    sum_qkv = ring.scatter(cols_of(dwqkv), cut_rows)
-    w_down_grad = sum_down.astype(F32).reshape(w_down.shape)
-    w_out_grad = sum_out.astype(F32).reshape(w_out.shape)
-    w_up_grad = sum_up.astype(F32).transpose(1, 0, 2).reshape(w_up.shape)
-    sum_qkv = sum_qkv.astype(F32).transpose(1, 0, 2)
-    wq_grad, wk_grad, wv_grad = [sum_qkv[:, :, i * hq : (i + 1) * hq].reshape(w_query.shape) for i in range(3)]
-
-    g32 = g_qkv.astype(F32)
-    slot_grad = jnp.concatenate(
-        [
-            jnp.sum(g32, axis=0).reshape(8, 3 * hq),
-            bu_part[0].reshape(8, unit),
-        ],
-        1,
-    )
+    out_block, grad_pre, bu_part, kept_d = ff_down_bwd(grad_r2, wd, act, slope, output)
+    out_block, grad_r1, grad_attn, vg1, kept_u, tot_d = ff_up_bwd(
+        grad_r2, hidden_low, grad_pre, wu, normed1, inv1, feat_all, output, out_block, kept_d
+    )
+    x_grad, g_part, kept_q, kept_o, own_d, own_u = attend_bwd(
+        grad_attn, wo, att, qkv, linv, prob, x, w_qkv, grad_r1, tot_d, kept_u
+    )
+
+    slot_grad = jnp.concatenate([g_part[0].reshape(8, 3 * hq), bu_part[0].reshape(8, unit)], 1)
+    slot_grad = jnp.pad(slot_grad, ((0, 0), (0, 1024 - slot_grad.shape[1]))).reshape(8, 8, 128)
     feat_grad = jnp.stack([vg1[2], vg1[0], vg1[1], vg2[2], vg2[0], vg2[1]])
-    slot_grad = slot_grad[0::2] + ring.core(slot_grad[1::2])
-    slot_grad = slot_grad[0::2] + ring.x(slot_grad[1::2])
-    slot_grad = slot_grad[0] + ring.y(slot_grad[1])
-    for s in (1, 2):
-        slot_grad = slot_grad + lax.ppermute(slot_grad, "row", [(i, i ^ s) for i in range(R)])
-    pair = jnp.stack([slot_grad, ring.core(slot_grad)])
-    slot_grad = ring.absolute(jnp.concatenate([pair, ring.x(pair)], 0))
-    bq_grad = slot_grad[:, :hq].reshape(-1)
-    bv_grad = slot_grad[:, 2 * hq : 3 * hq].reshape(-1)
-    bu_grad = slot_grad[:, 3 * hq :].reshape(-1)
-    feat_grad = feat_grad + ring.core(feat_grad)
-    feat_grad = feat_grad + ring.x(feat_grad)
-    feat_grad = feat_grad + ring.y(feat_grad)
-    own = feat_grad[:, :feat]
-    for s in range(1, R):
-        own = own + ring.shift(feat_grad[:, s * feat : (s + 1) * feat], -s)
+    feat_grad = feat_grad.reshape(6, R, feat).transpose(1, 0, 2).reshape(R, 6 * feat)
+    feat_grad = jnp.pad(feat_grad, ((0, 0), (0, 2048 - 6 * feat))).reshape(8, 8, 128)
+    pick = [slot_grad[t : t + 1] for t in (0, 4, 2, 6)]
+    tiles = jnp.concatenate(pick + [feat_grad] + [slot_grad[t : t + 1] for t in (1, 5, 3, 7)], 0)
+
+    x_grad_block, gq, go, gd, gu, slot_sum, own = last(x_grad, kept_q, kept_o, own_d, own_u, tiles)
+    wq_grad, wk_grad, wv_grad = [gq[:, i * 4 * hq : (i + 1) * 4 * hq].astype(F32) for i in range(3)]
+    w_out_grad, w_up_grad, w_down_grad = go.astype(F32), gu.astype(F32), gd.astype(F32)
+    slot_sum = slot_sum.reshape(4, 1024)
+    bq_grad = slot_sum[:, :hq].reshape(-1)
+    bv_grad = slot_sum[:, 2 * hq : 3 * hq].reshape(-1)
+    bu_grad = slot_sum[:, 3 * hq : 3 * hq + unit].reshape(-1)
+    own = own.reshape(-1)[: 6 * feat].reshape(6, feat)
     return (
         out_block, x_grad_block, wq_grad, bq_grad, wk_grad, wv_grad, bv_grad, w_out_grad, own[0], own[1], own[2],
         w_up_grad, bu_grad, w_down_grad, own[3], own[4], own[5],

time: 667 us -> 508 us (0.76); the launches traced: 656 us -> 506 us
  waiting for transfers between devices: 167 us -> 0.01 us
  Pallas kernels: 304 us -> 460 us
  starting transfers between devices: 53.6 us -> 9.04 us
  other arithmetic: 50.4 us -> 9.98 us
  local copies, waits for them, and re-layouts: 52.8 us -> 25.8 us
  matrix products: 25.3 us -> 0 us
    pallas_call x2 -> x4, Pallas kernels: 91 us -> 242 us  [the longest x1 81.3 us: attend_bwd(): pl.pallas_call(attend_bwd_kernel, grid=(8,), in_specs=[const(SEQ, width),...]
    ppermute x21 -> x3, waiting for transfers between devices: 78.4 us -> 0.01 us  [shift(): return lax.ppermute(v, 'row', [(i, (i + s) % n) for i in range(n)])]
    ppermute x40 -> x0, waiting for transfers between devices: 66.1 us -> none  [the longest x15 60.8 us: x(): return lax.ppermute(v, 'dp', [(i, i ^ 2) for i in range(4)])]
    dot_general x4 -> x0, matrix products: 25.3 us -> none  [the longest x2 12.9 us: tmm(): lax.dot_general(a, b, (((0,), (0,)), ((), ())), preferred_element_type=F32)]
    ppermute x40 -> x0, starting transfers between devices: 24.7 us -> none  [the longest x15 15.3 us: x(): return lax.ppermute(v, 'dp', [(i, i ^ 2) for i in range(4)])]
    ppermute x11 -> x1, waiting for transfers between devices: 22.5 us -> 0.01 us  [y(): return lax.ppermute(v, 'col', [(0, 1), (1, 0)])]
    convert_element_type x23 -> x4, other arithmetic: 29.1 us -> 7.21 us  [the longest x1 2.4 us: whole_sequences(): gq[:, i * 4 * hq:(i + 1) * 4 * hq].astype(F32)]
    slice x23 -> x2, local copies, waits for them, and re-layouts: 14.3 us -> 0.95 us  [the longest x1 0.93 us: whole_sequences(): g_part[0].reshape(8, 3 * hq)]
  transfers between devices with their start and end apart: 73 -> 5, of which waited for: 31 -> 0; matrix products, arithmetic and copies ran while one was open for 12% -> 2% of each run, Pallas kernels for 10% -> 14%
where the time goes in v3:
time: 508 us; the launch traced here: 506 us
  Pallas kernels  460 us (91%)
  local copies, waits for them, and re-layouts  25.8 us (5%)
  other arithmetic  9.98 us (2%)
  starting transfers between devices  9.04 us (2%)
    pallas_call x1, Pallas kernels, attend_bwd(): pl.pallas_call(attend_bwd_kernel, grid=(8,), in_specs=[const(SEQ, width),...  81.3 us
    pallas_call x1, Pallas kernels, last(): pl.pallas_call(last_kernel, in_specs=[ANY, ANY, ANY, ANY, ANY, vmem], out...  76.2 us
    pallas_call x1, Pallas kernels, attend_fwd(): pl.pallas_call(attend_fwd_kernel, grid=(slots,), in_specs=[pl.BlockSpec((...  75.6 us
    pallas_call x1, Pallas kernels, ff_fwd(): pl.pallas_call(ff_fwd_kernel, grid=(8,), in_specs=[const(SEQ, width), con...  72.9 us
    pallas_call x1, Pallas kernels, first(): pl.pallas_call(first_kernel, in_specs=[ANY, ANY], out_specs=[ANY, ANY], o...  69.4 us
    pallas_call x1, Pallas kernels, ff_up_bwd(): pl.pallas_call(ff_up_bwd_kernel, grid=(8,), in_specs=[const(SEQ, width),...  52.9 us
    pallas_call x1, Pallas kernels, ff_down_bwd(): pl.pallas_call(ff_down_bwd_kernel, grid=(8,), in_specs=[const(SEQ, width)...  31.6 us
  transfers between devices with their start and end apart: 5, of which 0 were waited for; matrix products, arithmetic and copies ran while one was open for 2% of the time, Pallas kernels for 14%

profile of v3, /device:TPU:0, one launch (start us, length us, event | category | flops | bytes accessed | tf_op | source)
XLA Modules:
  0.0 505.7 jit_solution(3167527303338752981)
XLA Ops:
  0.7 0.7 stack.27
  4.7 5.1 %collective-permute-start.4 = (bf16[8,256]{1,0:T(8,128)(2,1)S(1)}, bf16[8,256]{1,0:T(8,128)(2,1)S(1)}, u32[]{:S(2)}, u32[]{:S(2)}) collective-permute-start(bf16[8,256]{1,0:T(8,128)(2,1)S(1)} %stack.33), channel_id=1, source_target_pairs={{0,6},{2,0},{4,2},{6,4},{1,7},{3,1},{5,3},{7,5},{8,14},{10,8},{12,... | collective-permute-start | bytes 12296 | tf_op jit(solution)/shard_map/ppermute | solution.py:1169
  9.8 1.0 collective-permute-start.2
  13.6 1.6 collective-permute-start
  15.1 1.3 collective-permute-start.1
  17.2 1.7 constant_dynamic-slice_fusion.2.pd
  18.9 0.8 constant_dynamic-slice_fusion.5
  19.7 0.9 constant_dynamic-slice_fusion.3
  21.3 1.5 constant_dynamic-slice_fusion.1.po
  22.8 69.4 %first.1 = (bf16[1024,1024]{1,0:T(8,128)(2,1)}, bf16[1024,3072]{1,0:T(8,128)(2,1)}) custom-call(bf16[4096,256]{1,0:T(8,128)(2,1)} %tokens.1, bf16[256,384]{1,0:T(8,128)(2,1)} %pad_maximum_fusion.piece), custom_call_target="tpu_custom_call" | custom-call | tf_op jit(solution)/shard_map/first/pallas_call | solution.py:308
  94.1 1.0 copy.39.seg_col_ref
  95.1 75.6 %attend_fwd.1 = (bf16[1024,3072]{1,0:T(8,128)(2,1)}, bf16[1024,1024]{1,0:T(8,128)(2,1)}, bf16[16,1024,1024]{2,1,0:T(8,128)(2,1)}, f32[1024,1024]{1,0:T(8,128)}, ...) custom-call(bf16[1024,1024]{1,0:T(8,128)(2,1)} %get-tuple-element.59.x_ref, ...), custom_call_target="tpu_custom_call" | custom-call | flops 17179869184 | bytes 41943040 | tf_op jit(solution)/shard_map/attend_fwd/pallas_call | solution.py:116
  170.8 72.9 %ff_fwd.1 = (bf16[1024,4096]{1,0:T(8,128)(2,1)}, bf16[4096,1024]{1,0:T(8,128)(2,1)}, bf16[1024,4096]{1,0:T(8,128)(2,1)}, bf16[1024,4096]{1,0:T(8,128)(2,1)}, bf1...) custom-call(bf16[1024,1024]{1,0:T(8,128)(2,1)} %get-tuple-element.59, ...), custom_call_target="tpu_custom_call", output_to_operand_aliasing={{0}: (6, {}), {1}: (7, {})} | custom-call | tf_op jit(solution)/shard_map/ff_fwd/pallas_call | solution.py:470
  243.7 0.8 slice.147
  244.5 0.8 slice.148
  245.2 31.6 %ff_down_bwd.1 = (bf16[4096,256]{1,0:T(8,128)(2,1)}, bf16[1024,4096]{1,0:T(8,128)(2,1)}, f32[8,4096]{1,0:T(8,128)}, bf16[3,512,1024]{2,1,0:T(8,128)(2,1)}) custom-call(f32[1024,1024]{1,0:T(8,128)} %get-tuple-element.65.r2_ref, bf16[4096,1024]{1,0:T(8,128)(2,1)} %get-tuple-element.67.wd_ref, bf16[1024,4096]{1,0:T(8,128)(2,1)} %get-tuple-element.68.act_ref, ...), custom_call_target="tpu_custom_call" | custom-call | tf_op jit(solution)/shard_map/ff_down_bwd/pallas_call | solution.py:758
  276.8 52.9 %ff_up_bwd.1 = (bf16[4096,256]{1,0:T(8,128)(2,1)}, f32[1024,1024]{1,0:T(8,128)}, bf16[1024,1024]{1,0:T(8,128)(2,1)}, f32[8,1024]{1,0:T(8,128)}, bf16[3,1024,512]...) custom-call(f32[1024,1024]{1,0:T(8,128)} %get-tuple-element.65.r2_ref, ...), custom_call_target="tpu_custom_call", output_to_operand_aliasing={{0}: (8, {})} | custom-call | tf_op jit(solution)/shard_map/ff_up_bwd/pallas_call | solution.py:836
  329.7 0.8 slice.145
  330.5 0.8 slice.146
  331.3 81.3 %attend_bwd.1 = (bf16[1024,1024]{1,0:T(8,128)(2,1)}, f32[8,3072]{1,0:T(8,128)}, bf16[3,1024,384]{2,1,0:T(8,128)(2,1)}, bf16[3,128,1024]{2,1,0:T(8,128)(2,1)}, bf...) custom-call(bf16[1024,1024]{1,0:T(8,128)(2,1)} %get-tuple-element.78.gattn_ref, ...), custom_call_target="tpu_custom_call" | custom-call | tf_op jit(solution)/shard_map/attend_bwd/pallas_call | solution.py:965
  412.6 0.9 slice_reduce_fusion.1
  413.6 0.9 slice_reduce_fusion
  415.3 76.2 %last.1 = (bf16[4096,256]{1,0:T(8,128)(2,1)}, bf16[256,1536]{1,0:T(8,128)(2,1)}, bf16[512,256]{1,0:T(8,128)(2,1)}, bf16[2048,256]{1,0:T(8,128)(2,1)}, bf16[256,2...) custom-call(bf16[1024,1024]{1,0:T(8,128)(2,1)} %get-tuple-element.85.xg, ...), custom_call_target="tpu_custom_call" | custom-call | tf_op jit(solution)/shard_map/last/pallas_call | solution.py:1127
  491.5 0.8 copy.45
  492.9 1.4 fusion.1
  494.9 1.8 convert_element_type.33
  496.7 2.4 slice_convert_fusion
  499.1 1.6 convert_element_type.34
  500.7 1.5 convert_element_type.35
  502.2 0.9 copy-done.2
  503.0 1.3 copy.59
  504.4 1.3 copy.60
  (64 shorter events, 11.3 us)
Async XLA Ops:
  0.7 15.8 %copy-start = (bf16[256,2048]{1,0:T(8,128)(2,1)S(1)}, bf16[256,2048]{1,0:T(8,128)(2,1)}, u32[]{:S(2)}) copy-start(bf16[256,2048]{1,0:T(8,128)(2,1)} %param.30) | copy-start | bytes 3145732
  4.7 87.4 %collective-permute-start.4 = (bf16[8,256]{1,0:T(8,128)(2,1)S(1)}, bf16[8,256]{1,0:T(8,128)(2,1)S(1)}, u32[]{:S(2)}, u32[]{:S(2)}) collective-permute-start(bf16[8,256]{1,0:T(8,128)(2,1)S(1)} %stack.33), channel_id=1, source_target_pairs={{0,6},{2,0},{4,2},{6,4},{1,7},{3,1},{5,3},{7,5},{8,14},{10,8},{12,... | collective-permute-start | bytes 12296 | tf_op jit(solution)/shard_map/ppermute | solution.py:1169
  9.8 82.4 %collective-permute-start.3 = (bf16[8,256]{1,0:T(8,128)(2,1)S(1)}, bf16[8,256]{1,0:T(8,128)(2,1)S(1)}, u32[]{:S(2)}, u32[]{:S(2)}) collective-permute-start(bf16[8,256]{1,0:T(8,128)(2,1)S(1)} %stack.33), channel_id=1, source_target_pairs={{0,4},{2,6},{4,0},{6,2},{1,5},{3,7},{5,1},{7,3},{8,12},{10,14},{12... | collective-permute-start | bytes 12296 | tf_op jit(solution)/shard_map/ppermute | solution.py:1169
  9.8 82.4 %collective-permute-start.2 = (bf16[8,256]{1,0:T(8,128)(2,1)S(1)}, bf16[8,256]{1,0:T(8,128)(2,1)S(1)}, u32[]{:S(2)}, u32[]{:S(2)}) collective-permute-start(bf16[8,256]{1,0:T(8,128)(2,1)S(1)} %stack.33), channel_id=1, source_target_pairs={{0,2},{2,4},{4,6},{6,0},{1,3},{3,5},{5,7},{7,1},{8,10},{10,12},{12... | collective-permute-start | bytes 12296 | tf_op jit(solution)/shard_map/ppermute | solution.py:1169
  13.6 79.3 %collective-permute-start = (bf16[4,896]{1,0:T(4,128)(2,1)S(1)}, bf16[4,896]{1,0:T(4,128)(2,1)S(1)}, u32[]{:S(2)}, u32[]{:S(2)}) collective-permute-start(bf16[4,896]{1,0:T(4,128)(2,1)S(1)} %maximum_select_fusion), channel_id=1, source_target_pairs={{0,1},{1,0},{2,3},{3,2},{4,5},{5,4},{6,7},{7,6},{8,9},{9,8},{10,11... | collective-permute-start | bytes 21512 | tf_op jit(solution)/shard_map/ppermute | solution.py:1172
  15.1 79.0 %collective-permute-start.1 = (s32[2048]{0:T(1024)}, s32[2048]{0:T(1024)S(1)}, u32[]{:S(2)}, u32[]{:S(2)}) collective-permute-start(s32[2048]{0:T(1024)} %param.20), channel_id=1, source_target_pairs={{0,0},{4,1},{1,2},{5,3},{2,4},{6,5},{3,6},{7,7},{8,8},{12,9},{9,10... | collective-permute-start | bytes 24584 | tf_op jit(solution)/shard_map/ppermute | solution.py:1198
  94.1 1.0 copy-start.7
  414.7 0.6 copy-start.6
  491.5 7.6 %copy-start.5 = (bf16[256,2048]{1,0:T(8,128)(2,1)S(1)}, bf16[256,2048]{1,0:T(8,128)(2,1)}, u32[]{:S(2)}) copy-start(bf16[256,2048]{1,0:T(8,128)(2,1)} %get-tuple-element.99) | copy-start | bytes 3145732
  496.7 4.0 copy-start.4
  500.7 2.3 copy-start.2
  502.2 2.2 copy-start.3
  503.0 2.6 copy-start.1

commit v4 on v3

--- a/solution.py
+++ b/solution.py
@@ -16,6 +16,15 @@
 F32 = jnp.float32
 NEG = -1e30
 QB = 256
+VMEM_LIMIT = 56 * 1024 * 1024
+MESH = pl.DeviceIdType.MESH
+ANY = pl.BlockSpec(memory_space=pl.ANY)
+DMA = pltpu.SemaphoreType.DMA
+ONCE = pl.Buffered(1)
+
+
+def const(*shape):
+    return pl.BlockSpec(shape, lambda j: (0,) * len(shape), pipeline_mode=ONCE)
 
 
 def mm(a, b):
@@ -41,7 +50,7 @@
     q = qkv_ref[rows, 0:128]
     k = qkv_ref[:, 128:256]
     v = qkv_ref[:, 256:384]
-    seg_col = seg_col_ref[rows, :]
+    seg_col = seg_col_ref[rows, 0:1]
     outs = []
     for h in range(2):
         mine = (lane < HD) if h == 0 else (lane >= HD)
@@ -60,124 +69,139 @@
 
 
 def attend_fwd_kernel(
-    x_ref, w_ref, b_ref, seg_col_ref, seg_row_ref, po, pu, pd,
-    qkv_ref, o_ref, p_ref, linv_ref, wo, wu, wd, o_recv, o_sent, u_recv, u_sent, d_recv, d_sent,
+    x_ref, w_ref, b_ref, seg_ref, cot, wo_in, wu_in, wd_in,
+    qkv_ref, o_ref, p_ref, linv_ref, wo, wu, wd, cot_first,
+    seg_col_ref, seg_row_ref, cot_own, i_sems, o_recv, o_sent, u_recv, u_sent, d_recv, d_sent,
 ):
     j = pl.program_id(0)
     peers = Peers()
-    go = Gather(peers, po, wo, False, o_recv, o_sent, RING + NEAR + FAR)
-    gu = Gather(peers, pu, wu, True, u_recv, u_sent, RING + NEAR)
-    gd = Gather(peers, pd, wd, False, d_recv, d_sent, RING + DOWN_NEAR)
+    go = Gather(peers, None, wo, False, o_recv, o_sent, RING + LATER_NEAR + FAR)
+    gu = Gather(peers, None, wu, True, u_recv, u_sent, RING + LATER_NEAR)
+    gd = Gather(peers, None, wd, False, d_recv, d_sent, RING + DOWN_NEAR)
     every = (go, gu, gd)
-
-    def hook(at, *stages):
-        @pl.when(j == at)
-        def _():
-            for which, blocks in stages:
-                for g in which:
-                    g.relay(*blocks)
+    inward = Inward(peers, cot, cot_first, cot_own, i_sems, (0,))
+
+    plan = {
+        8: ((go, (1, 0)), (gu, (1, 0))),
+        12: ((gd, (1, 0)), (go, (1, 2), (1, 4), (2, 0)), (gu, (1, 2), (1, 4))),
+        16: ((gu, (2, 0)), (go, (0, 6), (1, 6)), (gd, (1, 2), (1, 4))),
+        20: ((gd, (2, 0)), (go, (2, 2), (2, 4), (3, 0)), (gu, (2, 2), (2, 4))),
+        25: ((gu, (3, 0)), (go, (2, 6), (3, 2), (3, 4)), (gd, (2, 2), (2, 4))),
+        29: ((gd, (3, 0)), (gu, (3, 2), (3, 4)), (go, (3, 6))),
+    }
+
+    def hook(i):
+        for at, work in plan.items():
+            if at % 4 == i:
+                @pl.when(j == at // 4)
+                def _(at=at, work=work):
+                    for g, *blocks in work:
+                        g.relay(*blocks)
+                    if at == 20:
+                        inward.settle()
+                        inward.start(0)
 
     @pl.when(j == 0)
     def _():
-        peers.greet(ALL_PEERS)
+        peers.hello(ALL_PEERS)
+        inward.load()
+        tile = seg_ref[4 * peers.c + peers.r]
+        for i in range(8):
+            row = tile[i : i + 1, :]
+            at = lax.broadcasted_iota(jnp.int32, (1, 128), 1) + i * 128
+            row = jnp.where(row == 0, -1 - at, row)
+            seg_row_ref[:, i * 128 : (i + 1) * 128] = row
+            seg_col_ref[i * 128 : (i + 1) * 128, :] = jnp.transpose(jnp.broadcast_to(row, (128, 128)))
+
+    qkv_ref[...] = (mm(x_ref[...], w_ref[...]) + b_ref[0, :, 0:384]).astype(BF)
+    @pl.when(j == 0)
+    def _():
+        peers.meet(ALL_PEERS)
         for g in every:
-            g.start()
+            g.emit(0, 0)
+        go.emit(0, 2)
 
     seg_row = seg_row_ref[...]
-    hook(1, ((go, gu), [(1, 0)]))
-    hook(2, (every, [(0, 2), (0, 4)]))
-    hook(3, ((go, gu), [(2, 0)]), ((go,), [(1, 2), (1, 4)]))
-    hook(4, ((gu, gd), [(1, 2), (1, 4)]))
-    hook(5, ((go, gu), [(3, 0)]))
-    hook(6, (every, [(2, 2), (2, 4)]), ((go,), [(0, 6), (1, 6)]))
-    hook(7, ((go,), [(3, 2), (3, 4)]))
-    qkv_ref[...] = (mm(x_ref[...], w_ref[...]) + b_ref[...]).astype(BF)
     for i in range(SEQ // QB):
-        if i == SEQ // QB // 2:
-            hook(1, ((gd,), [(1, 0)]))
-            hook(3, ((gd,), [(2, 0)]))
-            hook(5, ((gd,), [(3, 0)]))
-            hook(7, ((go,), [(2, 6), (3, 6)]), ((gu,), [(3, 2), (3, 4)]))
+        hook(i)
         attend_rows(qkv_ref, seg_col_ref, seg_row, o_ref, p_ref, linv_ref, i)
 
     @pl.when(j == 7)
     def _():
         for g in every:
             g.finish()
-
-
-VMEM_LIMIT = 56 * 1024 * 1024
-
-
-def attend_fwd(x, w_qkv, b_qkv, seg_col, seg_row, po, pu, pd):
+        inward.finish()
+
+
+def attend_fwd(x, w_qkv, b_slot, seg, cot, wo, wu, wd):
     slots = w_qkv.shape[1] // 384
-    whole = pl.BlockSpec(memory_space=pl.ANY)
-    dma = pltpu.SemaphoreType.DMA
     return pl.pallas_call(
         attend_fwd_kernel,
         grid=(slots,),
         in_specs=[
-            pl.BlockSpec((SEQ, x.shape[1]), lambda j: (0, 0)),
+            const(SEQ, x.shape[1]),
             pl.BlockSpec((x.shape[1], 384), lambda j: (0, j)),
-            pl.BlockSpec((1, 384), lambda j: (0, j)),
-            pl.BlockSpec((SEQ, 1), lambda j: (0, 0)),
-            pl.BlockSpec((1, SEQ), lambda j: (0, 0)),
-            whole,
-            whole,
-            whole,
+            pl.BlockSpec((1, 1, b_slot.shape[2]), lambda j: (j, 0, 0)),
+            const(8, 8, 128),
+            ANY,
+            ANY,
+            ANY,
+            ANY,
         ],
         out_specs=[
             pl.BlockSpec((SEQ, 384), lambda j: (0, j)),
             pl.BlockSpec((SEQ, 128), lambda j: (0, j)),
             pl.BlockSpec((2, SEQ, SEQ), lambda j: (j, 0, 0)),
             pl.BlockSpec((SEQ, 128), lambda j: (0, j)),
-            whole,
-            whole,
-            whole,
+            ANY,
+            ANY,
+            ANY,
+            ANY,
         ],
         out_shape=[
             jax.ShapeDtypeStruct((SEQ, slots * 384), BF),
             jax.ShapeDtypeStruct((SEQ, slots * 128), BF),
             jax.ShapeDtypeStruct((slots * 2, SEQ, SEQ), BF),
             jax.ShapeDtypeStruct((SEQ, slots * 128), F32),
-            jax.ShapeDtypeStruct((8 * po.shape[0], 4 * po.shape[1]), BF),
-            jax.ShapeDtypeStruct((4 * pu.shape[0], 8 * pu.shape[1]), BF),
-            jax.ShapeDtypeStruct((8 * pd.shape[0], 4 * pd.shape[1]), BF),
-        ],
-        scratch_shapes=[dma((32,)), dma((32,))] * 3,
+            jax.ShapeDtypeStruct(wo.shape, BF),
+            jax.ShapeDtypeStruct(wu.shape, BF),
+            jax.ShapeDtypeStruct(wd.shape, BF),
+            jax.ShapeDtypeStruct((SEQ // CHUNKS, x.shape[1]), BF),
+        ],
+        input_output_aliases={5: 4, 6: 5, 7: 6},
+        scratch_shapes=[
+            pltpu.VMEM((SEQ, 128), jnp.int32),
+            pltpu.VMEM((1, SEQ), jnp.int32),
+            pltpu.VMEM((SEQ // CHUNKS, cot.shape[1]), BF),
+            sems_of_exchange(),
+            *[DMA((32,))] * 6,
+        ],
         compiler_params=pltpu.CompilerParams(vmem_limit_bytes=VMEM_LIMIT, collective_id=1, has_side_effects=True),
-        cost_estimate=pl.CostEstimate(
-            flops=slots * 2 * 4 * SEQ * SEQ * 256,
-            bytes_accessed=slots * 5 * SEQ * SEQ,
-            transcendentals=slots * 2 * SEQ * SEQ,
-        ),
         name="attend_fwd",
-    )(x, w_qkv, b_qkv, seg_col, seg_row, po, pu, pd)
-
-
-MESH = pl.DeviceIdType.MESH
-ANY = pl.BlockSpec(memory_space=pl.ANY)
-DMA = pltpu.SemaphoreType.DMA
+    )(x, w_qkv, b_slot, seg, cot, wo, wu, wd)
 
 
 class Peers:
     def __init__(self):
         self.r = lax.axis_index("row")
-        d = lax.axis_index("dp")
+        self.c = lax.axis_index("col")
+        self.d = d = lax.axis_index("dp")
         self.ids = {
             "core": {"dp": d + 1 - 2 * lax.rem(d, 2)},
             "x": {"dp": lax.rem(d + 2, 4)},
-            "y": {"col": 1 - lax.axis_index("col")},
+            "y": {"col": 1 - self.c},
             1: {"row": lax.rem(self.r + 1, 4)},
             2: {"row": lax.rem(self.r + 2, 4)},
             3: {"row": lax.rem(self.r + 3, 4)},
         }
 
-    def greet(self, names):
+    def hello(self, names):
         barrier = pltpu.get_barrier_semaphore()
         for name in names:
             pl.semaphore_signal(barrier, inc=1, device_id=self.ids[name], device_id_type=MESH)
-        pl.semaphore_wait(barrier, len(names))
+
+    def meet(self, names):
+        pl.semaphore_wait(pltpu.get_barrier_semaphore(), len(names))
 
 
 def send(peers, name, src, dst, send_sem, recv_sem):
@@ -201,7 +225,9 @@
 RING = [(1, s, 0, s + 1, 0) for s in range(3)]
 NEAR = [e for s in range(4) for e in near_edges(s) + second_edges(s)]
 FAR = [e for s in range(4) for e in far_edges(s)]
-DOWN_NEAR = [e for s in range(3) for e in near_edges(s) + second_edges(s)] + [("core", 3, 0, 3, 1)]
+OWN_BLOCK = near_edges(0) + second_edges(0)
+LATER_NEAR = [e for e in NEAR if e[1] > 0]
+DOWN_NEAR = [e for e in LATER_NEAR if e[1] < 3] + [("core", 3, 0, 3, 1)]
 DOWN_REST = [e for e in near_edges(3) if e[0] != "core"] + second_edges(3) + FAR
 
 
@@ -229,6 +255,12 @@
         for at, e in enumerate(self.edges):
             if e[1:3] == (s, t):
                 assert at not in self.emitted
+                self.emitted.add(at)
+                self.copy(at).start()
+
+    def emit_own_slot(self, s):
+        for at, e in enumerate(self.edges):
+            if e[1:3] == (s, 0):
                 self.emitted.add(at)
                 self.copy(at).start()
 
@@ -262,61 +294,248 @@
             self.copy(at).wait_send()
 
 
+class Line:
+    WAVES = ((3, 2, 1), (1, 3, 2), (1, 3, 2), (1, 2, 3))
+
+    def __init__(self, peers, gather, sems):
+        self.peers, self.gather, self.sems = peers, gather, sems
+
+    def copy(self, up, s):
+        s2 = s + 1 if up else (s - 1 if s else 3)
+        g = self.gather
+        src = g.piece if s == 0 else g.blk(s, 0)
+        return send(
+            self.peers, 1 if up else 3, src, g.blk(s2, 0), self.sems.at[(0 if up else 4) + s], self.sems.at[7 + s2]
+        )
+
+    def each(self, what):
+        r = self.peers.r
+        for s in range(3):
+            @pl.when((r >= s) & (r < 3))
+            def _(s=s):
+                what(self.copy(True, s))
+        for s in (0, 3, 2):
+            @pl.when((r > 0) & (r <= (3 if s == 0 else s - 1)))
+            def _(s=s):
+                what(self.copy(False, s))
+
+    def start(self):
+        r = self.peers.r
+
+        @pl.when(r < 3)
+        def _():
+            self.copy(True, 0).start()
+
+        @pl.when(r > 0)
+        def _():
+            self.copy(False, 0).start()
+
+    def wave(self, k):
+        for row, order in enumerate(self.WAVES):
+            s = order[k]
+
+            @pl.when(self.peers.r == row)
+            def _(row=row, s=s):
+                self.copy(True, s - 1).wait_recv()
+                below = row >= s
+                if below and row < 3:
+                    self.copy(True, s).start()
+                if not below and row > 0:
+                    self.copy(False, s).start()
+                self.gather.emit_own_slot(s)
+
+    def finish(self):
+        self.each(lambda c: c.wait_send())
+
+
+CHUNKS = 4
+
+
+def sems_of_exchange():
+    return DMA((2, 4, CHUNKS))
+
+
 class Inward:
-    def __init__(self, peers, block, rows, recv, sent):
-        self.peers, self.block, self.rows, self.recv, self.sent = peers, block, rows, recv, sent
-
-    def copy(self, s):
+    def __init__(self, peers, block, rows, buf, sems, chunks=range(CHUNKS)):
+        self.peers, self.block, self.rows, self.buf, self.sems, self.chunks = peers, block, rows, buf, sems, chunks
+        self.n = SEQ // CHUNKS
+
+    def ends(self, s, first, count):
         r = lax.rem(self.peers.r + s, 4)
-        src = self.block.at[pl.ds(pl.multiple_of(r * SEQ, SEQ), SEQ), :]
         f = self.block.shape[1]
-        dst = self.rows.at[:, pl.ds(s * f, f)]
-        if s == 0:
-            return pltpu.make_async_copy(src, dst, self.sent.at[0])
-        return send(self.peers, s, src, dst, self.sent.at[s], self.recv.at[s])
-
-    def start(self):
-        for s in (2, 1, 3, 0):
-            self.copy(s).start()
+        src = self.block.at[pl.ds(pl.multiple_of(r * SEQ + first * self.n, self.n), count * self.n), :]
+        at = first if self.rows.shape[0] == SEQ else first - self.chunks[0]
+        return src, self.rows.at[pl.ds(at * self.n, count * self.n), pl.ds(s * f, f)]
+
+    def copy(self, s, k):
+        return send(self.peers, s, *self.ends(s, k, 1), self.sems.at[0, s, k], self.sems.at[1, s, k])
+
+    def own(self):
+        src, dst = self.ends(0, self.chunks[0], len(self.chunks))
+        return (
+            pltpu.make_async_copy(src, self.buf, self.sems.at[0, 0, 0]),
+            pltpu.make_async_copy(self.buf, dst, self.sems.at[1, 0, 0]),
+        )
+
+    def start(self, *chunks):
+        for k in chunks:
+            for s in (2, 1, 3):
+                self.copy(s, k).start()
+
+    def load(self):
+        self.own()[0].start()
+
+    def settle(self):
+        self.own()[0].wait()
+        self.own()[1].start()
 
     def finish(self):
-        self.copy(0).wait()
-        for s in (1, 2, 3):
-            self.copy(s).wait()
+        self.own()[1].wait()
+        for k in self.chunks:
+            for s in (1, 2, 3):
+                self.copy(s, k).wait()
 
 
 ALL_PEERS = ("core", "x", "y", 1, 2, 3)
 
 
-def first_kernel(tokens, piece, x, w, g_recv, g_sent, i_recv, i_sent):
+def first_kernel(
+    tokens, segments, w_query, w_key, w_value, w_out, w_up, w_down,
+    vectors,
+    x, w, wo, wu, wd, feat_out, slot_out, seg_out,
+    pq, po, pu, pd, rows_buf, feat, slot, l_sems, q_recv, q_sent, o_recv, o_sent, u_recv, u_sent, d_recv, d_sent,
+    i_sems, v_sems, z_sems,
+):
     peers = Peers()
-    peers.greet(ALL_PEERS)
-    g = Gather(peers, piece, w, True, g_recv, g_sent, RING + NEAR + FAR)
-    a = Inward(peers, tokens, x, i_recv, i_sent)
-    g.start()
-    a.start()
+    r, d = peers.r, peers.d
+
+    def own_cols(ref):
+        n = ref.shape[1] // 4
+        return ref.at[:, pl.ds(pl.multiple_of(d * n, n), n)]
+
+    def own_rows(ref):
+        n = ref.shape[0] // 4
+        return ref.at[pl.ds(pl.multiple_of(d * n, n), n), :]
+
+    peers.hello(ALL_PEERS)
+    heads = w_query.shape[1] // 4
+    loads = [
+        pltpu.make_async_copy(own_cols(ref), pq.at[:, pl.ds(i * heads, heads)], l_sems.at[i])
+        for i, ref in enumerate((w_query, w_key, w_value))
+    ]
+    loads += [
+        pltpu.make_async_copy(own_rows(w_out), po, l_sems.at[3]),
+        pltpu.make_async_copy(own_cols(w_up), pu, l_sems.at[4]),
+        pltpu.make_async_copy(own_rows(w_down), pd, l_sems.at[5]),
+    ]
+    for c in loads:
+        c.start()
+    feat[...] = jnp.zeros_like(feat)
+    f = feat.shape[1]
+    for i in range(6):
+        feat[i : i + 1, :] = vectors[:, i * f : (i + 1) * f]
+    units = slot.shape[2] - 3 * heads
+    at_q, at_v, at_u = 6 * f, 6 * f + 4 * heads, 6 * f + 8 * heads
+
+    def quarter(first, n, q):
+        return vectors[:, pl.ds(pl.multiple_of(first + q * n, 128), n)]
+
+    for t in range(4):
+        q = d
+        if t % 2:
+            q = q + 1 - 2 * lax.rem(q, 2)
+        if t // 2:
+            q = lax.rem(q + 2, 4)
+        slot[t, :, 0:heads] = quarter(at_q, heads, q)
+        slot[t, :, heads : 2 * heads] = jnp.zeros((1, heads), F32)
+        slot[t, :, 2 * heads : 3 * heads] = quarter(at_v, heads, q)
+        slot[t, :, 3 * heads :] = quarter(at_u, units, q)
+    for c in loads:
+        c.wait()
+
+    gq = Gather(peers, pq, w, True, q_recv, q_sent, NEAR + FAR)
+    line = Line(peers, gq, z_sems)
+    go = Gather(peers, po, wo, False, o_recv, o_sent, OWN_BLOCK)
+    gu = Gather(peers, pu, wu, True, u_recv, u_sent, OWN_BLOCK)
+    gd = Gather(peers, pd, wd, False, d_recv, d_sent, OWN_BLOCK)
+    later = (go, gu, gd)
+    inward = Inward(peers, tokens, x, rows_buf, i_sems)
+    inward.load()
+    here = seg_out.at[pl.ds(2 * r, 2)]
+    small = [
+        pltpu.make_async_copy(feat, feat_out.at[:, pl.ds(0, f)], v_sems.at[0]),
+        pltpu.make_async_copy(slot, slot_out.at[pl.ds(0, 4)], v_sems.at[1]),
+        pltpu.make_async_copy(segments, here, v_sems.at[2]),
+        send(peers, "y", slot, slot_out.at[pl.ds(4, 4)], v_sems.at[3], v_sems.at[4]),
+    ]
+    for i in (1, 2, 3):
+        small.append(send(peers, i, feat, feat_out.at[:, pl.ds(i * f, f)], v_sems.at[3 + 2 * i], v_sems.at[4 + 2 * i]))
+        small.append(send(peers, i, segments, here, v_sems.at[9 + 2 * i], v_sems.at[10 + 2 * i]))
+
+    peers.meet(ALL_PEERS)
+    line.start()
+    gq.start()
+    for c in small:
+        c.start()
+    for g in later:
+        g.start()
+    line.wave(0)
+    inward.settle()
+    gq.relay((0, 2), (0, 4))
+    line.wave(1)
+    for g in later:
+        g.relay((0, 2), (0, 4))
+    line.wave(2)
+    inward.start(*inward.chunks)
     for s in (1, 2, 3):
-        g.relay((s, 0), (s - 1, 2), (s - 1, 4))
-    g.relay((3, 2), (3, 4))
+        gq.relay((s, 2), (s, 4))
     for s in range(4):
-        g.relay((s, 6))
-    g.finish()
-    a.finish()
-
-
-def first(tokens, piece):
+        gq.relay((s, 6))
+    for c in small:
+        c.wait()
+    for g in (gq, *later):
+        g.finish()
+    line.finish()
+    inward.finish()
+
+
+def first(tokens, segments, weights, vectors):
+    w_query, _, _, w_out, w_up, w_down = weights
+    width = 4 * tokens.shape[1]
+    heads = w_query.shape[1] // 4
+    units = w_up.shape[1] // 4
+    vmem = pl.BlockSpec(memory_space=pltpu.VMEM)
     return pl.pallas_call(
         first_kernel,
-        in_specs=[ANY, ANY],
-        out_specs=[ANY, ANY],
+        in_specs=[ANY, vmem] + [ANY] * 6 + [vmem],
+        out_specs=[ANY] * 8,
         out_shape=[
-            jax.ShapeDtypeStruct((SEQ, 4 * tokens.shape[1]), BF),
-            jax.ShapeDtypeStruct((4 * piece.shape[0], 8 * piece.shape[1]), BF),
-        ],
-        scratch_shapes=[DMA((32,)), DMA((32,)), DMA((4,)), DMA((4,))],
-        compiler_params=pltpu.CompilerParams(collective_id=0, has_side_effects=True),
+            jax.ShapeDtypeStruct((SEQ, width), BF),
+            jax.ShapeDtypeStruct((width, 24 * heads), BF),
+            jax.ShapeDtypeStruct((8 * heads, width), BF),
+            jax.ShapeDtypeStruct((width, 8 * units), BF),
+            jax.ShapeDtypeStruct((8 * units, width), BF),
+            jax.ShapeDtypeStruct((8, width), F32),
+            jax.ShapeDtypeStruct((8, 1, 3 * heads + units), F32),
+            jax.ShapeDtypeStruct((8, 8, 128), jnp.int32),
+        ],
+        scratch_shapes=[
+            pltpu.VMEM((width // 4, 3 * heads), BF),
+            pltpu.VMEM((heads, width // 4), BF),
+            pltpu.VMEM((width // 4, units), BF),
+            pltpu.VMEM((units, width // 4), BF),
+            pltpu.VMEM((SEQ, width // 4), BF),
+            pltpu.VMEM((8, width // 4), F32),
+            pltpu.VMEM((4, 1, 3 * heads + units), F32),
+            DMA((6,)),
+            *[DMA((32,))] * 8,
+            sems_of_exchange(),
+            DMA((20,)),
+            DMA((11,)),
+        ],
+        compiler_params=pltpu.CompilerParams(vmem_limit_bytes=VMEM_LIMIT, collective_id=0, has_side_effects=True),
         name="first",
-    )(tokens, piece)
+    )(tokens, segments, *weights, vectors)
 
 
 RB = 128
@@ -354,15 +573,16 @@
 
 
 def ff_fwd_kernel(
-    x_ref, att_ref, wo_ref, vec_ref, bu_ref, cot, wu_in, wd_in,
+    x_ref, att_ref, wo_ref, vec_ref, b_ref, cot, cot_first, wu_in, wd_in,
     wu, wd, act_ref, slope_ref, hlow_ref, normed1_ref, inv1_ref, out_ref, r2_ref, vg_ref,
-    acc, wu_buf, wd_buf, cot_buf, buf_sem, u_recv, u_sent, d_recv, d_sent, i_recv, i_sent,
+    acc, wu_buf, wd_buf, cot_buf, cot_own, buf_sem, u_recv, u_sent, d_recv, d_sent, i_sems, c_sem,
 ):
     j = pl.program_id(0)
     peers = Peers()
     gu = Gather(peers, None, wu, True, u_recv, u_sent, FAR)
     gd = Gather(peers, None, wd, False, d_recv, d_sent, DOWN_REST)
-    inward = Inward(peers, cot, cot_buf, i_recv, i_sent)
+    inward = Inward(peers, cot, cot_buf, cot_own, i_sems, range(1, CHUNKS))
+    early = pltpu.make_async_copy(cot_first, cot_buf.at[pl.ds(0, SEQ // CHUNKS), :], c_sem)
     n = wu_buf.shape[2]
 
     def fetch(t, slot):
@@ -374,16 +594,20 @@
 
     @pl.when(j == 0)
     def _():
-        peers.greet(ALL_PEERS)
+        peers.hello(ALL_PEERS)
         for t in range(2):
             for c in fetch(t, t):
                 c.start()
+        early.start()
+        inward.load()
+        acc[...] = jnp.zeros_like(acc)
+        peers.meet(ALL_PEERS)
         gd.emit(3, 0)
-        for s in range(3):
+        for s in (0, 1, 2):
             gu.emit(s, 2 if s % 2 == 0 else 4)
             gd.emit(s, 2 if s % 2 == 0 else 4)
         gu.emit(3, 4)
-        inward.start()
+        inward.start(*inward.chunks)
 
         def body(rows):
             v = x_ref[rows, :].astype(F32) + mm(att_ref[rows, :], wo_ref[...]) + vec_ref[0:1, :]
@@ -393,14 +617,12 @@
             hlow_ref[rows, :] = (normed * vec_ref[1:2, :] + vec_ref[2:3, :]).astype(BF)
 
         row_blocks(body)
-        acc[...] = jnp.zeros_like(acc)
         gd.relay((3, 2), (3, 4))
 
     @pl.when(j == 1)
     def _():
         gd.arrived(3, 3)
-        for s in range(4):
-            gu.relay((s, 6))
+        inward.settle()
 
     @pl.when(j == 2)
     def _():
@@ -408,8 +630,8 @@
 
     @pl.when(j == 4)
     def _():
-        for s in range(4):
-            gd.relay((s, 6))
+        for g in (gu, gd):
+            g.relay((0, 6), (1, 6), (2, 6), (3, 6))
 
     @pl.when(j == 5)
     def _():
@@ -422,7 +644,7 @@
         c.wait()
     w_up = wu_buf.at[slot]
     w_down = wd_buf.at[slot]
-    bias = bu_ref[...]
+    bias = b_ref[0, :, 384:]
     for i in range(SEQ // 256):
         rows = slice(i * 256, (i + 1) * 256)
         act, slope = gelu_and_slope(mm(hlow_ref[rows, :], w_up[...]) + bias)
@@ -439,6 +661,7 @@
     @pl.when(j == 7)
     def _():
         inward.finish()
+        early.wait()
         vg_ref[...] = jnp.zeros_like(vg_ref)
 
         def body(rows):
@@ -457,14 +680,7 @@
         gd.finish()
 
 
-ONCE = pl.Buffered(1)
-
-
-def const(*shape):
-    return pl.BlockSpec(shape, lambda j: (0,) * len(shape), pipeline_mode=ONCE)
-
-
-def ff_fwd(x, att, wo, vec, bu, cot, wu, wd):
+def ff_fwd(x, att, wo, vec, bu, cot, cot_first, wu, wd):
     width, units = wu.shape
     n = units // 8
     return pl.pallas_call(
@@ -475,7 +691,8 @@
             const(SEQ, width),
             const(width, width),
             const(8, width),
-            pl.BlockSpec((1, n), lambda j: (0, j)),
+            pl.BlockSpec((1, 1, bu.shape[2]), lambda j: (j, 0, 0)),
+            ANY,
             ANY,
             ANY,
             ANY,
@@ -504,30 +721,36 @@
             jax.ShapeDtypeStruct((SEQ, width), F32),
             jax.ShapeDtypeStruct((8, width), F32),
         ],
-        input_output_aliases={6: 0, 7: 1},
+        input_output_aliases={7: 0, 8: 1},
         scratch_shapes=[
             pltpu.VMEM((SEQ, width), F32),
             pltpu.VMEM((2, width, n), BF),
             pltpu.VMEM((2, n, width), BF),
             pltpu.VMEM((SEQ, width), BF),
+            pltpu.VMEM((SEQ - SEQ // CHUNKS, width // 4), BF),
             DMA((2, 2)),
             DMA((32,)),
             DMA((32,)),
             DMA((32,)),
             DMA((32,)),
-            DMA((4,)),
-            DMA((4,)),
+            sems_of_exchange(),
+            DMA,
         ],
         compiler_params=pltpu.CompilerParams(vmem_limit_bytes=VMEM_LIMIT, collective_id=2, has_side_effects=True),
         name="ff_fwd",
-    )(x, att, wo, vec, bu, cot, wu, wd)
+    )(x, att, wo, vec, bu, cot, cot_first, wu, wd)
 
 
 ORDER = (7, 6, 1, 3, 5, 0, 2, 4)
+PAIRS = (7, 6, 3, 2, 5, 4, 1, 0)
 
 
 def slot_at(j):
     return jnp.where(j < 2, 7 - j, jnp.where(j < 5, 2 * j - 3, 2 * j - 10))
+
+
+def pair_at(j):
+    return jnp.where(j < 2, 7 - j, jnp.where(j < 4, 5 - j, jnp.where(j < 6, 9 - j, 7 - j)))
 
 
 def sum_rows(dst, *srcs):
@@ -546,8 +769,6 @@
 
 
 class Fold:
-    SCRATCH = 12
-
     @staticmethod
     def scratch(a, b):
         return [
@@ -558,14 +779,14 @@
             DMA((12,)),
         ]
 
-    def __init__(self, peers, stage, land, corner, land_corner, sems):
-        self.peers, self.stage, self.land, self.corner, self.land_corner, self.sems = (
-            peers, stage, land, corner, land_corner, sems,
+    def __init__(self, peers, order, stage, land, corner, land_corner, sems):
+        self.peers, self.order, self.stage, self.land, self.corner, self.land_corner, self.sems = (
+            peers, order, stage, land, corner, land_corner, sems,
         )
         self.half = corner.shape[0] // 2
 
     def to_core(self, p):
-        k = (ORDER[p] - 1) // 2
+        k = (self.order[p] - 1) // 2
         return send(self.peers, "core", self.stage.at[p % 2], self.land.at[k], self.sems.at[4 + k], self.sems.at[k])
 
     def to_side(self, h):
@@ -573,18 +794,21 @@
         return send(self.peers, "xy"[1 - h], src, self.land_corner.at[h], self.sems.at[10 + h], self.sems.at[8 + h])
 
     def before(self, j):
-        for p in (2, 4, 5, 6):
+        for p in range(2, 8):
+            if self.order[p - 2] % 2 == 0:
+                continue
+
             @pl.when(j == p)
             def _(p=p):
                 self.to_core(p - 2).wait_send()
 
     def from_core(self, t):
         k = t // 2
-        self.to_core(ORDER.index(t + 1)).wait_recv()
+        self.to_core(self.order.index(t + 1)).wait_recv()
         return self.land.at[k]
 
-    def after(self, j, out):
-        for p, t in enumerate(ORDER):
+    def after(self, j, outs):
+        for p, t in enumerate(self.order):
             @pl.when(j == p)
             def _(p=p, t=t):
                 mine = self.stage.at[p % 2]
@@ -597,6 +821,7 @@
                     self.to_side(0).start()
                     self.to_side(1).start()
                     return
+                out = outs[t]
                 if t == 0:
                     sum_rows(out, mine, theirs)
                     return
@@ -608,30 +833,96 @@
                     sum_rows(out.at[rows, :], mine.at[rows, :], theirs.at[rows, :], *more)
 
     def finish(self):
+        for p in (6, 7):
+            if self.order[p] % 2:
+                self.to_core(p).wait_send()
         self.to_side(0).wait_send()
         self.to_side(1).wait_send()
 
 
 class Cross:
-    def __init__(self, peers, kept, own, land_x, land_y, sems):
-        self.peers, self.kept, self.own, self.land_x, self.land_y, self.sems = peers, kept, own, land_x, land_y, sems
-
-    def copies(self):
-        s = self.sems
-        return (
-            send(self.peers, "x", self.kept.at[1], self.land_x, s.at[0], s.at[1]),
-            send(self.peers, "y", self.kept.at[2], self.land_y, s.at[2], s.at[3]),
-            pltpu.make_async_copy(self.kept.at[0], self.own, s.at[4]),
+    def __init__(self, peers, for_x, for_y, land_x, land_y, sems, cuts=1):
+        self.peers, self.sems, self.cuts = peers, sems, cuts
+        self.ends = {"x": (for_x, land_x), "y": (for_y, land_y)}
+        self.n = land_x.shape[0] // cuts
+
+    def copy(self, way, h=0):
+        src, dst = self.ends[way]
+        rows = pl.ds(h * self.n, self.n)
+        at = 4 * h + 2 * "xy".index(way)
+        return send(self.peers, way, src.at[rows, :], dst.at[rows, :], self.sems.at[at], self.sems.at[at + 1])
+
+    def start(self, ways="xy", h=0):
+        for way in ways:
+            self.copy(way, h).start()
+
+    def finish(self, own, out):
+        for h in range(self.cuts):
+            for way in "xy":
+                self.copy(way, h).wait()
+        sum_rows(out, own, self.ends["x"][1], self.ends["y"][1])
+
+
+class Whole:
+    @staticmethod
+    def scratch(a, b):
+        return [
+            pltpu.VMEM((8 * a, b), BF),
+            pltpu.VMEM((4, a, b), BF),
+            pltpu.VMEM((4, a, b), BF),
+            pltpu.VMEM((2, a // 2, b), BF),
+            pltpu.VMEM((a, b), BF),
+            pltpu.VMEM((a, b), BF),
+            DMA((12,)),
+            DMA((4,)),
+        ]
+
+    def __init__(self, peers, total, land, kept, land_corner, land_x, land_y, sems, c_sems):
+        self.peers, self.total, self.land, self.kept, self.land_corner, self.sems = (
+            peers, total, land, kept, land_corner, sems,
         )
+        self.a = land.shape[1]
+        self.half = self.a // 2
+        self.cross = Cross(peers, kept.at[1], kept.at[2], land_x, land_y, c_sems)
+
+    def block(self, t):
+        return self.total.at[pl.ds(t * self.a, self.a), :]
+
+    def to_core(self, k):
+        return send(
+            self.peers, "core", self.block(2 * k + 1), self.land.at[k], self.sems.at[4 + k], self.sems.at[k]
+        )
+
+    def to_side(self, h):
+        src = self.kept.at[3, pl.ds(h * self.half, self.half), :]
+        return send(self.peers, "xy"[1 - h], src, self.land_corner.at[h], self.sems.at[10 + h], self.sems.at[8 + h])
 
     def start(self):
-        for c in self.copies():
-            c.start()
+        for k in (3, 1, 2, 0):
+            self.to_core(k).start()
+
+    def corner(self):
+        for k in (3, 1, 2, 0):
+            self.to_core(k).wait_recv()
+            sum_rows(self.kept.at[k], self.block(2 * k), self.land.at[k])
+            if k == 3:
+                self.to_side(0).start()
+                self.to_side(1).start()
+
+    def sides(self):
+        for h in range(2):
+            self.to_side(h).wait_recv()
+            rows = pl.ds(h * self.half, self.half)
+            mine = self.kept.at[1 + h, rows, :]
+            sum_rows(mine, mine, self.land_corner.at[h])
+        self.cross.start()
 
     def finish(self, out):
-        for c in self.copies():
-            c.wait()
-        sum_rows(out, self.own, self.land_x, self.land_y)
+        self.cross.finish(self.kept.at[0], out)
+        for k in range(4):
+            self.to_core(k).wait_send()
+        for h in range(2):
+            self.to_side(h).wait_send()
 
 
 class Deal:
@@ -653,6 +944,74 @@
         for s in (1, 2, 3):
             self.copy(s).wait()
         sum_rows(out, self.part(0), self.land.at[0], self.land.at[1], self.land.at[2])
+
+
+class LineDeal:
+    def __init__(self, peers, total, by_rows, land, tmp, sems):
+        self.peers, self.land, self.tmp, self.sems = peers, land, tmp, sems
+        self.part = Deal(peers, total, by_rows, None, None).part
+
+    def copy(self, up, b, row, src):
+        go = (b - row if up else row - b) - 1
+        at = (0 if up else 3) + go
+        return send(
+            self.peers, 1 if up else 3, src, self.land.at[0 if up else 1, go], self.sems.at[at], self.sems.at[6 + at]
+        )
+
+    def slot(self, b, row):
+        return (row - b) % 4
+
+    def first(self, up, b, row):
+        return self.copy(up, b, row, self.part(self.slot(b, row)))
+
+    def pass_on(self, up, b, row):
+        go = (b - row if up else row - b) - 1
+        tmp = self.tmp.at[0 if up else 1, go]
+        return self.copy(up, b, row, tmp), tmp
+
+    def got(self, up, b, row):
+        go = b - row if up else row - b
+        at = (0 if up else 3) + go
+        land = self.land.at[0 if up else 1, go]
+        send(self.peers, 1 if up else 3, land, land, self.sems.at[at], self.sems.at[6 + at]).wait_recv()
+        return land
+
+    STEPS = (((1, True, 3), (1, True, 2), (2, False, 0), (2, False, 1)), ((2, True, 3), (1, False, 0)))
+    STARTS = ((0, True, 3), (0, True, 2), (0, True, 1), (3, False, 0), (3, False, 1), (3, False, 2))
+
+    def when(self, row, run):
+        pl.when(self.peers.r == row)(run)
+
+    def start(self):
+        for row, up, b in self.STARTS:
+            self.when(row, lambda up=up, b=b, row=row: self.first(up, b, row).start())
+
+    def step(self, k):
+        for row, up, b in self.STEPS[k]:
+            def run(row=row, up=up, b=b):
+                land = self.got(up, b, row)
+                copy, tmp = self.pass_on(up, b, row)
+                sum_rows(tmp, land, self.part(self.slot(b, row)))
+                copy.start()
+
+            self.when(row, run)
+
+    def finish(self, out):
+        for row in range(4):
+            def run(row=row):
+                lands = []
+                if row > 0:
+                    lands.append(self.got(True, row, row))
+                if row < 3:
+                    lands.append(self.got(False, row, row))
+                sum_rows(out, self.part(0), *lands)
+
+            self.when(row, run)
+        for row, up, b in self.STARTS:
+            self.when(row, lambda up=up, b=b, row=row: self.first(up, b, row).wait_send())
+        for moves in self.STEPS:
+            for row, up, b in moves:
+                self.when(row, lambda up=up, b=b, row=row: self.pass_on(up, b, row)[0].wait_send())
 
 
 class Spread:
@@ -692,55 +1051,79 @@
 
 
 class Outward:
-    def __init__(self, peers, rows, block, sems, parts=(2, 1, 3, 0)):
-        self.peers, self.rows, self.block, self.sems, self.parts = peers, rows, block, sems, parts
-
-    def copy(self, s):
+    def __init__(self, peers, rows, block, buf, sems, parts=(2, 1, 3, 0)):
+        self.peers, self.rows, self.block, self.buf, self.sems = peers, rows, block, buf, sems
+        self.away = [s for s in parts if s]
+        self.stays = 0 in parts
+        self.n = SEQ // CHUNKS
+
+    def ends(self, s, first, count):
         f = self.block.shape[1]
-        src = self.rows.at[:, pl.ds(s * f, f)]
-        dst = self.block.at[pl.ds(pl.multiple_of(self.peers.r * SEQ, SEQ), SEQ), :]
-        if s == 0:
-            return pltpu.make_async_copy(src, dst, self.sems.at[0])
-        return send(self.peers, 4 - s, src, dst, self.sems.at[s], self.sems.at[4 + s])
-
-    def start(self):
-        for s in self.parts:
-            self.copy(s).start()
+        mine = pl.ds(pl.multiple_of(self.peers.r * SEQ + first * self.n, self.n), count * self.n)
+        return self.rows.at[pl.ds(first * self.n, count * self.n), pl.ds(s * f, f)], self.block.at[mine, :]
+
+    def copy(self, s, k):
+        return send(self.peers, 4 - s, *self.ends(s, k, 1), self.sems.at[0, s, k], self.sems.at[1, s, k])
+
+    def load(self):
+        return pltpu.make_async_copy(self.ends(0, 0, CHUNKS)[0], self.buf, self.sems.at[0, 0, 0])
+
+    def store(self):
+        src, dst = self.ends(0, 0, CHUNKS)
+        return pltpu.make_async_copy(src if self.buf is None else self.buf, dst, self.sems.at[1, 0, 0])
+
+    def start(self, *chunks):
+        for k in chunks:
+            for s in self.away:
+                self.copy(s, k).start()
+
+    def settle(self):
+        self.load().wait()
+        self.store().start()
 
     def finish(self):
-        for s in self.parts:
-            self.copy(s).wait()
+        if self.stays:
+            self.store().wait()
+        for k in range(CHUNKS):
+            for s in self.away:
+                self.copy(s, k).wait()
 
 
 def ff_down_bwd_kernel(
     r2_ref, wd_ref, act_ref, slope_ref, out, out_block, gp_ref, bu_ref, kept_ref,
-    gfed, stage, land, corner, land_corner, f_sems, o_sems,
+    gfed, out_own, stage, land, corner, land_corner, f_sems, o_sems,
 ):
     j = pl.program_id(0)
     peers = Peers()
-    outward = Outward(peers, out, out_block, o_sems, (2, 0))
-    fold = Fold(peers, stage, land, corner, land_corner, f_sems)
+    outward = Outward(peers, out, out_block, out_own, o_sems, (2, 0))
+    fold = Fold(peers, ORDER, stage, land, corner, land_corner, f_sems)
 
     @pl.when(j == 0)
     def _():
-        peers.greet(ALL_PEERS)
-        outward.start()
+        peers.hello(ALL_PEERS)
+        outward.load().start()
 
         def body(rows):
             gfed[rows, :] = r2_ref[rows, :].astype(BF)
 
         row_blocks(body)
-
-    bsum = jnp.zeros((1, bu_ref.shape[1]), F32)
+        peers.meet(ALL_PEERS)
+        outward.start(*range(CHUNKS))
+
+    bsum = jnp.zeros((1, bu_ref.shape[2]), F32)
     for i in range(SEQ // 256):
         rows = slice(i * 256, (i + 1) * 256)
         g = (mm_t(gfed[rows, :], wd_ref[...]) * slope_ref[rows, :].astype(F32)).astype(BF)
         gp_ref[rows, :] = g
         bsum += jnp.sum(g.astype(F32), axis=0, keepdims=True)
-    bu_ref[...] = jnp.broadcast_to(bsum, bu_ref.shape)
+    bu_ref[0] = bsum
     fold.before(j)
     stage[lax.rem(j, 2)] = tmm(act_ref[...], gfed[...]).astype(BF)
-    fold.after(j, kept_ref.at[0])
+    fold.after(j, {t: kept_ref.at[0] for t in (0, 2, 4)})
+
+    @pl.when(j == 1)
+    def _():
+        outward.settle()
 
     @pl.when(j == 7)
     def _():
@@ -768,16 +1151,21 @@
         out_specs=[
             ANY,
             pl.BlockSpec((SEQ, n), lambda j: (0, slot_at(j))),
-            pl.BlockSpec((8, n), lambda j: (0, slot_at(j))),
+            pl.BlockSpec((1, 1, n), lambda j: (slot_at(j), 0, 0)),
             kept_spec(n, width),
         ],
         out_shape=[
             jax.ShapeDtypeStruct((4 * SEQ, width // 4), BF),
             jax.ShapeDtypeStruct((SEQ, units), BF),
-            jax.ShapeDtypeStruct((8, units), F32),
+            jax.ShapeDtypeStruct((8, 1, n), F32),
             jax.ShapeDtypeStruct((3, n, width), BF),
         ],
-        scratch_shapes=[pltpu.VMEM((SEQ, width), BF), *Fold.scratch(n, width), DMA((8,))],
+        scratch_shapes=[
+            pltpu.VMEM((SEQ, width), BF),
+            pltpu.VMEM((SEQ, width // 4), BF),
+            *Fold.scratch(n, width),
+            sems_of_exchange(),
+        ],
         compiler_params=pltpu.CompilerParams(vmem_limit_bytes=VMEM_LIMIT, collective_id=3, has_side_effects=True),
         name="ff_down_bwd",
     )(r2, wd, act, slope, out)
@@ -790,23 +1178,31 @@
 ):
     j = pl.program_id(0)
     peers = Peers()
-    outward = Outward(peers, out, out_block, o_sems, (1, 3))
-    fold = Fold(peers, stage, land, corner, land_corner, f_sems)
-    cross = Cross(peers, kept_d, own_d, land_x, land_y, c_sems)
+    outward = Outward(peers, out, out_block, None, o_sems, (1, 3))
+    fold = Fold(peers, ORDER, stage, land, corner, land_corner, f_sems)
+    cross = Cross(peers, kept_d.at[1], kept_d.at[2], land_x, land_y, c_sems, 2)
+    load = pltpu.make_async_copy(kept_d.at[0], own_d, c_sems.at[8])
 
     @pl.when(j == 0)
     def _():
-        peers.greet(ALL_PEERS)
-        cross.start()
-        outward.start()
+        peers.hello(ALL_PEERS)
+        load.start()
         r1_ref[...] = r2_ref[...]
         for i in range(SEQ // 256):
             rows = slice(i * 256, (i + 1) * 256)
             hlow_t[:, rows] = jnp.transpose(hlow_ref[rows, :])
+        peers.meet(ALL_PEERS)
+        cross.start()
+        outward.start(*range(CHUNKS))
 
     fold.before(j)
     stage[lax.rem(j, 2)] = mm(hlow_t[...], gp_ref[...]).astype(BF)
-    fold.after(j, kept_ref.at[0])
+    fold.after(j, {t: kept_ref.at[0] for t in (0, 2, 4)})
+
+    @pl.when(j == 1)
+    def _():
+        cross.start(h=1)
+
     r1_ref[...] += mm_t(gp_ref[...], wu_ref[...])
 
     @pl.when(j == 7)
@@ -825,7 +1221,8 @@
             vg_ref[2:3, :] += jnp.sum(low.astype(F32), axis=0, keepdims=True)
 
         row_blocks(body)
-        cross.finish(own_ref)
+        load.wait()
+        cross.finish(own_d, own_ref)
         fold.finish()
         outward.finish()
 
@@ -871,8 +1268,8 @@
             pltpu.VMEM((n, width), BF),
             pltpu.VMEM((n, width), BF),
             pltpu.VMEM((n, width), BF),
-            DMA((5,)),
-            DMA((8,)),
+            DMA((9,)),
+            sems_of_exchange(),
         ],
         compiler_params=pltpu.CompilerParams(vmem_limit_bytes=VMEM_LIMIT, collective_id=4, has_side_effects=True),
         name="ff_up_bwd",
@@ -880,44 +1277,58 @@
 
 
 def attend_bwd_kernel(
-    gattn_ref, wo_ref, att_ref, qkv_ref, linv_ref, p_ref, x_ref, w_ref, r1, tot_d, kept_u,
-    xg_ref, gsum_ref, kept_q, kept_o, down_ref, up_ref,
-    x_t, acc, ds_ref, g_ref, a_sem,
-    q_stage, q_land, q_corner, q_land_corner, q_sems, o_stage, o_land, o_corner, o_land_corner, o_sems,
+    gattn_ref, wo_ref, att_ref, qkv_ref, linv_ref, p_ref, x_ref, att_all, tot_d, kept_u,
+    g_ref, gsum_ref, tot_q, tot_o, down_ref, up_ref,
+    x_t, ds_ref,
+    q_stage, q_land, q_corner, q_land_corner, q_sems,
+    q_kept, q_x, q_y, q_c, o_total, o_land, o_kept, o_land_corner, o_x, o_y, o_sems, o_c,
     zd_land, zd_sems, own_u, land_x, land_y, c_sems, tot_u, zu_land, zu_sems,
 ):
     j = pl.program_id(0)
     peers = Peers()
-    fold_q = Fold(peers, q_stage, q_land, q_corner, q_land_corner, q_sems)
-    fold_o = Fold(peers, o_stage, o_land, o_corner, o_land_corner, o_sems)
+    fold_q = Fold(peers, PAIRS, q_stage, q_land, q_corner, q_land_corner, q_sems)
+    whole_o = Whole(peers, o_total, o_land, o_kept, o_land_corner, o_x, o_y, o_sems, o_c)
+    cross_q = Cross(peers, q_kept.at[1], q_kept.at[2], q_x, q_y, q_c)
     deal_d = Deal(peers, tot_d, False, zd_land, zd_sems)
-    cross_u = Cross(peers, kept_u, own_u, land_x, land_y, c_sems)
+    cross_u = Cross(peers, kept_u.at[1], kept_u.at[2], land_x, land_y, c_sems)
     deal_u = Deal(peers, tot_u, True, zu_land, zu_sems)
-    load = pltpu.make_async_copy(r1, acc, a_sem)
+    load_u = pltpu.make_async_copy(kept_u.at[0], own_u, c_sems.at[4])
 
     @pl.when(j == 0)
     def _():
-        peers.greet(ALL_PEERS)
-        load.start()
-        cross_u.start()
-        deal_d.start()
+        load_u.start()
+        peers.hello(ALL_PEERS)
         for i in range(SEQ // 256):
             rows = slice(i * 256, (i + 1) * 256)
             x_t[:, rows] = jnp.transpose(x_ref[rows, :])
-        load.wait()
+        load_u.wait()
+        peers.meet(ALL_PEERS)
+        cross_u.start()
+        deal_d.start()
+        o_total[...] = tmm(att_all[...], gattn_ref[...]).astype(BF)
+        whole_o.start()
+
+    @pl.when(j == 1)
+    def _():
+        whole_o.corner()
+
+    @pl.when(j == 3)
+    def _():
+        whole_o.sides()
+
+    @pl.when(j == 6)
+    def _():
+        whole_o.finish(tot_o)
 
     @pl.when(j == 4)
     def _():
-        cross_u.finish(tot_u)
+        cross_u.finish(own_u, tot_u)
         deal_u.start()
         deal_d.finish(down_ref)
 
     lane = lax.broadcasted_iota(jnp.int32, (SEQ, 128), 1)
     scale = HD ** (-0.5)
-    fold_o.before(j)
     fold_q.before(j)
-    o_stage[lax.rem(j, 2)] = tmm(att_ref[...], gattn_ref[...]).astype(BF)
-    fold_o.after(j, kept_o.at[0])
     q = qkv_ref[:, 0:128]
     k = qkv_ref[:, 128:256]
     v = qkv_ref[:, 256:384]
@@ -942,23 +1353,26 @@
     g_ref[:, 0:128] = (jnp.where(lane < HD, dq[0], dq[1]) * scale).astype(BF)
     g_ref[:, 128:256] = (jnp.transpose(jnp.concatenate(dk_t, 0)) * scale).astype(BF)
     g_ref[:, 256:384] = jnp.transpose(jnp.concatenate(dv_t, 0)).astype(BF)
-    gsum_ref[...] = jnp.broadcast_to(jnp.sum(g_ref[...].astype(F32), axis=0, keepdims=True), gsum_ref.shape)
+    gsum_ref[0] = jnp.sum(g_ref[...].astype(F32), axis=0, keepdims=True)
     q_stage[lax.rem(j, 2)] = mm(x_t[...], g_ref[...]).astype(BF)
-    fold_q.after(j, kept_q.at[0])
-    acc[...] += mm_t(g_ref[...], w_ref[...])
+    fold_q.after(j, {t: q_kept.at[t // 2] for t in (0, 2, 4)})
+
+    @pl.when(j == PAIRS.index(2))
+    def _():
+        cross_q.start("x")
+
+    @pl.when(j == PAIRS.index(4))
+    def _():
+        cross_q.start("y")
 
     @pl.when(j == 7)
     def _():
-        def body(rows):
-            xg_ref[rows, :] = acc[rows, :].astype(BF)
-
-        row_blocks(body)
         deal_u.finish(up_ref)
-        fold_o.finish()
         fold_q.finish()
-
-
-def attend_bwd(gattn, wo, att, qkv, linv, p, x, w_qkv, r1, tot_d, kept_u):
+        cross_q.finish(q_kept.at[0], tot_q)
+
+
+def attend_bwd(gattn, wo, att, qkv, linv, p, x, tot_d, kept_u):
     width = x.shape[1]
     heads = 128
     n = tot_d.shape[0]
@@ -967,41 +1381,41 @@
         grid=(8,),
         in_specs=[
             const(SEQ, width),
-            pl.BlockSpec((heads, width), lambda j: (slot_at(j), 0)),
-            pl.BlockSpec((SEQ, heads), lambda j: (0, slot_at(j))),
-            pl.BlockSpec((SEQ, 3 * heads), lambda j: (0, slot_at(j))),
-            pl.BlockSpec((SEQ, heads), lambda j: (0, slot_at(j))),
-            pl.BlockSpec((2, SEQ, SEQ), lambda j: (slot_at(j), 0, 0)),
+            pl.BlockSpec((heads, width), lambda j: (pair_at(j), 0)),
+            pl.BlockSpec((SEQ, heads), lambda j: (0, pair_at(j))),
+            pl.BlockSpec((SEQ, 3 * heads), lambda j: (0, pair_at(j))),
+            pl.BlockSpec((SEQ, heads), lambda j: (0, pair_at(j))),
+            pl.BlockSpec((2, SEQ, SEQ), lambda j: (pair_at(j), 0, 0)),
             const(SEQ, width),
-            pl.BlockSpec((width, 3 * heads), lambda j: (0, slot_at(j))),
-            ANY,
+            const(SEQ, width),
             const(n, width),
             ANY,
         ],
         out_specs=[
-            const(SEQ, width),
-            pl.BlockSpec((8, 3 * heads), lambda j: (0, slot_at(j))),
-            kept_spec(width, 3 * heads),
-            kept_spec(heads, width),
+            pl.BlockSpec((SEQ, 3 * heads), lambda j: (0, pair_at(j))),
+            pl.BlockSpec((1, 1, 3 * heads), lambda j: (pair_at(j), 0, 0)),
+            const(width, 3 * heads),
+            const(heads, width),
             const(n, width // 4),
             const(width // 4, n),
         ],
         out_shape=[
-            jax.ShapeDtypeStruct((SEQ, width), BF),
-            jax.ShapeDtypeStruct((8, 24 * heads), F32),
-            jax.ShapeDtypeStruct((3, width, 3 * heads), BF),
-            jax.ShapeDtypeStruct((3, heads, width), BF),
+            jax.ShapeDtypeStruct((SEQ, 24 * heads), BF),
+            jax.ShapeDtypeStruct((8, 1, 3 * heads), F32),
+            jax.ShapeDtypeStruct((width, 3 * heads), BF),
+            jax.ShapeDtypeStruct((heads, width), BF),
             jax.ShapeDtypeStruct((n, width // 4), BF),
             jax.ShapeDtypeStruct((width // 4, n), BF),
         ],
         scratch_shapes=[
             pltpu.VMEM((width, SEQ), BF),
-            pltpu.VMEM((SEQ, width), F32),
             pltpu.VMEM((2, SEQ, SEQ), BF),
-            pltpu.VMEM((SEQ, 3 * heads), BF),
-            DMA,
             *Fold.scratch(width, 3 * heads),
-            *Fold.scratch(heads, width),
+            pltpu.VMEM((3, width, 3 * heads), BF),
+            pltpu.VMEM((width, 3 * heads), BF),
+            pltpu.VMEM((width, 3 * heads), BF),
+            DMA((4,)),
+            *Whole.scratch(heads, width),
             pltpu.VMEM((3, n, width // 4), BF),
             DMA((6,)),
             pltpu.VMEM((width, n), BF),
@@ -1014,22 +1428,51 @@
         ],
         compiler_params=pltpu.CompilerParams(vmem_limit_bytes=VMEM_LIMIT, collective_id=5, has_side_effects=True),
         name="attend_bwd",
-    )(gattn, wo, att, qkv, linv, p, x, w_qkv, r1, tot_d, kept_u)
+    )(gattn, wo, att, qkv, linv, p, x, att, tot_d, kept_u)
 
 
 def last_kernel(
-    xg, kept_q, kept_o, own_d, own_u, vec_ref,
+    tot_q, tot_o, own_d, own_u, g_part, u_part, vec1, vec2, g, w, r1,
     x_block, gq, go, gd, gu, slot_out, feat_ref,
-    q_own, q_x, q_y, q_c, q_tot, q_land, q_z, q_sum, o_own, o_x, o_y, o_c, o_tot, o_land, o_z, o_sum,
-    v1, v2, v3, l1, l2, l3, l4, v_own, v_sems, out_sems, s_sems,
+    g_buf, w_buf, acc, xg, ld_sems,
+    q_land, q_tmp, q_z, q_sum, o_land, o_tmp, o_z, o_sum,
+    vec_ref, v1, v2, v3, l1, l2, l3, l4, v_own, v_sems, out_sems, s_sems,
 ):
     peers = Peers()
-    peers.greet(ALL_PEERS)
-    outward = Outward(peers, xg, x_block, out_sems)
-    cross_q = Cross(peers, kept_q, q_own, q_x, q_y, q_c)
-    cross_o = Cross(peers, kept_o, o_own, o_x, o_y, o_c)
-    deal_q = Deal(peers, q_tot, True, q_land, q_z)
-    deal_o = Deal(peers, o_tot, False, o_land, o_z)
+    outward = Outward(peers, xg, x_block, None, out_sems)
+    deal_q = LineDeal(peers, tot_q, True, q_land, q_tmp, q_z)
+    deal_o = LineDeal(peers, tot_o, False, o_land, o_tmp, o_z)
+    loads = (
+        pltpu.make_async_copy(w, w_buf, ld_sems.at[0]),
+        pltpu.make_async_copy(g, g_buf, ld_sems.at[1]),
+        pltpu.make_async_copy(r1, acc, ld_sems.at[2]),
+    )
+    peers.hello(ALL_PEERS)
+    for c in loads:
+        c.start()
+
+    def products(k):
+        rows = slice(k * (SEQ // CHUNKS), (k + 1) * (SEQ // CHUNKS))
+        xg[rows, :] = (mm_t(g_buf[rows, :], w_buf[...]) + acc[rows, :]).astype(BF)
+        outward.start(k)
+
+    vec_ref[...] = jnp.zeros_like(vec_ref)
+    heads3, units = g_part.shape[2], u_part.shape[2]
+    for k, t in enumerate((0, 4, 2, 6, 1, 5, 3, 7)):
+        k = k if k < 4 else k + 8
+        for i in range(heads3 // 128):
+            vec_ref[k, i : i + 1, :] = g_part[t, :, i * 128 : (i + 1) * 128]
+        for i in range(units // 128):
+            at = heads3 // 128 + i
+            vec_ref[k, at : at + 1, :] = u_part[t, :, i * 128 : (i + 1) * 128]
+    f = vec1.shape[1] // 4
+    rows = [(vec1, 2), (vec1, 0), (vec1, 1), (vec2, 2), (vec2, 0), (vec2, 1)]
+    for k in range(4):
+        for v, (ref, row) in enumerate(rows):
+            for i in range(f // 128):
+                at = v * (f // 128) + i
+                first = k * f + i * 128
+                vec_ref[4 + 2 * k + at // 8, at % 8 : at % 8 + 1, :] = ref[row : row + 1, first : first + 128]
 
     def rows_at(ref):
         n = ref.shape[0] // 4
@@ -1058,75 +1501,72 @@
         src = v3.at[pl.ds(4 + 2 * (4 - i), 2)]
         to_rows.append(send(peers, i, src, l4.at[i - 1, pl.ds(1, 2)], v_sems.at[8 + 4 * i], v_sems.at[9 + 4 * i]))
 
+    peers.meet(ALL_PEERS)
+    deal_o.start()
+    deal_q.start()
     to_core.start()
-    cross_o.start()
-    cross_q.start()
     spread_d.start()
     spread_u.start()
-    outward.start()
-
+    for c in loads:
+        c.wait()
+    products(0)
+    deal_o.step(0)
+    deal_q.step(0)
+    products(1)
     to_core.wait()
     v1[0:4] = vec_ref[0:4] + l1[8:12]
     v1[4:12] = vec_ref[4:12] + l1[0:8]
     to_x.start()
+    deal_o.step(1)
+    deal_q.step(1)
+    products(2)
+    products(3)
+    outward.store().start()
     to_x.wait()
     v2[0:2] = v1[0:2] + l2[0:2]
     v2[4:12] = v1[4:12] + l2[2:10]
     v2[2:4] = v1[2:4]
     to_y.start()
-    cross_o.finish(o_tot)
-    deal_o.start()
+    spread_d.relay()
+    spread_u.relay()
+    deal_o.finish(o_sum)
+    spread_o.start()
+    deal_q.finish(q_sum)
+    for sp in spread_q:
+        sp.start()
     to_y.wait()
     v3[0:1] = v2[0:1] + l3[0:1]
     v3[4:12] = v2[4:12] + l3[3:11]
     for c in to_rows:
         c.start()
-    cross_q.finish(q_tot)
-    deal_q.start()
+    spread_o.relay()
+    for sp in spread_q:
+        sp.relay()
     for c in to_rows:
         c.wait()
     v_own[...] = v3[0] + l4[0, 0] + l4[1, 0] + l4[2, 0]
     feat_ref[...] = v3[4:6] + l4[0, 1:3] + l4[1, 1:3] + l4[2, 1:3]
     spread_v.start()
-    spread_d.relay()
-    spread_u.relay()
-    deal_o.finish(o_sum)
-    spread_o.start()
     spread_v.relay()
-    deal_q.finish(q_sum)
-    for sp in spread_q:
-        sp.start()
-    spread_o.relay()
-    for sp in spread_q:
-        sp.relay()
     for sp in (spread_d, spread_u, spread_o, spread_v, *spread_q):
         sp.finish()
     outward.finish()
 
 
-def last(xg, kept_q, kept_o, own_d, own_u, vec):
-    width = xg.shape[1]
+def last(tot_q, tot_o, own_d, own_u, g_part, u_part, vec1, vec2, g, w, r1):
+    width = r1.shape[1]
     part = width // 4
     n = own_d.shape[0]
-    heads = kept_o.shape[1]
+    heads = tot_o.shape[0]
     vmem = pl.BlockSpec(memory_space=pltpu.VMEM)
 
     def bufs(a, b, by_rows):
         piece = (a // 4, b) if by_rows else (a, b // 4)
-        return [
-            pltpu.VMEM((a, b), BF),
-            pltpu.VMEM((a, b), BF),
-            pltpu.VMEM((a, b), BF),
-            DMA((5,)),
-            pltpu.VMEM((a, b), BF),
-            pltpu.VMEM((3, *piece), BF),
-            DMA((6,)),
-            pltpu.VMEM(piece, BF),
-        ]
+        return [pltpu.VMEM((2, 3, *piece), BF), pltpu.VMEM((2, 2, *piece), BF), DMA((12,)), pltpu.VMEM(piece, BF)]
 
     return pl.pallas_call(
         last_kernel,
-        in_specs=[ANY, ANY, ANY, ANY, ANY, vmem],
+        in_specs=[vmem] * 8 + [ANY] * 3,
         out_specs=[ANY, ANY, ANY, ANY, ANY, ANY, vmem],
         out_shape=[
             jax.ShapeDtypeStruct((4 * SEQ, part), BF),
@@ -1138,8 +1578,14 @@
             jax.ShapeDtypeStruct((2, 8, 128), F32),
         ],
         scratch_shapes=[
+            pltpu.VMEM((SEQ, 24 * heads), BF),
+            pltpu.VMEM((width, 24 * heads), BF),
+            pltpu.VMEM((SEQ, width), F32),
+            pltpu.VMEM((SEQ, width), BF),
+            DMA((3,)),
             *bufs(width, 3 * heads, True),
             *bufs(heads, width, False),
+            pltpu.VMEM((16, 8, 128), F32),
             pltpu.VMEM((12, 8, 128), F32),
             pltpu.VMEM((12, 8, 128), F32),
             pltpu.VMEM((12, 8, 128), F32),
@@ -1149,96 +1595,47 @@
             pltpu.VMEM((3, 3, 8, 128), F32),
             pltpu.VMEM((8, 128), F32),
             DMA((24,)),
-            DMA((8,)),
+            sems_of_exchange(),
             DMA((7, 7)),
         ],
         compiler_params=pltpu.CompilerParams(vmem_limit_bytes=VMEM_LIMIT, collective_id=6, has_side_effects=True),
         name="last",
-    )(xg, kept_q, kept_o, own_d, own_u, vec)
-
-
-class Ring:
-    def __init__(self):
-        self.r = lax.axis_index("row")
-        self.c = lax.axis_index("col")
-        self.d = lax.axis_index("dp")
-        self.rows = lax.axis_size("row")
-
-    def shift(self, v, s):
-        n = self.rows
-        return lax.ppermute(v, "row", [(i, (i + s) % n) for i in range(n)])
-
-    def y(self, v):
-        return lax.ppermute(v, "col", [(0, 1), (1, 0)])
-
-    def absolute(self, quarters):
-        a = jnp.where(self.d % 2 == 1, quarters[jnp.array([1, 0, 3, 2])], quarters)
-        return jnp.where(self.d // 2 == 1, jnp.concatenate([a[2:], a[:2]], 0), a)
-
-
-def quarter(v, d, axis):
-    n = v.shape[axis] // 4
-    return lax.dynamic_slice_in_dim(v, d * n, n, axis)
+    )(tot_q, tot_o, own_d, own_u, g_part, u_part, vec1, vec2, g, w, r1)
 
 
 def whole_sequences(
     tokens, segments, w_query, b_query, w_key, w_value, b_value, w_out, b_out, norm1_gain, norm1_shift,
     w_up, b_up, w_down, b_down, norm2_gain, norm2_shift, cotangent,
 ):
-    ring = Ring()
-    r, c, d = ring.r, ring.c, ring.d
-    R, C = lax.axis_size("row"), lax.axis_size("col")
+    R = lax.axis_size("row")
     feat = tokens.shape[1]
-
-    pairs = []
-    for row in range(R):
-        for col in range(C):
-            n = col * R + row
-            pairs.append((n, row * C + col))
-    seg = lax.ppermute(segments, ("row", "col"), pairs)
-    seg = lax.dynamic_slice_in_dim(seg, ((c * R + r) % C) * SEQ, SEQ, 0)
-    ids = jnp.where(seg == 0, -1 - jnp.arange(SEQ, dtype=jnp.int32), seg)
-    seg_col, seg_row = ids[:, None], ids[None, :]
-
-    qkv_piece = jnp.concatenate([quarter(w, d, 1) for w in (w_query, w_key, w_value)], 1)
-    x, w_qkv = first(tokens, qkv_piece)
-
-    feat_vec = jnp.stack([b_out, norm1_gain, norm1_shift, b_down, norm2_gain, norm2_shift, b_out, b_out])
-    feat_all = jnp.concatenate([feat_vec] + [ring.shift(feat_vec, s) for s in range(1, R)], 1).astype(F32)
     hq = b_query.shape[0] // 4
     unit = b_up.shape[0] // 4
-    slot_vec = jnp.concatenate(
-        [b_query.reshape(4, hq), jnp.zeros((4, hq), BF), b_value.reshape(4, hq), b_up.reshape(4, unit)], 1
-    )
-    slot_vec = ring.absolute(slot_vec)
-    slot_vec = jnp.concatenate([slot_vec, ring.y(slot_vec)], 0).astype(F32)
-    b_qkv = slot_vec[:, : 3 * hq].reshape(1, -1)
-    bu = slot_vec[:, 3 * hq :].reshape(1, -1)
-
-    qkv, att, prob, linv, wo, wu, wd = attend_fwd(
-        x, w_qkv, b_qkv, seg_col, seg_row, quarter(w_out, d, 0), quarter(w_up, d, 1), quarter(w_down, d, 0)
-    )
+    vectors = (b_out, norm1_gain, norm1_shift, b_down, norm2_gain, norm2_shift, b_query, b_value, b_up)
+    vectors = jnp.concatenate(vectors).astype(F32).reshape(1, -1)
+    x, w_qkv, wo, wu, wd, feat_all, b_slot, seg = first(
+        tokens,
+        segments.reshape(2, 8, 128),
+        (w_query, w_key, w_value, w_out, w_up, w_down),
+        vectors,
+    )
+
+    qkv, att, prob, linv, wo, wu, wd, cot_first = attend_fwd(x, w_qkv, b_slot, seg, cotangent, wo, wu, wd)
     wu, wd, act, slope, hidden_low, normed1, inv1, output, grad_r2, vg2 = ff_fwd(
-        x, att, wo, feat_all, bu, cotangent, wu, wd
+        x, att, wo, feat_all, b_slot, cotangent, cot_first, wu, wd
     )
 
     out_block, grad_pre, bu_part, kept_d = ff_down_bwd(grad_r2, wd, act, slope, output)
     out_block, grad_r1, grad_attn, vg1, kept_u, tot_d = ff_up_bwd(
         grad_r2, hidden_low, grad_pre, wu, normed1, inv1, feat_all, output, out_block, kept_d
     )
-    x_grad, g_part, kept_q, kept_o, own_d, own_u = attend_bwd(
-        grad_attn, wo, att, qkv, linv, prob, x, w_qkv, grad_r1, tot_d, kept_u
-    )
-
-    slot_grad = jnp.concatenate([g_part[0].reshape(8, 3 * hq), bu_part[0].reshape(8, unit)], 1)
-    slot_grad = jnp.pad(slot_grad, ((0, 0), (0, 1024 - slot_grad.shape[1]))).reshape(8, 8, 128)
-    feat_grad = jnp.stack([vg1[2], vg1[0], vg1[1], vg2[2], vg2[0], vg2[1]])
-    feat_grad = feat_grad.reshape(6, R, feat).transpose(1, 0, 2).reshape(R, 6 * feat)
-    feat_grad = jnp.pad(feat_grad, ((0, 0), (0, 2048 - 6 * feat))).reshape(8, 8, 128)
-    pick = [slot_grad[t : t + 1] for t in (0, 4, 2, 6)]
-    tiles = jnp.concatenate(pick + [feat_grad] + [slot_grad[t : t + 1] for t in (1, 5, 3, 7)], 0)
-
-    x_grad_block, gq, go, gd, gu, slot_sum, own = last(x_grad, kept_q, kept_o, own_d, own_u, tiles)
+    g_qkv, g_part, tot_q, tot_o, own_d, own_u = attend_bwd(
+        grad_attn, wo, att, qkv, linv, prob, x, tot_d, kept_u
+    )
+
+    x_grad_block, gq, go, gd, gu, slot_sum, own = last(
+        tot_q, tot_o, own_d, own_u, g_part, bu_part, vg1, vg2, g_qkv, w_qkv, grad_r1
+    )
     wq_grad, wk_grad, wv_grad = [gq[:, i * 4 * hq : (i + 1) * 4 * hq].astype(F32) for i in range(3)]
     w_out_grad, w_up_grad, w_down_grad = go.astype(F32), gu.astype(F32), gd.astype(F32)
     slot_sum = slot_sum.reshape(4, 1024)

time: 508 us -> 443 us (0.87)
  Pallas kernels: 460 us -> 422 us
  local copies, waits for them, and re-layouts: 25.8 us -> 12 us
  starting transfers between devices: 9.04 us -> 0 us
    pallas_call x3, Pallas kernels: 221 us -> 205 us  [the longest x1 72.3 us: first(): pl.pallas_call(first_kernel, in_specs=[ANY, vmem] + [ANY] * 6 + [vmem], o...]
    pallas_call x1, Pallas kernels: 72.9 us -> 63.6 us  [ff_fwd(): pl.pallas_call(ff_fwd_kernel, grid=(8,), in_specs=[const(SEQ, width), con...]
    ppermute x5 -> x0, starting transfers between devices: 9.04 us -> none  [the longest x3 6.11 us: shift(): return lax.ppermute(v, 'row', [(i, (i + s) % n) for i in range(n)])]
    pallas_call x1, Pallas kernels: 52.9 us -> 46.4 us  [ff_up_bwd(): pl.pallas_call(ff_up_bwd_kernel, grid=(8,), in_specs=[const(SEQ, width),...]
    pallas_call x1, Pallas kernels: 81.3 us -> 75.6 us  [attend_bwd(): pl.pallas_call(attend_bwd_kernel, grid=(8,), in_specs=[const(SEQ, width),...]
    dynamic_slice x5 -> x0, local copies, waits for them, and re-layouts: 5.59 us -> none  [quarter(): return lax.dynamic_slice_in_dim(v, d * n, n, axis)]
  transfers between devices with their start and end apart: 5 -> 0, of which waited for: 0 -> 0; matrix products, arithmetic and copies ran while one was open for 2% -> 0% of each run, Pallas kernels for 14% -> 0%
where the time goes in v4:
time: 443 us
  Pallas kernels  422 us (95%)
  local copies, waits for them, and re-layouts  12 us (3%)
  other arithmetic  7.84 us (2%)
    pallas_call x1, Pallas kernels, attend_bwd(): pl.pallas_call(attend_bwd_kernel, grid=(8,), in_specs=[const(SEQ, width),...  75.6 us
    pallas_call x1, Pallas kernels, first(): pl.pallas_call(first_kernel, in_specs=[ANY, vmem] + [ANY] * 6 + [vmem], o...  72.3 us
    pallas_call x1, Pallas kernels, last(): pl.pallas_call(last_kernel, in_specs=[vmem] * 8 + [ANY] * 3, out_specs=[A...  71 us
    pallas_call x1, Pallas kernels, ff_fwd(): pl.pallas_call(ff_fwd_kernel, grid=(8,), in_specs=[const(SEQ, width), con...  63.6 us
    pallas_call x1, Pallas kernels, attend_fwd(): pl.pallas_call(attend_fwd_kernel, grid=(slots,), in_specs=[const(SEQ, x.s...  61.8 us
    pallas_call x1, Pallas kernels, ff_up_bwd(): pl.pallas_call(ff_up_bwd_kernel, grid=(8,), in_specs=[const(SEQ, width),...  46.4 us
    pallas_call x1, Pallas kernels, ff_down_bwd(): pl.pallas_call(ff_down_bwd_kernel, grid=(8,), in_specs=[const(SEQ, width)...  31.2 us
    unnamed x21, local copies, waits for them, and re-layouts  9.33 us

profile of v4, /device:TPU:0, one launch (start us, length us, event | category | flops | bytes accessed | tf_op | source)
XLA Modules:
  0.0 442.6 jit_solution(14272298431773307645)
XLA Ops:
  0.7 0.7 constant_dynamic-update-slice_fusion.8
  1.3 0.7 constant_dynamic-update-slice_fusion.7
  2.0 0.7 constant_dynamic-update-slice_fusion.6
  2.6 0.7 constant_dynamic-update-slice_fusion.5
  3.3 0.7 constant_dynamic-update-slice_fusion.4
  4.0 0.7 constant_dynamic-update-slice_fusion.3
  4.6 0.7 constant_dynamic-update-slice_fusion.2
  5.3 0.7 constant_dynamic-update-slice_fusion.1
  6.0 0.7 constant_dynamic-update-slice_fusion
  6.7 0.6 convert_element_type.28.vectors
  7.3 72.3 %first.1 = (bf16[1024,1024]{1,0:T(8,128)(2,1)}, bf16[1024,3072]{1,0:T(8,128)(2,1)}, bf16[1024,1024]{1,0:T(8,128)(2,1)}, bf16[1024,4096]{1,0:T(8,128)(2,1)}, bf16...) custom-call(bf16[4096,256]{1,0:T(8,128)(2,1)} %tokens.1, ...), custom_call_target="tpu_custom_call" | custom-call | tf_op jit(solution)/shard_map/first/pallas_call | solution.py:508
  79.7 61.8 %attend_fwd.1 = (bf16[1024,3072]{1,0:T(8,128)(2,1)}, bf16[1024,1024]{1,0:T(8,128)(2,1)}, bf16[16,1024,1024]{2,1,0:T(8,128)(2,1)}, f32[1024,1024]{1,0:T(8,128)}, ...) custom-call(bf16[1024,1024]{1,0:T(8,128)(2,1)} %get-tuple-element.66, ...), custom_call_target="tpu_custom_call", output_to_operand_aliasing={{4}: (5, {}), {5}: (6, {}), {6}: (7, {})} | custom-call | tf_op jit(solution)/shard_map/attend_fwd/pallas_call | solution.py:138
  141.5 63.6 %ff_fwd.1 = (bf16[1024,4096]{1,0:T(8,128)(2,1)}, bf16[4096,1024]{1,0:T(8,128)(2,1)}, bf16[1024,4096]{1,0:T(8,128)(2,1)}, bf16[1024,4096]{1,0:T(8,128)(2,1)}, bf1...) custom-call(bf16[1024,1024]{1,0:T(8,128)(2,1)} %get-tuple-element.66, ...), custom_call_target="tpu_custom_call", output_to_operand_aliasing={{0}: (7, {}), {1}: (8, {})} | custom-call | tf_op jit(solution)/shard_map/ff_fwd/pallas_call | solution.py:686
  205.1 31.2 %ff_down_bwd.1 = (bf16[4096,256]{1,0:T(8,128)(2,1)}, bf16[1024,4096]{1,0:T(8,128)(2,1)}, f32[8,1,512]{2,1,0:T(1,128)}, bf16[3,512,1024]{2,1,0:T(8,128)(2,1)}) custom-call(f32[1024,1024]{1,0:T(8,128)} %get-tuple-element.79.r2_ref, bf16[4096,1024]{1,0:T(8,128)(2,1)} %get-tuple-element.81.wd_ref, bf16[1024,4096]{1,0:T(8,128)(2,1)} %get-tuple-element.82.act_ref, ...), custom_call_target="tpu_custom_call" | custom-call | tf_op jit(solution)/shard_map/ff_down_bwd/pallas_call | solution.py:1141
  236.3 46.4 %ff_up_bwd.1 = (bf16[4096,256]{1,0:T(8,128)(2,1)}, f32[1024,1024]{1,0:T(8,128)}, bf16[1024,1024]{1,0:T(8,128)(2,1)}, f32[8,1024]{1,0:T(8,128)}, bf16[3,1024,512]...) custom-call(f32[1024,1024]{1,0:T(8,128)} %get-tuple-element.79.r2_ref, ...), custom_call_target="tpu_custom_call", output_to_operand_aliasing={{0}: (8, {})} | custom-call | tf_op jit(solution)/shard_map/ff_up_bwd/pallas_call | solution.py:1233
  282.7 75.6 %attend_bwd.1 = (bf16[1024,3072]{1,0:T(8,128)(2,1)}, f32[8,1,384]{2,1,0:T(1,128)}, bf16[1024,384]{1,0:T(8,128)(2,1)}, bf16[128,1024]{1,0:T(8,128)(2,1)}, bf16[51...) custom-call(bf16[1024,1024]{1,0:T(8,128)(2,1)} %get-tuple-element.92.gattn_ref, bf16[1024,1024]{1,0:T(8,128)(2,1)} %get-tuple-element.74.wo_ref, ...), custom_call_target="tpu_custom_call" | custom-call | tf_op jit(solution)/shard_map/attend_bwd/pallas_call | solution.py:1379
  358.4 71.0 %last.1 = (bf16[4096,256]{1,0:T(8,128)(2,1)}, bf16[256,1536]{1,0:T(8,128)(2,1)}, bf16[512,256]{1,0:T(8,128)(2,1)}, bf16[2048,256]{1,0:T(8,128)(2,1)}, bf16[256,2...) custom-call(bf16[1024,384]{1,0:T(8,128)(2,1)} %get-tuple-element.98.tot_q, ...), custom_call_target="tpu_custom_call" | custom-call | tf_op jit(solution)/shard_map/last/pallas_call | solution.py:1567
  429.4 0.0 copy-start.3
  429.4 1.4 fusion
  430.8 0.7 copy.44
  431.5 0.6 slice_bitcast_fusion.1
  432.1 0.6 copy.42
  432.7 1.9 convert_element_type.32
  434.6 2.3 slice_convert_fusion
  436.9 0.0 copy-done.3
  436.9 1.6 convert_element_type.33
  438.5 0.0 copy-done.2
  438.5 1.5 convert_element_type.34
  440.0 0.0 copy-done
  440.0 1.3 copy.61
  441.3 0.0 copy-done.1
  441.3 1.3 copy.62
  (4 shorter events, 0.0 us)
Async XLA Ops:
  429.4 7.5 %copy-start.3 = (bf16[256,2048]{1,0:T(8,128)(2,1)S(1)}, bf16[256,2048]{1,0:T(8,128)(2,1)}, u32[]{:S(2)}) copy-start(bf16[256,2048]{1,0:T(8,128)(2,1)} %get-tuple-element.113) | copy-start | bytes 3145732
  432.7 5.7 %copy-start.2 = (bf16[2048,256]{1,0:T(8,128)(2,1)S(1)}, bf16[2048,256]{1,0:T(8,128)(2,1)}, u32[]{:S(2)}) copy-start(bf16[2048,256]{1,0:T(8,128)(2,1)} %get-tuple-element.114) | copy-start | bytes 3145732
  436.9 3.0 copy-start
  438.5 2.8 copy-start.1

commit v5 on v4

--- a/solution.py
+++ b/solution.py
@@ -43,20 +43,28 @@
     return jax.nn.gelu(v, approximate=False)
 
 
-def attend_rows(qkv_ref, seg_col_ref, seg_row, o_ref, p_ref, linv_ref, i):
+def attend_rows(qkv_ref, seg_col_ref, seg_row, o_ref, p_ref, linv_ref, hook):
     lane = lax.broadcasted_iota(jnp.int32, (QB, 128), 1)
     scale = HD ** (-0.5) * math.log2(math.e)
-    rows = slice(i * QB, (i + 1) * QB)
-    q = qkv_ref[rows, 0:128]
     k = qkv_ref[:, 128:256]
     v = qkv_ref[:, 256:384]
-    seg_col = seg_col_ref[rows, 0:1]
+    units = [(i, h) for i in range(SEQ // QB) for h in range(2)]
+
+    def scores(i, h):
+        q = qkv_ref[i * QB : (i + 1) * QB, 0:128]
+        mine = (lane < HD) if h == 0 else (lane >= HD)
+        return mm_t(jnp.where(mine, q, jnp.zeros_like(q)), k)
+
+    ahead = scores(*units[0])
     outs = []
-    for h in range(2):
-        mine = (lane < HD) if h == 0 else (lane >= HD)
-        qm = jnp.where(mine, q, jnp.zeros_like(q))
-        s = mm_t(qm, k)
-        s = jnp.where(seg_col == seg_row, s * scale, NEG)
+    for at, (i, h) in enumerate(units):
+        rows = slice(i * QB, (i + 1) * QB)
+        if h == 0:
+            hook(i)
+        s = ahead
+        if at + 1 < len(units):
+            ahead = scores(*units[at + 1])
+        s = jnp.where(seg_col_ref[rows, 0:1] == seg_row, s * scale, NEG)
         top = jnp.max(s, axis=1, keepdims=True)
         p = jnp.exp2(s - top)
         total = jnp.sum(p, axis=1, keepdims=True)
@@ -64,25 +72,28 @@
         p_ref[h, rows, :] = pb
         inv = 1.0 / total
         outs.append((mm(pb, v) * inv, jnp.broadcast_to(inv, (QB, 128))))
-    o_ref[rows, :] = jnp.where(lane < HD, outs[0][0], outs[1][0]).astype(BF)
-    linv_ref[rows, :] = jnp.where(lane < HD, outs[0][1], outs[1][1])
+        if h == 1:
+            o_ref[rows, :] = jnp.where(lane < HD, outs[0][0], outs[1][0]).astype(BF)
+            linv_ref[rows, :] = jnp.where(lane < HD, outs[0][1], outs[1][1])
+            outs = []
 
 
 def attend_fwd_kernel(
     x_ref, w_ref, b_ref, seg_ref, cot, wo_in, wu_in, wd_in,
     qkv_ref, o_ref, p_ref, linv_ref, wo, wu, wd, cot_first,
-    seg_col_ref, seg_row_ref, cot_own, i_sems, o_recv, o_sent, u_recv, u_sent, d_recv, d_sent,
+    x_buf, seg_col_ref, seg_row_ref, cot_own, i_sems, o_recv, o_sent, u_recv, u_sent, d_recv, d_sent,
 ):
     j = pl.program_id(0)
     peers = Peers()
     go = Gather(peers, None, wo, False, o_recv, o_sent, RING + LATER_NEAR + FAR)
-    gu = Gather(peers, None, wu, True, u_recv, u_sent, RING + LATER_NEAR)
-    gd = Gather(peers, None, wd, False, d_recv, d_sent, RING + DOWN_NEAR)
+    gu = Gather(peers, None, wu, True, u_recv, u_sent, RING + LATER_NEAR + far_edges(0))
+    gd = Gather(peers, None, wd, False, d_recv, d_sent, RING + DOWN_NEAR + far_edges(0, 1))
     every = (go, gu, gd)
     inward = Inward(peers, cot, cot_first, cot_own, i_sems, (0,))
 
     plan = {
         8: ((go, (1, 0)), (gu, (1, 0))),
+        10: ((gu, (0, 6)), (gd, (0, 6))),
         12: ((gd, (1, 0)), (go, (1, 2), (1, 4), (2, 0)), (gu, (1, 2), (1, 4))),
         16: ((gu, (2, 0)), (go, (0, 6), (1, 6)), (gd, (1, 2), (1, 4))),
         20: ((gd, (2, 0)), (go, (2, 2), (2, 4), (3, 0)), (gu, (2, 2), (2, 4))),
@@ -105,6 +116,9 @@
     def _():
         peers.hello(ALL_PEERS)
         inward.load()
+        f = x_ref.shape[2]
+        for s in range(4):
+            x_buf[:, s * f : (s + 1) * f] = x_ref[s]
         tile = seg_ref[4 * peers.c + peers.r]
         for i in range(8):
             row = tile[i : i + 1, :]
@@ -113,18 +127,18 @@
             seg_row_ref[:, i * 128 : (i + 1) * 128] = row
             seg_col_ref[i * 128 : (i + 1) * 128, :] = jnp.transpose(jnp.broadcast_to(row, (128, 128)))
 
-    qkv_ref[...] = (mm(x_ref[...], w_ref[...]) + b_ref[0, :, 0:384]).astype(BF)
+    qkv_ref[...] = (mm(x_buf[...], w_ref[...]) + b_ref[0, :, 0:384]).astype(BF)
     @pl.when(j == 0)
     def _():
         peers.meet(ALL_PEERS)
         for g in every:
             g.emit(0, 0)
         go.emit(0, 2)
+        gu.emit(0, 2)
+        gd.emit(0, 4)
 
     seg_row = seg_row_ref[...]
-    for i in range(SEQ // QB):
-        hook(i)
-        attend_rows(qkv_ref, seg_col_ref, seg_row, o_ref, p_ref, linv_ref, i)
+    attend_rows(qkv_ref, seg_col_ref, seg_row, o_ref, p_ref, linv_ref, hook)
 
     @pl.when(j == 7)
     def _():
@@ -139,8 +153,8 @@
         attend_fwd_kernel,
         grid=(slots,),
         in_specs=[
-            const(SEQ, x.shape[1]),
-            pl.BlockSpec((x.shape[1], 384), lambda j: (0, j)),
+            const(*x.shape),
+            pl.BlockSpec((w_qkv.shape[0], 384), lambda j: (0, j)),
             pl.BlockSpec((1, 1, b_slot.shape[2]), lambda j: (j, 0, 0)),
             const(8, 8, 128),
             ANY,
@@ -166,10 +180,11 @@
             jax.ShapeDtypeStruct(wo.shape, BF),
             jax.ShapeDtypeStruct(wu.shape, BF),
             jax.ShapeDtypeStruct(wd.shape, BF),
-            jax.ShapeDtypeStruct((SEQ // CHUNKS, x.shape[1]), BF),
+            jax.ShapeDtypeStruct((SEQ // CHUNKS, w_qkv.shape[0]), BF),
         ],
         input_output_aliases={5: 4, 6: 5, 7: 6},
         scratch_shapes=[
+            pltpu.VMEM((SEQ, w_qkv.shape[0]), BF),
             pltpu.VMEM((SEQ, 128), jnp.int32),
             pltpu.VMEM((1, SEQ), jnp.int32),
             pltpu.VMEM((SEQ // CHUNKS, cot.shape[1]), BF),
@@ -218,8 +233,12 @@
     return [("core", s, 2, s, 3), ("core", s, 4, s, 5)]
 
 
-def far_edges(s):
-    return [("y", s, 2, s, 6) if s % 2 == 0 else ("x", s, 4, s, 6), ("core", s, 6, s, 7)]
+def far_edges(s, flip=0):
+    return [("y", s, 2, s, 6) if (s + flip) % 2 == 0 else ("x", s, 4, s, 6), ("core", s, 6, s, 7)]
+
+
+def emit_far(gather, s, flip=0):
+    gather.emit(s, 2 if (s + flip) % 2 == 0 else 4)
 
 
 RING = [(1, s, 0, s + 1, 0) for s in range(3)]
@@ -227,8 +246,10 @@
 FAR = [e for s in range(4) for e in far_edges(s)]
 OWN_BLOCK = near_edges(0) + second_edges(0)
 LATER_NEAR = [e for e in NEAR if e[1] > 0]
+UP_FAR = [e for s in (1, 2, 3) for e in far_edges(s)]
+DOWN_FAR = [e for s in (1, 2, 3) for e in far_edges(s, 1)]
 DOWN_NEAR = [e for e in LATER_NEAR if e[1] < 3] + [("core", 3, 0, 3, 1)]
-DOWN_REST = [e for e in near_edges(3) if e[0] != "core"] + second_edges(3) + FAR
+DOWN_REST = [e for e in near_edges(3) if e[0] != "core"] + second_edges(3) + DOWN_FAR
 
 
 class Gather:
@@ -349,23 +370,25 @@
 
 
 CHUNKS = 4
-
-
-def sems_of_exchange():
-    return DMA((2, 4, CHUNKS))
+FINE = 8
+
+
+def sems_of_exchange(cuts=CHUNKS):
+    return DMA((2, 4, cuts))
 
 
 class Inward:
-    def __init__(self, peers, block, rows, buf, sems, chunks=range(CHUNKS)):
+    def __init__(self, peers, block, rows, buf, sems, chunks=range(CHUNKS), cuts=CHUNKS):
         self.peers, self.block, self.rows, self.buf, self.sems, self.chunks = peers, block, rows, buf, sems, chunks
-        self.n = SEQ // CHUNKS
+        self.n = SEQ // cuts
 
     def ends(self, s, first, count):
         r = lax.rem(self.peers.r + s, 4)
         f = self.block.shape[1]
         src = self.block.at[pl.ds(pl.multiple_of(r * SEQ + first * self.n, self.n), count * self.n), :]
-        at = first if self.rows.shape[0] == SEQ else first - self.chunks[0]
-        return src, self.rows.at[pl.ds(at * self.n, count * self.n), pl.ds(s * f, f)]
+        at = first if self.rows.shape[-2] == SEQ else first - self.chunks[0]
+        rows = pl.ds(at * self.n, count * self.n)
+        return src, self.rows.at[s, rows, :] if len(self.rows.shape) == 3 else self.rows.at[rows, pl.ds(s * f, f)]
 
     def copy(self, s, k):
         return send(self.peers, s, *self.ends(s, k, 1), self.sems.at[0, s, k], self.sems.at[1, s, k])
@@ -459,7 +482,7 @@
     gu = Gather(peers, pu, wu, True, u_recv, u_sent, OWN_BLOCK)
     gd = Gather(peers, pd, wd, False, d_recv, d_sent, OWN_BLOCK)
     later = (go, gu, gd)
-    inward = Inward(peers, tokens, x, rows_buf, i_sems)
+    inward = Inward(peers, tokens, x, rows_buf, i_sems, range(FINE), FINE)
     inward.load()
     here = seg_out.at[pl.ds(2 * r, 2)]
     small = [
@@ -479,14 +502,17 @@
         c.start()
     for g in later:
         g.start()
+    inward.start(0)
     line.wave(0)
+    inward.start(1)
     inward.settle()
     gq.relay((0, 2), (0, 4))
     line.wave(1)
+    inward.start(2)
     for g in later:
         g.relay((0, 2), (0, 4))
     line.wave(2)
-    inward.start(*inward.chunks)
+    inward.start(*range(3, FINE))
     for s in (1, 2, 3):
         gq.relay((s, 2), (s, 4))
     for s in range(4):
@@ -510,7 +536,7 @@
         in_specs=[ANY, vmem] + [ANY] * 6 + [vmem],
         out_specs=[ANY] * 8,
         out_shape=[
-            jax.ShapeDtypeStruct((SEQ, width), BF),
+            jax.ShapeDtypeStruct((4, SEQ, width // 4), BF),
             jax.ShapeDtypeStruct((width, 24 * heads), BF),
             jax.ShapeDtypeStruct((8 * heads, width), BF),
             jax.ShapeDtypeStruct((width, 8 * units), BF),
@@ -529,7 +555,7 @@
             pltpu.VMEM((4, 1, 3 * heads + units), F32),
             DMA((6,)),
             *[DMA((32,))] * 8,
-            sems_of_exchange(),
+            sems_of_exchange(FINE),
             DMA((20,)),
             DMA((11,)),
         ],
@@ -538,7 +564,7 @@
     )(tokens, segments, *weights, vectors)
 
 
-RB = 128
+RB = 256
 
 
 def norm_rows(v):
@@ -579,7 +605,7 @@
 ):
     j = pl.program_id(0)
     peers = Peers()
-    gu = Gather(peers, None, wu, True, u_recv, u_sent, FAR)
+    gu = Gather(peers, None, wu, True, u_recv, u_sent, UP_FAR)
     gd = Gather(peers, None, wd, False, d_recv, d_sent, DOWN_REST)
     inward = Inward(peers, cot, cot_buf, cot_own, i_sems, range(1, CHUNKS))
     early = pltpu.make_async_copy(cot_first, cot_buf.at[pl.ds(0, SEQ // CHUNKS), :], c_sem)
@@ -603,14 +629,15 @@
         acc[...] = jnp.zeros_like(acc)
         peers.meet(ALL_PEERS)
         gd.emit(3, 0)
-        for s in (0, 1, 2):
-            gu.emit(s, 2 if s % 2 == 0 else 4)
-            gd.emit(s, 2 if s % 2 == 0 else 4)
-        gu.emit(3, 4)
+        for s in (1, 2):
+            emit_far(gu, s)
+            emit_far(gd, s, 1)
+        emit_far(gu, 3)
         inward.start(*inward.chunks)
 
         def body(rows):
-            v = x_ref[rows, :].astype(F32) + mm(att_ref[rows, :], wo_ref[...]) + vec_ref[0:1, :]
+            x = jnp.concatenate([x_ref[s, rows, :] for s in range(4)], 1)
+            v = x.astype(F32) + mm(att_ref[rows, :], wo_ref[...]) + vec_ref[0:1, :]
             normed, inv = norm_rows(v)
             normed1_ref[rows, :] = normed
             inv1_ref[rows, :] = jnp.broadcast_to(inv, (RB, 128))
@@ -631,11 +658,11 @@
     @pl.when(j == 4)
     def _():
         for g in (gu, gd):
-            g.relay((0, 6), (1, 6), (2, 6), (3, 6))
+            g.relay((1, 6), (2, 6), (3, 6))
 
     @pl.when(j == 5)
     def _():
-        for s in range(4):
+        for s in (1, 2, 3):
             gu.arrived(s, 7)
             gd.arrived(s, 7)
 
@@ -645,8 +672,8 @@
     w_up = wu_buf.at[slot]
     w_down = wd_buf.at[slot]
     bias = b_ref[0, :, 384:]
-    for i in range(SEQ // 256):
-        rows = slice(i * 256, (i + 1) * 256)
+    for i in range(SEQ // 512):
+        rows = slice(i * 512, (i + 1) * 512)
         act, slope = gelu_and_slope(mm(hlow_ref[rows, :], w_up[...]) + bias)
         act = act.astype(BF)
         act_ref[rows, :] = act
@@ -687,7 +714,7 @@
         ff_fwd_kernel,
         grid=(8,),
         in_specs=[
-            const(SEQ, width),
+            const(*x.shape),
             const(SEQ, width),
             const(width, width),
             const(8, width),
@@ -1298,9 +1325,9 @@
     def _():
         load_u.start()
         peers.hello(ALL_PEERS)
-        for i in range(SEQ // 256):
-            rows = slice(i * 256, (i + 1) * 256)
-            x_t[:, rows] = jnp.transpose(x_ref[rows, :])
+        f = x_ref.shape[2]
+        for s in range(4):
+            x_t[s * f : (s + 1) * f, :] = jnp.transpose(x_ref[s])
         load_u.wait()
         peers.meet(ALL_PEERS)
         cross_u.start()
@@ -1336,8 +1363,9 @@
     prod = do * att_ref[...].astype(F32)
     dob = do.astype(BF)
     q_t = jnp.transpose(q)
+    k_t = jnp.transpose(k)
     do_t = jnp.transpose(dob)
-    dq, dk_t, dv_t = [], [], []
+    dq_t, dk_t, dv_t = [], [], []
     for h in range(2):
         mine = (lane < HD) if h == 0 else (lane >= HD)
         delta = jnp.sum(jnp.where(mine, prod, 0.0), axis=1, keepdims=True)
@@ -1347,10 +1375,10 @@
             dp = mm_t(dom[rows], v)
             ds_ref[h, rows, :] = (p_ref[h, rows, :].astype(F32) * (dp - delta[rows])).astype(BF)
         feats = slice(h * HD, (h + 1) * HD)
-        dq.append(mm(ds_ref[h], k))
+        dq_t.append(mm_t(k_t[feats], ds_ref[h]))
         dk_t.append(mm(q_t[feats], ds_ref[h]))
         dv_t.append(mm(do_t[feats], p_ref[h]))
-    g_ref[:, 0:128] = (jnp.where(lane < HD, dq[0], dq[1]) * scale).astype(BF)
+    g_ref[:, 0:128] = (jnp.transpose(jnp.concatenate(dq_t, 0)) * scale).astype(BF)
     g_ref[:, 128:256] = (jnp.transpose(jnp.concatenate(dk_t, 0)) * scale).astype(BF)
     g_ref[:, 256:384] = jnp.transpose(jnp.concatenate(dv_t, 0)).astype(BF)
     gsum_ref[0] = jnp.sum(g_ref[...].astype(F32), axis=0, keepdims=True)
@@ -1373,7 +1401,7 @@
 
 
 def attend_bwd(gattn, wo, att, qkv, linv, p, x, tot_d, kept_u):
-    width = x.shape[1]
+    width = wo.shape[1]
     heads = 128
     n = tot_d.shape[0]
     return pl.pallas_call(
@@ -1386,7 +1414,7 @@
             pl.BlockSpec((SEQ, 3 * heads), lambda j: (0, pair_at(j))),
             pl.BlockSpec((SEQ, heads), lambda j: (0, pair_at(j))),
             pl.BlockSpec((2, SEQ, SEQ), lambda j: (pair_at(j), 0, 0)),
-            const(SEQ, width),
+            const(*x.shape),
             const(SEQ, width),
             const(n, width),
             ANY,
@@ -1612,7 +1640,12 @@
     hq = b_query.shape[0] // 4
     unit = b_up.shape[0] // 4
     vectors = (b_out, norm1_gain, norm1_shift, b_down, norm2_gain, norm2_shift, b_query, b_value, b_up)
-    vectors = jnp.concatenate(vectors).astype(F32).reshape(1, -1)
+    size = sum(v.shape[0] for v in vectors)
+    first_at, packed = 0, 0.0
+    for v in vectors:
+        packed += jnp.pad(v.astype(F32), (first_at, size - first_at - v.shape[0]))
+        first_at += v.shape[0]
+    vectors = packed.reshape(1, -1)
     x, w_qkv, wo, wu, wd, feat_all, b_slot, seg = first(
         tokens,
         segments.reshape(2, 8, 128),

time: 443 us -> 430 us (0.971); the launches traced: 443 us -> 423 us
  Pallas kernels: 422 us -> 408 us
  local copies, waits for them, and re-layouts: 12 us -> 6.59 us
    pallas_call x1, Pallas kernels: 72.3 us -> 64.2 us  [first(): pl.pallas_call(first_kernel, in_specs=[ANY, vmem] + [ANY] * 6 + [vmem], o...]
    unnamed x21 -> x13, local copies, waits for them, and re-layouts: 9.33 us -> 3.98 us
    pallas_call x2, Pallas kernels: 125 us -> 120 us  [the longest x1 62.4 us: attend_fwd(): pl.pallas_call(attend_fwd_kernel, grid=(slots,), in_specs=[const(*x.shape...]
where the time goes in v5:
time: 430 us; the launch traced here: 423 us
  Pallas kernels  408 us (95%)
  other arithmetic  8.01 us (2%)
  local copies, waits for them, and re-layouts  6.59 us (2%)
    pallas_call x1, Pallas kernels, attend_bwd(): pl.pallas_call(attend_bwd_kernel, grid=(8,), in_specs=[const(SEQ, width),...  75.6 us
    pallas_call x1, Pallas kernels, last(): pl.pallas_call(last_kernel, in_specs=[vmem] * 8 + [ANY] * 3, out_specs=[A...  69.7 us
    pallas_call x1, Pallas kernels, first(): pl.pallas_call(first_kernel, in_specs=[ANY, vmem] + [ANY] * 6 + [vmem], o...  64.2 us
    pallas_call x1, Pallas kernels, attend_fwd(): pl.pallas_call(attend_fwd_kernel, grid=(slots,), in_specs=[const(*x.shape...  62.4 us
    pallas_call x1, Pallas kernels, ff_fwd(): pl.pallas_call(ff_fwd_kernel, grid=(8,), in_specs=[const(*x.shape), const...  57.9 us
    pallas_call x1, Pallas kernels, ff_up_bwd(): pl.pallas_call(ff_up_bwd_kernel, grid=(8,), in_specs=[const(SEQ, width),...  46.3 us
    pallas_call x1, Pallas kernels, ff_down_bwd(): pl.pallas_call(ff_down_bwd_kernel, grid=(8,), in_specs=[const(SEQ, width)...  31.3 us

profile of v5, /device:TPU:0, one launch (start us, length us, event | category | flops | bytes accessed | tf_op | source)
XLA Modules:
  0.0 423.3 jit_solution(3100568037732481234)
XLA Ops:
  0.7 0.8 convert_add_fusion
  1.5 0.6 reshape.69.vectors
  2.1 64.2 %first.1 = (bf16[4,1024,256]{2,1,0:T(8,128)(2,1)}, bf16[1024,3072]{1,0:T(8,128)(2,1)}, bf16[1024,1024]{1,0:T(8,128)(2,1)}, bf16[1024,4096]{1,0:T(8,128)(2,1)}, b...) custom-call(bf16[4096,256]{1,0:T(8,128)(2,1)} %tokens.1, ...), custom_call_target="tpu_custom_call" | custom-call | tf_op jit(solution)/shard_map/first/pallas_call | solution.py:534
  66.3 62.4 %attend_fwd.1 = (bf16[1024,3072]{1,0:T(8,128)(2,1)}, bf16[1024,1024]{1,0:T(8,128)(2,1)}, bf16[16,1024,1024]{2,1,0:T(8,128)(2,1)}, f32[1024,1024]{1,0:T(8,128)}, ...) custom-call(bf16[4,1024,256]{2,1,0:T(8,128)(2,1)} %get-tuple-element, ...), custom_call_target="tpu_custom_call", output_to_operand_aliasing={{4}: (5, {}), {5}: (6, {}), {6}: (7, {})} | custom-call | tf_op jit(solution)/shard_map/attend_fwd/pallas_call | solution.py:152
  128.7 57.9 %ff_fwd.1 = (bf16[1024,4096]{1,0:T(8,128)(2,1)}, bf16[4096,1024]{1,0:T(8,128)(2,1)}, bf16[1024,4096]{1,0:T(8,128)(2,1)}, bf16[1024,4096]{1,0:T(8,128)(2,1)}, bf1...) custom-call(bf16[4,1024,256]{2,1,0:T(8,128)(2,1)} %get-tuple-element, ...), custom_call_target="tpu_custom_call", output_to_operand_aliasing={{0}: (7, {}), {1}: (8, {})} | custom-call | tf_op jit(solution)/shard_map/ff_fwd/pallas_call | solution.py:713
  186.6 31.3 %ff_down_bwd.1 = (bf16[4096,256]{1,0:T(8,128)(2,1)}, bf16[1024,4096]{1,0:T(8,128)(2,1)}, f32[8,1,512]{2,1,0:T(1,128)}, bf16[3,512,1024]{2,1,0:T(8,128)(2,1)}) custom-call(f32[1024,1024]{1,0:T(8,128)} %get-tuple-element.79.r2_ref, bf16[4096,1024]{1,0:T(8,128)(2,1)} %get-tuple-element.81.wd_ref, bf16[1024,4096]{1,0:T(8,128)(2,1)} %get-tuple-element.82.act_ref, ...), custom_call_target="tpu_custom_call" | custom-call | tf_op jit(solution)/shard_map/ff_down_bwd/pallas_call | solution.py:1168
  217.9 46.3 %ff_up_bwd.1 = (bf16[4096,256]{1,0:T(8,128)(2,1)}, f32[1024,1024]{1,0:T(8,128)}, bf16[1024,1024]{1,0:T(8,128)(2,1)}, f32[8,1024]{1,0:T(8,128)}, bf16[3,1024,512]...) custom-call(f32[1024,1024]{1,0:T(8,128)} %get-tuple-element.79.r2_ref, ...), custom_call_target="tpu_custom_call", output_to_operand_aliasing={{0}: (8, {})} | custom-call | tf_op jit(solution)/shard_map/ff_up_bwd/pallas_call | solution.py:1260
  264.3 75.6 %attend_bwd.1 = (bf16[1024,3072]{1,0:T(8,128)(2,1)}, f32[8,1,384]{2,1,0:T(1,128)}, bf16[1024,384]{1,0:T(8,128)(2,1)}, bf16[128,1024]{1,0:T(8,128)(2,1)}, bf16[51...) custom-call(bf16[1024,1024]{1,0:T(8,128)(2,1)} %get-tuple-element.92.gattn_ref, bf16[1024,1024]{1,0:T(8,128)(2,1)} %get-tuple-element.74.wo_ref, ...), custom_call_target="tpu_custom_call" | custom-call | tf_op jit(solution)/shard_map/attend_bwd/pallas_call | solution.py:1407
  339.9 69.7 %last.1 = (bf16[4096,256]{1,0:T(8,128)(2,1)}, bf16[256,1536]{1,0:T(8,128)(2,1)}, bf16[512,256]{1,0:T(8,128)(2,1)}, bf16[2048,256]{1,0:T(8,128)(2,1)}, bf16[256,2...) custom-call(bf16[1024,384]{1,0:T(8,128)(2,1)} %get-tuple-element.98.tot_q, ...), custom_call_target="tpu_custom_call" | custom-call | tf_op jit(solution)/shard_map/last/pallas_call | solution.py:1595
  409.7 0.0 copy-start.3
  409.7 1.4 fusion
  411.1 0.7 copy.44
  411.8 0.6 slice_bitcast_fusion.1
  412.4 0.6 copy.42
  413.0 0.0 copy-start.2
  413.0 1.9 convert_element_type.48
  414.9 2.3 slice_convert_fusion
  417.2 0.0 copy-done.3
  417.2 0.0 copy-start
  417.2 1.6 convert_element_type.49
  418.7 0.0 copy-done.2
  418.7 0.0 copy-start.1
  418.7 1.5 convert_element_type.50
  420.2 0.0 copy-done
  420.2 1.3 copy.53
  421.5 0.0 copy-done.1
  421.5 1.3 copy.54
  (1 shorter events, 0.0 us)
Async XLA Ops:
  409.7 7.5 %copy-start.3 = (bf16[256,2048]{1,0:T(8,128)(2,1)S(1)}, bf16[256,2048]{1,0:T(8,128)(2,1)}, u32[]{:S(2)}) copy-start(bf16[256,2048]{1,0:T(8,128)(2,1)} %get-tuple-element.113) | copy-start | bytes 3145732
  413.0 5.7 %copy-start.2 = (bf16[2048,256]{1,0:T(8,128)(2,1)S(1)}, bf16[2048,256]{1,0:T(8,128)(2,1)}, u32[]{:S(2)}) copy-start(bf16[2048,256]{1,0:T(8,128)(2,1)} %get-tuple-element.114) | copy-start | bytes 3145732
  417.2 3.0 copy-start
  418.7 2.8 copy-start.1

commit v6 on v5

--- a/solution.py
+++ b/solution.py
@@ -43,7 +43,7 @@
     return jax.nn.gelu(v, approximate=False)
 
 
-def attend_rows(qkv_ref, seg_col_ref, seg_row, o_ref, p_ref, linv_ref, hook):
+def attend_rows(qkv_ref, seg_col_ref, seg_row, o_ref, p_ref, linv_ref):
     lane = lax.broadcasted_iota(jnp.int32, (QB, 128), 1)
     scale = HD ** (-0.5) * math.log2(math.e)
     k = qkv_ref[:, 128:256]
@@ -59,8 +59,6 @@
     outs = []
     for at, (i, h) in enumerate(units):
         rows = slice(i * QB, (i + 1) * QB)
-        if h == 0:
-            hook(i)
         s = ahead
         if at + 1 < len(units):
             ahead = scores(*units[at + 1])
@@ -80,7 +78,7 @@
 
 def attend_fwd_kernel(
     x_ref, w_ref, b_ref, seg_ref, cot, wo_in, wu_in, wd_in,
-    qkv_ref, o_ref, p_ref, linv_ref, wo, wu, wd, cot_first,
+    qkv_ref, o_ref, p_ref, linv_ref, x_t, wo, wu, wd, cot_first,
     x_buf, seg_col_ref, seg_row_ref, cot_own, i_sems, o_recv, o_sent, u_recv, u_sent, d_recv, d_sent,
 ):
     j = pl.program_id(0)
@@ -92,25 +90,18 @@
     inward = Inward(peers, cot, cot_first, cot_own, i_sems, (0,))
 
     plan = {
-        8: ((go, (1, 0)), (gu, (1, 0))),
-        10: ((gu, (0, 6)), (gd, (0, 6))),
-        12: ((gd, (1, 0)), (go, (1, 2), (1, 4), (2, 0)), (gu, (1, 2), (1, 4))),
-        16: ((gu, (2, 0)), (go, (0, 6), (1, 6)), (gd, (1, 2), (1, 4))),
-        20: ((gd, (2, 0)), (go, (2, 2), (2, 4), (3, 0)), (gu, (2, 2), (2, 4))),
-        25: ((gu, (3, 0)), (go, (2, 6), (3, 2), (3, 4)), (gd, (2, 2), (2, 4))),
-        29: ((gd, (3, 0)), (gu, (3, 2), (3, 4)), (go, (3, 6))),
+        2: ((go, (1, 0)), (gu, (1, 0)), (gu, (0, 6)), (gd, (0, 6))),
+        3: ((gd, (1, 0)), (go, (1, 2), (1, 4), (2, 0))),
+        4: ((gu, (1, 2), (1, 4), (2, 0)), (go, (0, 6), (1, 6))),
+        5: ((gd, (1, 2), (1, 4), (2, 0)), (go, (2, 2), (2, 4), (3, 0))),
+        6: ((gu, (2, 2), (2, 4)), (gu, (3, 0))),
+        7: ((gd, (2, 2), (2, 4)), (go, (2, 6), (3, 2), (3, 4))),
+        8: ((gd, (3, 0)), (gu, (3, 2), (3, 4)), (go, (3, 6))),
     }
 
-    def hook(i):
-        for at, work in plan.items():
-            if at % 4 == i:
-                @pl.when(j == at // 4)
-                def _(at=at, work=work):
-                    for g, *blocks in work:
-                        g.relay(*blocks)
-                    if at == 20:
-                        inward.settle()
-                        inward.start(0)
+    def relay(step):
+        for g, *blocks in plan[step]:
+            g.relay(*blocks)
 
     @pl.when(j == 0)
     def _():
@@ -137,11 +128,23 @@
         gu.emit(0, 2)
         gd.emit(0, 4)
 
+    for at in range(2, 8):
+        @pl.when(j == at)
+        def _(at=at):
+            relay(at)
+            if at == 5:
+                inward.settle()
+                inward.start(0)
+
     seg_row = seg_row_ref[...]
-    attend_rows(qkv_ref, seg_col_ref, seg_row, o_ref, p_ref, linv_ref, hook)
+    attend_rows(qkv_ref, seg_col_ref, seg_row, o_ref, p_ref, linv_ref)
 
     @pl.when(j == 7)
     def _():
+        f = x_ref.shape[2]
+        for s in range(4):
+            x_t[s * f : (s + 1) * f, :] = jnp.transpose(x_ref[s])
+        relay(8)
         for g in every:
             g.finish()
         inward.finish()
@@ -167,6 +170,7 @@
             pl.BlockSpec((SEQ, 128), lambda j: (0, j)),
             pl.BlockSpec((2, SEQ, SEQ), lambda j: (j, 0, 0)),
             pl.BlockSpec((SEQ, 128), lambda j: (0, j)),
+            const(w_qkv.shape[0], SEQ),
             ANY,
             ANY,
             ANY,
@@ -177,12 +181,13 @@
             jax.ShapeDtypeStruct((SEQ, slots * 128), BF),
             jax.ShapeDtypeStruct((slots * 2, SEQ, SEQ), BF),
             jax.ShapeDtypeStruct((SEQ, slots * 128), F32),
+            jax.ShapeDtypeStruct((w_qkv.shape[0], SEQ), BF),
             jax.ShapeDtypeStruct(wo.shape, BF),
             jax.ShapeDtypeStruct(wu.shape, BF),
             jax.ShapeDtypeStruct(wd.shape, BF),
             jax.ShapeDtypeStruct((SEQ // CHUNKS, w_qkv.shape[0]), BF),
         ],
-        input_output_aliases={5: 4, 6: 5, 7: 6},
+        input_output_aliases={5: 5, 6: 6, 7: 7},
         scratch_shapes=[
             pltpu.VMEM((SEQ, w_qkv.shape[0]), BF),
             pltpu.VMEM((SEQ, 128), jnp.int32),
@@ -581,11 +586,11 @@
 
 
 def gelu_and_slope(v):
-    z = jnp.abs(v) * (0.5 ** 0.5)
-    t = 1.0 / (1.0 + 0.3275911 * z)
-    poly = t * (0.254829592 + t * (-0.284496736 + t * (1.421413741 + t * (-1.453152027 + t * 1.061405429))))
-    bell = jnp.exp2(z * z * -math.log2(math.e))
-    tail = 0.5 * poly * bell
+    t = 1.0 / (1.0 + (0.3275911 * 0.5 ** 0.5) * jnp.abs(v))
+    half = (0.127414796, -0.142248368, 0.7107068705, -0.7265760135, 0.5307027145)
+    poly = t * (half[0] + t * (half[1] + t * (half[2] + t * (half[3] + t * half[4]))))
+    bell = jnp.exp2(v * v * (-0.5 * math.log2(math.e)))
+    tail = poly * bell
     cdf = jnp.where(v >= 0, 1.0 - tail, tail)
     return v * cdf, cdf + v * bell * (1.0 / math.sqrt(2.0 * math.pi))
 
@@ -1304,9 +1309,9 @@
 
 
 def attend_bwd_kernel(
-    gattn_ref, wo_ref, att_ref, qkv_ref, linv_ref, p_ref, x_ref, att_all, tot_d, kept_u,
+    gattn_ref, wo_ref, att_ref, qkv_ref, linv_ref, p_ref, x_t, att_all, tot_d, kept_u,
     g_ref, gsum_ref, tot_q, tot_o, down_ref, up_ref,
-    x_t, ds_ref,
+    ds_ref,
     q_stage, q_land, q_corner, q_land_corner, q_sems,
     q_kept, q_x, q_y, q_c, o_total, o_land, o_kept, o_land_corner, o_x, o_y, o_sems, o_c,
     zd_land, zd_sems, own_u, land_x, land_y, c_sems, tot_u, zu_land, zu_sems,
@@ -1325,9 +1330,6 @@
     def _():
         load_u.start()
         peers.hello(ALL_PEERS)
-        f = x_ref.shape[2]
-        for s in range(4):
-            x_t[s * f : (s + 1) * f, :] = jnp.transpose(x_ref[s])
         load_u.wait()
         peers.meet(ALL_PEERS)
         cross_u.start()
@@ -1400,7 +1402,7 @@
         cross_q.finish(q_kept.at[0], tot_q)
 
 
-def attend_bwd(gattn, wo, att, qkv, linv, p, x, tot_d, kept_u):
+def attend_bwd(gattn, wo, att, qkv, linv, p, x_t, tot_d, kept_u):
     width = wo.shape[1]
     heads = 128
     n = tot_d.shape[0]
@@ -1414,7 +1416,7 @@
             pl.BlockSpec((SEQ, 3 * heads), lambda j: (0, pair_at(j))),
             pl.BlockSpec((SEQ, heads), lambda j: (0, pair_at(j))),
             pl.BlockSpec((2, SEQ, SEQ), lambda j: (pair_at(j), 0, 0)),
-            const(*x.shape),
+            const(*x_t.shape),
             const(SEQ, width),
             const(n, width),
             ANY,
@@ -1436,7 +1438,6 @@
             jax.ShapeDtypeStruct((width // 4, n), BF),
         ],
         scratch_shapes=[
-            pltpu.VMEM((width, SEQ), BF),
             pltpu.VMEM((2, SEQ, SEQ), BF),
             *Fold.scratch(width, 3 * heads),
             pltpu.VMEM((3, width, 3 * heads), BF),
@@ -1456,7 +1457,7 @@
         ],
         compiler_params=pltpu.CompilerParams(vmem_limit_bytes=VMEM_LIMIT, collective_id=5, has_side_effects=True),
         name="attend_bwd",
-    )(gattn, wo, att, qkv, linv, p, x, att, tot_d, kept_u)
+    )(gattn, wo, att, qkv, linv, p, x_t, att, tot_d, kept_u)
 
 
 def last_kernel(
@@ -1653,7 +1654,7 @@
         vectors,
     )
 
-    qkv, att, prob, linv, wo, wu, wd, cot_first = attend_fwd(x, w_qkv, b_slot, seg, cotangent, wo, wu, wd)
+    qkv, att, prob, linv, x_t, wo, wu, wd, cot_first = attend_fwd(x, w_qkv, b_slot, seg, cotangent, wo, wu, wd)
     wu, wd, act, slope, hidden_low, normed1, inv1, output, grad_r2, vg2 = ff_fwd(
         x, att, wo, feat_all, b_slot, cotangent, cot_first, wu, wd
     )
@@ -1663,7 +1664,7 @@
         grad_r2, hidden_low, grad_pre, wu, normed1, inv1, feat_all, output, out_block, kept_d
     )
     g_qkv, g_part, tot_q, tot_o, own_d, own_u = attend_bwd(
-        grad_attn, wo, att, qkv, linv, prob, x, tot_d, kept_u
+        grad_attn, wo, att, qkv, linv, prob, x_t, tot_d, kept_u
     )
 
     x_grad_block, gq, go, gd, gu, slot_sum, own = last(

time: 430 us -> 429 us (level)
  no operation moved by 1% of the time
where the time goes in v6:
time: 429 us; the launch traced here: 422 us
  Pallas kernels  406 us (95%)
  other arithmetic  8.01 us (2%)
  local copies, waits for them, and re-layouts  6.59 us (2%)
    pallas_call x1, Pallas kernels, attend_bwd(): pl.pallas_call(attend_bwd_kernel, grid=(8,), in_specs=[const(SEQ, width),...  75.5 us
    pallas_call x1, Pallas kernels, last(): pl.pallas_call(last_kernel, in_specs=[vmem] * 8 + [ANY] * 3, out_specs=[A...  70.3 us
    pallas_call x1, Pallas kernels, first(): pl.pallas_call(first_kernel, in_specs=[ANY, vmem] + [ANY] * 6 + [vmem], o...  64.2 us
    pallas_call x1, Pallas kernels, attend_fwd(): pl.pallas_call(attend_fwd_kernel, grid=(slots,), in_specs=[const(*x.shape...  61.8 us
    pallas_call x1, Pallas kernels, ff_fwd(): pl.pallas_call(ff_fwd_kernel, grid=(8,), in_specs=[const(*x.shape), const...  57.2 us
    pallas_call x1, Pallas kernels, ff_up_bwd(): pl.pallas_call(ff_up_bwd_kernel, grid=(8,), in_specs=[const(SEQ, width),...  45.8 us
    pallas_call x1, Pallas kernels, ff_down_bwd(): pl.pallas_call(ff_down_bwd_kernel, grid=(8,), in_specs=[const(SEQ, width)...  31.3 us

profile of v6, /device:TPU:0, one launch (start us, length us, event | category | flops | bytes accessed | tf_op | source)
XLA Modules:
  0.0 421.8 jit_solution(16040655401403560987)
XLA Ops:
  0.7 0.8 convert_add_fusion
  1.5 0.6 reshape.69.vectors
  2.1 64.2 %first.1 = (bf16[4,1024,256]{2,1,0:T(8,128)(2,1)}, bf16[1024,3072]{1,0:T(8,128)(2,1)}, bf16[1024,1024]{1,0:T(8,128)(2,1)}, bf16[1024,4096]{1,0:T(8,128)(2,1)}, b...) custom-call(bf16[4096,256]{1,0:T(8,128)(2,1)} %tokens.1, ...), custom_call_target="tpu_custom_call" | custom-call | tf_op jit(solution)/shard_map/first/pallas_call | solution.py:539
  66.3 61.8 %attend_fwd.1 = (bf16[1024,3072]{1,0:T(8,128)(2,1)}, bf16[1024,1024]{1,0:T(8,128)(2,1)}, bf16[16,1024,1024]{2,1,0:T(8,128)(2,1)}, f32[1024,1024]{1,0:T(8,128)}, ...) custom-call(bf16[4,1024,256]{2,1,0:T(8,128)(2,1)} %get-tuple-element, ...), custom_call_target="tpu_custom_call", output_to_operand_aliasing={{5}: (5, {}), {6}: (6, {}), {7}: (7, {})} | custom-call | tf_op jit(solution)/shard_map/attend_fwd/pallas_call | solution.py:155
  128.1 57.2 %ff_fwd.1 = (bf16[1024,4096]{1,0:T(8,128)(2,1)}, bf16[4096,1024]{1,0:T(8,128)(2,1)}, bf16[1024,4096]{1,0:T(8,128)(2,1)}, bf16[1024,4096]{1,0:T(8,128)(2,1)}, bf1...) custom-call(bf16[4,1024,256]{2,1,0:T(8,128)(2,1)} %get-tuple-element, ...), custom_call_target="tpu_custom_call", output_to_operand_aliasing={{0}: (7, {}), {1}: (8, {})} | custom-call | tf_op jit(solution)/shard_map/ff_fwd/pallas_call | solution.py:718
  185.3 31.3 %ff_down_bwd.1 = (bf16[4096,256]{1,0:T(8,128)(2,1)}, bf16[1024,4096]{1,0:T(8,128)(2,1)}, f32[8,1,512]{2,1,0:T(1,128)}, bf16[3,512,1024]{2,1,0:T(8,128)(2,1)}) custom-call(f32[1024,1024]{1,0:T(8,128)} %get-tuple-element.80.r2_ref, bf16[4096,1024]{1,0:T(8,128)(2,1)} %get-tuple-element.82.wd_ref, bf16[1024,4096]{1,0:T(8,128)(2,1)} %get-tuple-element.83.act_ref, ...), custom_call_target="tpu_custom_call" | custom-call | tf_op jit(solution)/shard_map/ff_down_bwd/pallas_call | solution.py:1173
  216.6 45.8 %ff_up_bwd.1 = (bf16[4096,256]{1,0:T(8,128)(2,1)}, f32[1024,1024]{1,0:T(8,128)}, bf16[1024,1024]{1,0:T(8,128)(2,1)}, f32[8,1024]{1,0:T(8,128)}, bf16[3,1024,512]...) custom-call(f32[1024,1024]{1,0:T(8,128)} %get-tuple-element.80.r2_ref, ...), custom_call_target="tpu_custom_call", output_to_operand_aliasing={{0}: (8, {})} | custom-call | tf_op jit(solution)/shard_map/ff_up_bwd/pallas_call | solution.py:1265
  262.4 75.5 %attend_bwd.1 = (bf16[1024,3072]{1,0:T(8,128)(2,1)}, f32[8,1,384]{2,1,0:T(1,128)}, bf16[1024,384]{1,0:T(8,128)(2,1)}, bf16[128,1024]{1,0:T(8,128)(2,1)}, bf16[51...) custom-call(bf16[1024,1024]{1,0:T(8,128)(2,1)} %get-tuple-element.93.gattn_ref, bf16[1024,1024]{1,0:T(8,128)(2,1)} %get-tuple-element.75.wo_ref, ...), custom_call_target="tpu_custom_call" | custom-call | tf_op jit(solution)/shard_map/attend_bwd/pallas_call | solution.py:1409
  337.9 70.3 %last.1 = (bf16[4096,256]{1,0:T(8,128)(2,1)}, bf16[256,1536]{1,0:T(8,128)(2,1)}, bf16[512,256]{1,0:T(8,128)(2,1)}, bf16[2048,256]{1,0:T(8,128)(2,1)}, bf16[256,2...) custom-call(bf16[1024,384]{1,0:T(8,128)(2,1)} %get-tuple-element.100.tot_q, ...), custom_call_target="tpu_custom_call" | custom-call | tf_op jit(solution)/shard_map/last/pallas_call | solution.py:1596
  408.2 0.0 copy-start.3
  408.2 1.4 fusion
  409.6 0.7 copy.44
  410.3 0.6 slice_bitcast_fusion.1
  410.9 0.6 copy.42
  411.5 0.0 copy-start.2
  411.5 1.9 convert_element_type.48
  413.4 2.3 slice_convert_fusion
  415.7 0.0 copy-done.3
  415.7 0.0 copy-start
  415.7 1.6 convert_element_type.49
  417.3 0.0 copy-done.2
  417.3 0.0 copy-start.1
  417.3 1.5 convert_element_type.50
  418.8 0.0 copy-done
  418.8 1.3 copy.53
  420.1 0.0 copy-done.1
  420.1 1.3 copy.54
  (1 shorter events, 0.0 us)
Async XLA Ops:
  408.2 7.5 %copy-start.3 = (bf16[256,2048]{1,0:T(8,128)(2,1)S(1)}, bf16[256,2048]{1,0:T(8,128)(2,1)}, u32[]{:S(2)}) copy-start(bf16[256,2048]{1,0:T(8,128)(2,1)} %get-tuple-element.115) | copy-start | bytes 3145732
  411.5 5.7 %copy-start.2 = (bf16[2048,256]{1,0:T(8,128)(2,1)S(1)}, bf16[2048,256]{1,0:T(8,128)(2,1)}, u32[]{:S(2)}) copy-start(bf16[2048,256]{1,0:T(8,128)(2,1)} %get-tuple-element.116) | copy-start | bytes 3145732
  415.7 3.0 copy-start
  417.3 2.8 copy-start.1

commit v7 on v6

--- a/solution.py
+++ b/solution.py
@@ -78,7 +78,7 @@
 
 def attend_fwd_kernel(
     x_ref, w_ref, b_ref, seg_ref, cot, wo_in, wu_in, wd_in,
-    qkv_ref, o_ref, p_ref, linv_ref, x_t, wo, wu, wd, cot_first,
+    qkv_ref, o_ref, p_ref, linv_ref, wo, wu, wd, cot_first,
     x_buf, seg_col_ref, seg_row_ref, cot_own, i_sems, o_recv, o_sent, u_recv, u_sent, d_recv, d_sent,
 ):
     j = pl.program_id(0)
@@ -141,9 +141,6 @@
 
     @pl.when(j == 7)
     def _():
-        f = x_ref.shape[2]
-        for s in range(4):
-            x_t[s * f : (s + 1) * f, :] = jnp.transpose(x_ref[s])
         relay(8)
         for g in every:
             g.finish()
@@ -170,7 +167,6 @@
             pl.BlockSpec((SEQ, 128), lambda j: (0, j)),
             pl.BlockSpec((2, SEQ, SEQ), lambda j: (j, 0, 0)),
             pl.BlockSpec((SEQ, 128), lambda j: (0, j)),
-            const(w_qkv.shape[0], SEQ),
             ANY,
             ANY,
             ANY,
@@ -181,13 +177,12 @@
             jax.ShapeDtypeStruct((SEQ, slots * 128), BF),
             jax.ShapeDtypeStruct((slots * 2, SEQ, SEQ), BF),
             jax.ShapeDtypeStruct((SEQ, slots * 128), F32),
-            jax.ShapeDtypeStruct((w_qkv.shape[0], SEQ), BF),
             jax.ShapeDtypeStruct(wo.shape, BF),
             jax.ShapeDtypeStruct(wu.shape, BF),
             jax.ShapeDtypeStruct(wd.shape, BF),
             jax.ShapeDtypeStruct((SEQ // CHUNKS, w_qkv.shape[0]), BF),
         ],
-        input_output_aliases={5: 5, 6: 6, 7: 7},
+        input_output_aliases={5: 4, 6: 5, 7: 6},
         scratch_shapes=[
             pltpu.VMEM((SEQ, w_qkv.shape[0]), BF),
             pltpu.VMEM((SEQ, 128), jnp.int32),
@@ -1309,9 +1304,9 @@
 
 
 def attend_bwd_kernel(
-    gattn_ref, wo_ref, att_ref, qkv_ref, linv_ref, p_ref, x_t, att_all, tot_d, kept_u,
+    gattn_ref, wo_ref, att_ref, qkv_ref, linv_ref, p_ref, x_ref, att_all, tot_d, kept_u,
     g_ref, gsum_ref, tot_q, tot_o, down_ref, up_ref,
-    ds_ref,
+    x_t, ds_ref,
     q_stage, q_land, q_corner, q_land_corner, q_sems,
     q_kept, q_x, q_y, q_c, o_total, o_land, o_kept, o_land_corner, o_x, o_y, o_sems, o_c,
     zd_land, zd_sems, own_u, land_x, land_y, c_sems, tot_u, zu_land, zu_sems,
@@ -1330,6 +1325,9 @@
     def _():
         load_u.start()
         peers.hello(ALL_PEERS)
+        f = x_ref.shape[2]
+        for s in range(4):
+            x_t[s * f : (s + 1) * f, :] = jnp.transpose(x_ref[s])
         load_u.wait()
         peers.meet(ALL_PEERS)
         cross_u.start()
@@ -1402,7 +1400,7 @@
         cross_q.finish(q_kept.at[0], tot_q)
 
 
-def attend_bwd(gattn, wo, att, qkv, linv, p, x_t, tot_d, kept_u):
+def attend_bwd(gattn, wo, att, qkv, linv, p, x, tot_d, kept_u):
     width = wo.shape[1]
     heads = 128
     n = tot_d.shape[0]
@@ -1416,7 +1414,7 @@
             pl.BlockSpec((SEQ, 3 * heads), lambda j: (0, pair_at(j))),
             pl.BlockSpec((SEQ, heads), lambda j: (0, pair_at(j))),
             pl.BlockSpec((2, SEQ, SEQ), lambda j: (pair_at(j), 0, 0)),
-            const(*x_t.shape),
+            const(*x.shape),
             const(SEQ, width),
             const(n, width),
             ANY,
@@ -1438,6 +1436,7 @@
             jax.ShapeDtypeStruct((width // 4, n), BF),
         ],
         scratch_shapes=[
+            pltpu.VMEM((width, SEQ), BF),
             pltpu.VMEM((2, SEQ, SEQ), BF),
             *Fold.scratch(width, 3 * heads),
             pltpu.VMEM((3, width, 3 * heads), BF),
@@ -1457,7 +1456,7 @@
         ],
         compiler_params=pltpu.CompilerParams(vmem_limit_bytes=VMEM_LIMIT, collective_id=5, has_side_effects=True),
         name="attend_bwd",
-    )(gattn, wo, att, qkv, linv, p, x_t, att, tot_d, kept_u)
+    )(gattn, wo, att, qkv, linv, p, x, att, tot_d, kept_u)
 
 
 def last_kernel(
@@ -1654,7 +1653,7 @@
         vectors,
     )
 
-    qkv, att, prob, linv, x_t, wo, wu, wd, cot_first = attend_fwd(x, w_qkv, b_slot, seg, cotangent, wo, wu, wd)
+    qkv, att, prob, linv, wo, wu, wd, cot_first = attend_fwd(x, w_qkv, b_slot, seg, cotangent, wo, wu, wd)
     wu, wd, act, slope, hidden_low, normed1, inv1, output, grad_r2, vg2 = ff_fwd(
         x, att, wo, feat_all, b_slot, cotangent, cot_first, wu, wd
     )
@@ -1664,7 +1663,7 @@
         grad_r2, hidden_low, grad_pre, wu, normed1, inv1, feat_all, output, out_block, kept_d
     )
     g_qkv, g_part, tot_q, tot_o, own_d, own_u = attend_bwd(
-        grad_attn, wo, att, qkv, linv, prob, x_t, tot_d, kept_u
+        grad_attn, wo, att, qkv, linv, prob, x, tot_d, kept_u
     )
 
     x_grad_block, gq, go, gd, gu, slot_sum, own = last(

time: 429 us -> 427 us (level)
  no operation moved by 1% of the time
where the time goes in v7:
time: 427 us; the launch traced here: 421 us
  Pallas kernels  405 us (95%)
  other arithmetic  8.01 us (2%)
  local copies, waits for them, and re-layouts  6.59 us (2%)
    pallas_call x1, Pallas kernels, attend_bwd(): pl.pallas_call(attend_bwd_kernel, grid=(8,), in_specs=[const(SEQ, width),...  75.6 us
    pallas_call x1, Pallas kernels, last(): pl.pallas_call(last_kernel, in_specs=[vmem] * 8 + [ANY] * 3, out_specs=[A...  70.3 us
    pallas_call x1, Pallas kernels, first(): pl.pallas_call(first_kernel, in_specs=[ANY, vmem] + [ANY] * 6 + [vmem], o...  64.2 us
    pallas_call x1, Pallas kernels, attend_fwd(): pl.pallas_call(attend_fwd_kernel, grid=(slots,), in_specs=[const(*x.shape...  60.5 us
    pallas_call x1, Pallas kernels, ff_fwd(): pl.pallas_call(ff_fwd_kernel, grid=(8,), in_specs=[const(*x.shape), const...  57.2 us
    pallas_call x1, Pallas kernels, ff_up_bwd(): pl.pallas_call(ff_up_bwd_kernel, grid=(8,), in_specs=[const(SEQ, width),...  45.8 us
    pallas_call x1, Pallas kernels, ff_down_bwd(): pl.pallas_call(ff_down_bwd_kernel, grid=(8,), in_specs=[const(SEQ, width)...  31.3 us

profile of v7, /device:TPU:0, one launch (start us, length us, event | category | flops | bytes accessed | tf_op | source)
XLA Modules:
  0.0 420.5 jit_solution(16283030290976137201)
XLA Ops:
  0.7 0.8 convert_add_fusion
  1.5 0.6 reshape.69.vectors
  2.1 64.2 %first.1 = (bf16[4,1024,256]{2,1,0:T(8,128)(2,1)}, bf16[1024,3072]{1,0:T(8,128)(2,1)}, bf16[1024,1024]{1,0:T(8,128)(2,1)}, bf16[1024,4096]{1,0:T(8,128)(2,1)}, b...) custom-call(bf16[4096,256]{1,0:T(8,128)(2,1)} %tokens.1, ...), custom_call_target="tpu_custom_call" | custom-call | tf_op jit(solution)/shard_map/first/pallas_call | solution.py:534
  66.3 60.5 %attend_fwd.1 = (bf16[1024,3072]{1,0:T(8,128)(2,1)}, bf16[1024,1024]{1,0:T(8,128)(2,1)}, bf16[16,1024,1024]{2,1,0:T(8,128)(2,1)}, f32[1024,1024]{1,0:T(8,128)}, ...) custom-call(bf16[4,1024,256]{2,1,0:T(8,128)(2,1)} %get-tuple-element, ...), custom_call_target="tpu_custom_call", output_to_operand_aliasing={{4}: (5, {}), {5}: (6, {}), {6}: (7, {})} | custom-call | tf_op jit(solution)/shard_map/attend_fwd/pallas_call | solution.py:152
  126.7 57.2 %ff_fwd.1 = (bf16[1024,4096]{1,0:T(8,128)(2,1)}, bf16[4096,1024]{1,0:T(8,128)(2,1)}, bf16[1024,4096]{1,0:T(8,128)(2,1)}, bf16[1024,4096]{1,0:T(8,128)(2,1)}, bf1...) custom-call(bf16[4,1024,256]{2,1,0:T(8,128)(2,1)} %get-tuple-element, ...), custom_call_target="tpu_custom_call", output_to_operand_aliasing={{0}: (7, {}), {1}: (8, {})} | custom-call | tf_op jit(solution)/shard_map/ff_fwd/pallas_call | solution.py:713
  184.0 31.3 %ff_down_bwd.1 = (bf16[4096,256]{1,0:T(8,128)(2,1)}, bf16[1024,4096]{1,0:T(8,128)(2,1)}, f32[8,1,512]{2,1,0:T(1,128)}, bf16[3,512,1024]{2,1,0:T(8,128)(2,1)}) custom-call(f32[1024,1024]{1,0:T(8,128)} %get-tuple-element.79.r2_ref, bf16[4096,1024]{1,0:T(8,128)(2,1)} %get-tuple-element.81.wd_ref, bf16[1024,4096]{1,0:T(8,128)(2,1)} %get-tuple-element.82.act_ref, ...), custom_call_target="tpu_custom_call" | custom-call | tf_op jit(solution)/shard_map/ff_down_bwd/pallas_call | solution.py:1168
  215.2 45.8 %ff_up_bwd.1 = (bf16[4096,256]{1,0:T(8,128)(2,1)}, f32[1024,1024]{1,0:T(8,128)}, bf16[1024,1024]{1,0:T(8,128)(2,1)}, f32[8,1024]{1,0:T(8,128)}, bf16[3,1024,512]...) custom-call(f32[1024,1024]{1,0:T(8,128)} %get-tuple-element.79.r2_ref, ...), custom_call_target="tpu_custom_call", output_to_operand_aliasing={{0}: (8, {})} | custom-call | tf_op jit(solution)/shard_map/ff_up_bwd/pallas_call | solution.py:1260
  261.0 75.6 %attend_bwd.1 = (bf16[1024,3072]{1,0:T(8,128)(2,1)}, f32[8,1,384]{2,1,0:T(1,128)}, bf16[1024,384]{1,0:T(8,128)(2,1)}, bf16[128,1024]{1,0:T(8,128)(2,1)}, bf16[51...) custom-call(bf16[1024,1024]{1,0:T(8,128)(2,1)} %get-tuple-element.92.gattn_ref, bf16[1024,1024]{1,0:T(8,128)(2,1)} %get-tuple-element.74.wo_ref, ...), custom_call_target="tpu_custom_call" | custom-call | tf_op jit(solution)/shard_map/attend_bwd/pallas_call | solution.py:1407
  336.6 70.3 %last.1 = (bf16[4096,256]{1,0:T(8,128)(2,1)}, bf16[256,1536]{1,0:T(8,128)(2,1)}, bf16[512,256]{1,0:T(8,128)(2,1)}, bf16[2048,256]{1,0:T(8,128)(2,1)}, bf16[256,2...) custom-call(bf16[1024,384]{1,0:T(8,128)(2,1)} %get-tuple-element.98.tot_q, ...), custom_call_target="tpu_custom_call" | custom-call | tf_op jit(solution)/shard_map/last/pallas_call | solution.py:1595
  406.9 0.0 copy-start.3
  406.9 1.4 fusion
  408.3 0.7 copy.44
  409.0 0.6 slice_bitcast_fusion.1
  409.6 0.6 copy.42
  410.2 0.0 copy-start.2
  410.2 1.9 convert_element_type.48
  412.1 2.3 slice_convert_fusion
  414.4 0.0 copy-done.3
  414.4 0.0 copy-start
  414.4 1.6 convert_element_type.49
  416.0 0.0 copy-done.2
  416.0 0.0 copy-start.1
  416.0 1.5 convert_element_type.50
  417.5 0.0 copy-done
  417.5 1.3 copy.53
  418.8 0.0 copy-done.1
  418.8 1.3 copy.54
  (1 shorter events, 0.0 us)
Async XLA Ops:
  406.9 7.5 %copy-start.3 = (bf16[256,2048]{1,0:T(8,128)(2,1)S(1)}, bf16[256,2048]{1,0:T(8,128)(2,1)}, u32[]{:S(2)}) copy-start(bf16[256,2048]{1,0:T(8,128)(2,1)} %get-tuple-element.113) | copy-start | bytes 3145732
  410.2 5.7 %copy-start.2 = (bf16[2048,256]{1,0:T(8,128)(2,1)S(1)}, bf16[2048,256]{1,0:T(8,128)(2,1)}, u32[]{:S(2)}) copy-start(bf16[2048,256]{1,0:T(8,128)(2,1)} %get-tuple-element.114) | copy-start | bytes 3145732
  414.4 3.0 copy-start
  416.0 2.8 copy-start.1

commit v8 on v7

--- a/solution.py
+++ b/solution.py
@@ -782,7 +782,7 @@
 
 def sum_rows(dst, *srcs):
     n = dst.shape[0]
-    step = min(n, 64)
+    step = min(n, 256)
 
     def run(i, carry):
         rows = pl.ds(pl.multiple_of(i * step, step), step)

time: 427 us -> 426 us (level)
  no operation moved by 1% of the time
where the time goes in v8:
time: 426 us; the launch traced here: 420 us
  Pallas kernels  404 us (95%)
  other arithmetic  8.01 us (2%)
  local copies, waits for them, and re-layouts  6.59 us (2%)
    pallas_call x1, Pallas kernels, attend_bwd(): pl.pallas_call(attend_bwd_kernel, grid=(8,), in_specs=[const(SEQ, width),...  74.9 us
    pallas_call x1, Pallas kernels, last(): pl.pallas_call(last_kernel, in_specs=[vmem] * 8 + [ANY] * 3, out_specs=[A...  70.5 us
    pallas_call x1, Pallas kernels, first(): pl.pallas_call(first_kernel, in_specs=[ANY, vmem] + [ANY] * 6 + [vmem], o...  64.2 us
    pallas_call x1, Pallas kernels, attend_fwd(): pl.pallas_call(attend_fwd_kernel, grid=(slots,), in_specs=[const(*x.shape...  60.5 us
    pallas_call x1, Pallas kernels, ff_fwd(): pl.pallas_call(ff_fwd_kernel, grid=(8,), in_specs=[const(*x.shape), const...  57.2 us
    pallas_call x1, Pallas kernels, ff_up_bwd(): pl.pallas_call(ff_up_bwd_kernel, grid=(8,), in_specs=[const(SEQ, width),...  45.4 us
    pallas_call x1, Pallas kernels, ff_down_bwd(): pl.pallas_call(ff_down_bwd_kernel, grid=(8,), in_specs=[const(SEQ, width)...  31.3 us

profile of v8, /device:TPU:0, one launch (start us, length us, event | category | flops | bytes accessed | tf_op | source)
XLA Modules:
  0.0 419.7 jit_solution(8899402754949059566)
XLA Ops:
  0.7 0.8 convert_add_fusion
  1.5 0.6 reshape.69.vectors
  2.1 64.2 %first.1 = (bf16[4,1024,256]{2,1,0:T(8,128)(2,1)}, bf16[1024,3072]{1,0:T(8,128)(2,1)}, bf16[1024,1024]{1,0:T(8,128)(2,1)}, bf16[1024,4096]{1,0:T(8,128)(2,1)}, b...) custom-call(bf16[4096,256]{1,0:T(8,128)(2,1)} %tokens.1, ...), custom_call_target="tpu_custom_call" | custom-call | tf_op jit(solution)/shard_map/first/pallas_call | solution.py:534
  66.3 60.5 %attend_fwd.1 = (bf16[1024,3072]{1,0:T(8,128)(2,1)}, bf16[1024,1024]{1,0:T(8,128)(2,1)}, bf16[16,1024,1024]{2,1,0:T(8,128)(2,1)}, f32[1024,1024]{1,0:T(8,128)}, ...) custom-call(bf16[4,1024,256]{2,1,0:T(8,128)(2,1)} %get-tuple-element, ...), custom_call_target="tpu_custom_call", output_to_operand_aliasing={{4}: (5, {}), {5}: (6, {}), {6}: (7, {})} | custom-call | tf_op jit(solution)/shard_map/attend_fwd/pallas_call | solution.py:152
  126.7 57.2 %ff_fwd.1 = (bf16[1024,4096]{1,0:T(8,128)(2,1)}, bf16[4096,1024]{1,0:T(8,128)(2,1)}, bf16[1024,4096]{1,0:T(8,128)(2,1)}, bf16[1024,4096]{1,0:T(8,128)(2,1)}, bf1...) custom-call(bf16[4,1024,256]{2,1,0:T(8,128)(2,1)} %get-tuple-element, ...), custom_call_target="tpu_custom_call", output_to_operand_aliasing={{0}: (7, {}), {1}: (8, {})} | custom-call | tf_op jit(solution)/shard_map/ff_fwd/pallas_call | solution.py:713
  184.0 31.3 %ff_down_bwd.1 = (bf16[4096,256]{1,0:T(8,128)(2,1)}, bf16[1024,4096]{1,0:T(8,128)(2,1)}, f32[8,1,512]{2,1,0:T(1,128)}, bf16[3,512,1024]{2,1,0:T(8,128)(2,1)}) custom-call(f32[1024,1024]{1,0:T(8,128)} %get-tuple-element.79.r2_ref, bf16[4096,1024]{1,0:T(8,128)(2,1)} %get-tuple-element.81.wd_ref, bf16[1024,4096]{1,0:T(8,128)(2,1)} %get-tuple-element.82.act_ref, ...), custom_call_target="tpu_custom_call" | custom-call | tf_op jit(solution)/shard_map/ff_down_bwd/pallas_call | solution.py:1168
  215.2 45.4 %ff_up_bwd.1 = (bf16[4096,256]{1,0:T(8,128)(2,1)}, f32[1024,1024]{1,0:T(8,128)}, bf16[1024,1024]{1,0:T(8,128)(2,1)}, f32[8,1024]{1,0:T(8,128)}, bf16[3,1024,512]...) custom-call(f32[1024,1024]{1,0:T(8,128)} %get-tuple-element.79.r2_ref, ...), custom_call_target="tpu_custom_call", output_to_operand_aliasing={{0}: (8, {})} | custom-call | tf_op jit(solution)/shard_map/ff_up_bwd/pallas_call | solution.py:1260
  260.6 74.9 %attend_bwd.1 = (bf16[1024,3072]{1,0:T(8,128)(2,1)}, f32[8,1,384]{2,1,0:T(1,128)}, bf16[1024,384]{1,0:T(8,128)(2,1)}, bf16[128,1024]{1,0:T(8,128)(2,1)}, bf16[51...) custom-call(bf16[1024,1024]{1,0:T(8,128)(2,1)} %get-tuple-element.92.gattn_ref, bf16[1024,1024]{1,0:T(8,128)(2,1)} %get-tuple-element.74.wo_ref, ...), custom_call_target="tpu_custom_call" | custom-call | tf_op jit(solution)/shard_map/attend_bwd/pallas_call | solution.py:1407
  335.5 70.5 %last.1 = (bf16[4096,256]{1,0:T(8,128)(2,1)}, bf16[256,1536]{1,0:T(8,128)(2,1)}, bf16[512,256]{1,0:T(8,128)(2,1)}, bf16[2048,256]{1,0:T(8,128)(2,1)}, bf16[256,2...) custom-call(bf16[1024,384]{1,0:T(8,128)(2,1)} %get-tuple-element.98.tot_q, ...), custom_call_target="tpu_custom_call" | custom-call | tf_op jit(solution)/shard_map/last/pallas_call | solution.py:1595
  406.1 0.0 copy-start.3
  406.1 1.4 fusion
  407.5 0.7 copy.44
  408.2 0.6 slice_bitcast_fusion.1
  408.8 0.6 copy.42
  409.4 0.0 copy-start.2
  409.4 1.9 convert_element_type.48
  411.3 2.3 slice_convert_fusion
  413.6 0.0 copy-done.3
  413.6 0.0 copy-start
  413.6 1.6 convert_element_type.49
  415.1 0.0 copy-done.2
  415.1 0.0 copy-start.1
  415.2 1.5 convert_element_type.50
  416.6 0.0 copy-done
  416.6 1.3 copy.53
  418.0 0.0 copy-done.1
  418.0 1.3 copy.54
  (1 shorter events, 0.0 us)
Async XLA Ops:
  406.1 7.5 %copy-start.3 = (bf16[256,2048]{1,0:T(8,128)(2,1)S(1)}, bf16[256,2048]{1,0:T(8,128)(2,1)}, u32[]{:S(2)}) copy-start(bf16[256,2048]{1,0:T(8,128)(2,1)} %get-tuple-element.113) | copy-start | bytes 3145732
  409.4 5.7 %copy-start.2 = (bf16[2048,256]{1,0:T(8,128)(2,1)S(1)}, bf16[2048,256]{1,0:T(8,128)(2,1)}, u32[]{:S(2)}) copy-start(bf16[2048,256]{1,0:T(8,128)(2,1)} %get-tuple-element.114) | copy-start | bytes 3145732
  413.6 3.0 copy-start
  415.1 2.8 copy-start.1
